TPU v7x, 512 devices: a whole 4x4x16 slice. The times are simulated.
512 devices in a mesh: wide: 128 (over y, z, core), narrow: 4 (over x).
Axes of the slice: x: 4, y: 4, z: 16, core: 2. Of those that a mesh axis runs over, the one named last changes fastest.
Arguments:
- mobility: float32 [2048, 64, 256], P('wide', 'narrow'), may hold values from 0.2 to 5
- sav_vector: float32 [2048, 64, 256], P('wide', 'narrow'), may hold values from -8 to 8
- cotangent: float32 [2048, 64, 256], P('wide', 'narrow'), may hold values from -8 to 8
Outputs:
- adjoint: float32 [2048, 64, 256], P('wide', 'narrow')
All inputs are finite; a program needn't handle non-finite values.
Results may differ from a plain program's by a relative error of at most 0.0019.
Values sent between devices are 32-bit elements; how exact they have to be, the bound alone decides.
No kernel may reach another device: no remote copies, remote signals or barrier semaphores. Data moves between devices by JAX's collectives and lax.ppermute only.
A program may use at most 128 MiB of HBM per device.

v0:
```python
import functools

import jax
import jax.numpy as jnp
from jax import lax
from jax.sharding import Mesh
from jax.sharding import PartitionSpec as P

LEVELS = 5
WIDE_NARROW = ("wide_0", "wide_1", "wide_2", "narrow")
WIDE = ("wide_0", "wide_1", "wide_2")


DAMPING = 0.8
BASE_TAU = 16.0


def with_halo(shard, sides, width):
    edges = {}
    for axis, dim in sides:
        size, length = (lax.axis_size(axis), shard.shape[dim])
        up = [(i, (i + 1) % size) for i in range(size - 1)]
        last = lax.slice_in_dim(shard, length - width, length, axis=dim)
        initial = lax.slice_in_dim(shard, 0, width, axis=dim)
        edges[dim] = (
            lax.ppermute(last, axis, up),
            lax.ppermute(initial, axis, [(b, a) for a, b in up]),
        )
    done = []
    for _, dim in sides:
        low, high = edges[dim]
        around = [(width, width) if d in done else (0, 0) for d in range(shard.ndim)]
        shard = jnp.concatenate([jnp.pad(low, around), shard, jnp.pad(high, around)], axis=dim)
        done.append(dim)
    return shard


def by_axis(shard, axes):
    return functools.reduce(lax.psum, axes, shard)


def face_terms(padded, tau):
    center = padded[1:-1, 1:-1, 1:-1]
    others = [
        padded[2:, 1:-1, 1:-1],
        padded[:-2, 1:-1, 1:-1],
        padded[1:-1, 2:, 1:-1],
        padded[1:-1, :-2, 1:-1],
        padded[1:-1, 1:-1, 2:],
        padded[1:-1, 1:-1, :-2],
    ]
    couplings = jnp.stack([0.5 * tau * (center + other) for other in others]).astype(jnp.bfloat16)
    diagonal = jnp.float32(1.0) + couplings[0].astype(jnp.float32)
    for index in range(1, 6):
        diagonal = diagonal + couplings[index].astype(jnp.float32)
    return (couplings, diagonal)


def coarsen(values):
    count, size_x, size_y, size_z = values.shape
    blocks = values.reshape(count, size_x // 2, 2, size_y // 2, 2, size_z // 2, 2)
    return blocks.mean(axis=(2, 4, 6))


def refine(values):
    return jnp.repeat(jnp.repeat(jnp.repeat(values, 2, axis=1), 2, axis=2), 2, axis=3)


def stencil(padded, couplings, diagonal):
    center = padded[:, 1:-1, 1:-1, 1:-1]
    others = [
        padded[:, 2:, 1:-1, 1:-1],
        padded[:, :-2, 1:-1, 1:-1],
        padded[:, 1:-1, 2:, 1:-1],
        padded[:, 1:-1, :-2, 1:-1],
        padded[:, 1:-1, 1:-1, 2:],
        padded[:, 1:-1, 1:-1, :-2],
    ]
    total = couplings[0].astype(jnp.float32)[None] * others[0]
    for index in range(1, 6):
        total = total + couplings[index].astype(jnp.float32)[None] * others[index]
    return diagonal[None] * center - total


def operate(iterate, couplings, diagonal):
    padded = with_halo(iterate, ((WIDE, 1), ("narrow", 2)), 1)
    padded = jnp.pad(padded, ((0, 0), (0, 0), (0, 0), (1, 1)))
    return stencil(padded, couplings, diagonal)


def relax_once(iterate, source, couplings, diagonal):
    return iterate + DAMPING * (source - operate(iterate, couplings, diagonal)) / diagonal[None]


def multigrid(source, level_index, operators):
    couplings, diagonal = operators[level_index]
    iterate = DAMPING * source / diagonal[None]
    if level_index == LEVELS - 1:
        return relax_once(iterate, source, couplings, diagonal)
    iterate = relax_once(iterate, source, couplings, diagonal)
    residual = source - operate(iterate, couplings, diagonal)
    correction = multigrid(coarsen(residual), level_index + 1, operators)
    iterate = iterate + refine(correction)
    iterate = relax_once(iterate, source, couplings, diagonal)
    return relax_once(iterate, source, couplings, diagonal)


def inner_sums(adjoint_b, sav_vector, cotangent):
    numerator, denominator = (
        by_axis(jnp.sum(adjoint_b * cotangent), WIDE_NARROW),
        by_axis(jnp.sum(sav_vector * adjoint_b), WIDE_NARROW),
    )
    return numerator / (1.0 + denominator)


def per_device(mobility, sav_vector, cotangent):
    operators = []
    mobile = mobility
    for level_index in range(LEVELS):
        tau = BASE_TAU / 4.0**level_index
        padded = with_halo(mobile, ((WIDE, 0), ("narrow", 1)), 1)
        padded = jnp.pad(padded, ((0, 0), (0, 0), (1, 1)))
        operators.append(face_terms(padded, tau))
        if level_index + 1 < LEVELS:
            mobile = coarsen(mobile[None])[0]
    paired = multigrid(jnp.stack([sav_vector, cotangent]), 0, operators)
    sav_ratio = inner_sums(paired[0], sav_vector, cotangent)
    return paired[1] - sav_ratio * paired[0]


def solution(mesh):
    split = Mesh(
        mesh.devices.reshape(4, 16, 2, mesh.shape["narrow"]),
        ("wide_0", "wide_1", "wide_2", "narrow"),
    )
    in_specs = (P(WIDE, "narrow", None), P(WIDE, "narrow", None), P(WIDE, "narrow", None))
    out_specs = P(WIDE, "narrow", None)
    return jax.shard_map(
        per_device, mesh=split, in_specs=in_specs, out_specs=out_specs, check_vma=False
    )
```

profile of v0, /device:TPU:1, one launch (start us, length us, event | category | flops | bytes accessed | tf_op | source)
XLA Modules:
  0.0 471.2 jit_solution(6358361139262738748)
XLA Ops:
  0.7 4.9 %collective-permute-start.1 = (f32[1,16,256]{2,1,0:T(8,128)S(1)}, f32[1,16,256]{2,1,0:T(8,128)S(1)}, u32[]{:S(2)}, u32[]{:S(2)}) collective-permute-start(f32[1,16,256]{2,1,0:T(8,128)S(1)} %get-tuple-element.61), channel_id=1, source_target_pairs={{0,4},{4,8},{8,12},{12,16},{16,20},{20,24},{24,28},{28,32},{32,36}... | collective-permute-start | bytes 49160 | tf_op jit(solution)/shard_map/ppermute | solution.py:26
  5.7 18.9 %reshape_broadcast_in_dim.3 = f32[8,2,8,2,128,2]{5,4,3,2,1,0:T(8,128)} reshape(f32[16,16,256]{2,1,0:T(8,128)} %param.3) | data formatting | bytes 524288 | tf_op jit(solution)/shard_map/reshape;broadcast_in_dim | solution.py:61
  24.5 7.0 %reduce_sum.105 = f32[8,8,128]{2,1,0:T(8,128)S(1)} reduce(f32[8,2,8,2,128,2]{5,4,3,2,1,0:T(8,128)} %reshape_broadcast_in_dim.3, f32[]{:T(128)} %constant.16.clone.1), dimensions={1,3,5}, to_apply=%region_1.2 | reduce | flops 57344 | bytes 294916 | tf_op jit(solution)/shard_map/reduce_sum | solution.py:62
  50.5 6.8 %collective-permute-start = (f32[1,16,256]{2,1,0:T(8,128)S(1)}, f32[1,16,256]{2,1,0:T(8,128)S(1)}, u32[]{:S(2)}, u32[]{:S(2)}) collective-permute-start(f32[1,16,256]{2,1,0:T(8,128)S(1)} %get-tuple-element.62), channel_id=1, source_target_pairs={{4,0},{8,4},{12,8},{16,12},{20,16},{24,20},{28,24},{32,28},{36,32}... | collective-permute-start | bytes 49160 | tf_op jit(solution)/shard_map/ppermute | solution.py:27
  93.0 4.8 %collective-permute-start.9 = (f32[2,1,16,256]{3,2,1,0:T(8,128)S(1)}, f32[2,1,16,256]{3,2,1,0:T(8,128)S(1)}, u32[]{:S(2)}, u32[]{:S(2)}) collective-permute-start(f32[2,1,16,256]{3,2,1,0:T(8,128)S(1)} %get-tuple-element.51), channel_id=1, source_target_pairs={{0,4},{4,8},{8,12},{12,16},{16,20},{20,24},{24,28},{28,32},{32,36}... | collective-permute-start | bytes 98312 | tf_op jit(solution)/shard_map/ppermute | solution.py:26
  103.8 34.8 %reshape.384 = f32[2,8,2,8,2,128,2]{6,5,4,3,2,1,0:T(8,128)} reshape(f32[2,16,16,256]{3,2,1,0:T(8,128)S(1)} %fusion.32) | data formatting | bytes 1048576 | tf_op jit(solution)/shard_map/reshape | solution.py:61
  138.6 12.2 %reduce_sum.104 = f32[2,8,8,128]{3,2,1,0:T(8,128)S(1)} reduce(f32[2,8,2,8,2,128,2]{6,5,4,3,2,1,0:T(8,128)} %reshape.384, f32[]{:T(128)} %constant.16.clone.1), dimensions={2,4,6}, to_apply=%region_0.1 | reduce | flops 114688 | bytes 589828 | tf_op jit(solution)/shard_map/reduce_sum | solution.py:62
  158.1 4.4 collective-permute-start.17
  170.7 4.8 %collective-permute-start.21 = (f32[2,1,8,128]{3,2,1,0:T(8,128)S(1)}, f32[2,1,8,128]{3,2,1,0:T(8,128)S(1)}, u32[]{:S(2)}, u32[]{:S(2)}) collective-permute-start(f32[2,1,8,128]{3,2,1,0:T(8,128)S(1)} %get-tuple-element.71), channel_id=1, source_target_pairs={{0,4},{4,8},{8,12},{12,16},{16,20},{20,24},{24,28},{28,32},{32,36}... | collective-permute-start | bytes 24584 | tf_op jit(solution)/shard_map/ppermute | solution.py:26
  180.3 5.5 %reshape.385 = f32[2,4,2,4,2,64,2]{6,5,4,3,2,1,0:T(8,128)} reshape(f32[2,8,8,128]{3,2,1,0:T(8,128)S(1)} %fusion.110) | data formatting | bytes 131072 | tf_op jit(solution)/shard_map/reshape | solution.py:61
  208.1 4.7 %collective-permute-start.33 = (f32[2,1,4,64]{3,2,1,0:T(4,128)S(1)}, f32[2,1,4,64]{3,2,1,0:T(4,128)S(1)}, u32[]{:S(2)}, u32[]{:S(2)}) collective-permute-start(f32[2,1,4,64]{3,2,1,0:T(4,128)S(1)} %get-tuple-element.93), channel_id=1, source_target_pairs={{0,4},{4,8},{8,12},{12,16},{16,20},{20,24},{24,28},{28,32},{32,36}... | collective-permute-start | bytes 6152 | tf_op jit(solution)/shard_map/ppermute | solution.py:26
  241.7 4.7 %collective-permute-start.45 = (f32[2,1,2,32]{3,2,1,0:T(2,128)S(1)}, f32[2,1,2,32]{3,2,1,0:T(2,128)S(1)}, u32[]{:S(2)}, u32[]{:S(2)}) collective-permute-start(f32[2,1,2,32]{3,2,1,0:T(2,128)S(1)} %get-tuple-element.118), channel_id=1, source_target_pairs={{0,4},{4,8},{8,12},{12,16},{16,20},{20,24},{24,28},{28,32},{32,36}... | collective-permute-start | bytes 1544 | tf_op jit(solution)/shard_map/ppermute | solution.py:26
  261.2 4.2 collective-permute-start.59
  267.4 6.0 %collective-permute-start.57 = (f32[2,1,2,32]{3,2,1,0:T(2,128)S(1)}, f32[2,1,2,32]{3,2,1,0:T(2,128)S(1)}, u32[]{:S(2)}, u32[]{:S(2)}) collective-permute-start(f32[2,1,2,32]{3,2,1,0:T(2,128)S(1)} %get-tuple-element.114), channel_id=1, source_target_pairs={{0,4},{4,8},{8,12},{12,16},{16,20},{20,24},{24,28},{28,32},{32,36}... | collective-permute-start | bytes 1544 | tf_op jit(solution)/shard_map/ppermute | solution.py:26
  275.6 4.3 collective-permute-start.63
  281.8 4.5 collective-permute-start.61
  288.9 4.3 collective-permute-start.67
  295.1 4.5 collective-permute-start.65
  301.9 4.3 collective-permute-start.71
  308.1 4.5 collective-permute-start.69
  315.5 4.3 collective-permute-start.75
  321.7 4.5 collective-permute-start.73
  328.7 4.3 collective-permute-start.79
  334.9 4.5 collective-permute-start.77
  350.7 4.3 collective-permute-start.83
  356.9 4.7 collective-permute-start.81
  365.1 4.3 collective-permute-start.87
  371.3 4.5 collective-permute-start.85
  378.9 45.3 %all-reduce.68 = (f32[]{:T(128)}, f32[]{:T(128)}) all-reduce(f32[]{:T(128)} %get-tuple-element.6, f32[]{:T(128)} %get-tuple-element.5), channel_id=1, replica_groups=mesh['wide_0'=4,'wide_1'=16,'wide_2'=2,'narrow'=4] {'wide_0'}, use_global_device_ids=true, to_apply=%region_11.12 | all-reduce | flops 2 | bytes 16 | tf_op jit(solution)/shard_map/psum | solution.py:39
  424.2 22.4 %all-reduce.66 = (f32[]{:T(128)}, f32[]{:T(128)}) all-reduce(f32[]{:T(128)} %get-tuple-element.11, f32[]{:T(128)} %get-tuple-element.12), channel_id=1, replica_groups=mesh['wide_0'=4,'wide_1'=16,'wide_2'=2,'narrow'=4] {'wide_1'}, use_global_device_ids=true, to_apply=%region_12.13 | all-reduce | flops 2 | bytes 16 | tf_op jit(solution)/shard_map/psum | solution.py:39
  446.6 14.3 %all-reduce.69 = (f32[]{:T(128)}, f32[]{:T(128)}) all-reduce(f32[]{:T(128)} %get-tuple-element.7, f32[]{:T(128)} %get-tuple-element.8), channel_id=1, replica_groups=mesh['wide_0'=4,'wide_1'=16,'wide_2'=2,'narrow'=4] {'wide_2'}, use_global_device_ids=true, to_apply=%region_13.14 | all-reduce | flops 2 | bytes 16 | tf_op jit(solution)/shard_map/psum | solution.py:39
  460.9 8.2 %all-reduce.67 = (f32[]{:T(128)}, f32[]{:T(128)}) all-reduce(f32[]{:T(128)} %get-tuple-element.13, f32[]{:T(128)} %get-tuple-element.14), channel_id=1, replica_groups=mesh['wide_0'=4,'wide_1'=16,'wide_2'=2,'narrow'=4] {'narrow'}, use_global_device_ids=true, to_apply=%region_14.15 | all-reduce | flops 2 | bytes 16 | tf_op jit(solution)/shard_map/psum | solution.py:39
  (371 shorter events, 191.8 us)
Async XLA Ops:
  0.7 64.0 %collective-permute-start.1 = (f32[1,16,256]{2,1,0:T(8,128)S(1)}, f32[1,16,256]{2,1,0:T(8,128)S(1)}, u32[]{:S(2)}, u32[]{:S(2)}) collective-permute-start(f32[1,16,256]{2,1,0:T(8,128)S(1)} %get-tuple-element.61), channel_id=1, source_target_pairs={{0,4},{4,8},{8,12},{12,16},{16,20},{20,24},{24,28},{28,32},{32,36}... | collective-permute-start | bytes 49160 | tf_op jit(solution)/shard_map/ppermute | solution.py:26
  31.5 27.2 %collective-permute-start.14 = (f32[8,1,128]{2,1,0:T(1,128)S(1)}, f32[8,1,128]{2,1,0:T(1,128)S(1)}, u32[]{:S(2)}, u32[]{:S(2)}) collective-permute-start(f32[8,1,128]{2,1,0:T(1,128)S(1)} %get-tuple-element.80), channel_id=1, source_target_pairs={{1,0},{2,1},{3,2},{5,4},{6,5},{7,6},{9,8},{10,9},{11,10},{13,12},{... | collective-permute-start | bytes 12296 | tf_op jit(solution)/shard_map/ppermute | solution.py:27
  32.8 29.9 %collective-permute-start.15 = (f32[8,1,128]{2,1,0:T(1,128)S(1)}, f32[8,1,128]{2,1,0:T(1,128)S(1)}, u32[]{:S(2)}, u32[]{:S(2)}) collective-permute-start(f32[8,1,128]{2,1,0:T(1,128)S(1)} %get-tuple-element.79), channel_id=1, source_target_pairs={{0,1},{1,2},{2,3},{4,5},{5,6},{6,7},{8,9},{9,10},{10,11},{12,13},{... | collective-permute-start | bytes 12296 | tf_op jit(solution)/shard_map/ppermute | solution.py:26
  50.5 19.8 %collective-permute-start = (f32[1,16,256]{2,1,0:T(8,128)S(1)}, f32[1,16,256]{2,1,0:T(8,128)S(1)}, u32[]{:S(2)}, u32[]{:S(2)}) collective-permute-start(f32[1,16,256]{2,1,0:T(8,128)S(1)} %get-tuple-element.62), channel_id=1, source_target_pairs={{4,0},{8,4},{12,8},{16,12},{20,16},{24,20},{28,24},{32,28},{36,32}... | collective-permute-start | bytes 49160 | tf_op jit(solution)/shard_map/ppermute | solution.py:27
  62.7 14.6 %collective-permute-start.12 = (f32[1,8,128]{2,1,0:T(8,128)S(1)}, f32[1,8,128]{2,1,0:T(8,128)S(1)}, u32[]{:S(2)}, u32[]{:S(2)}) collective-permute-start(f32[1,8,128]{2,1,0:T(8,128)S(1)} %get-tuple-element.82), channel_id=1, source_target_pairs={{4,0},{8,4},{12,8},{16,12},{20,16},{24,20},{28,24},{32,28},{36,32}... | collective-permute-start | bytes 12296 | tf_op jit(solution)/shard_map/ppermute | solution.py:27
  64.8 14.4 %collective-permute-start.13 = (f32[1,8,128]{2,1,0:T(8,128)S(1)}, f32[1,8,128]{2,1,0:T(8,128)S(1)}, u32[]{:S(2)}, u32[]{:S(2)}) collective-permute-start(f32[1,8,128]{2,1,0:T(8,128)S(1)} %get-tuple-element.81), channel_id=1, source_target_pairs={{0,4},{4,8},{8,12},{12,16},{16,20},{20,24},{24,28},{28,32},{32,36}... | collective-permute-start | bytes 12296 | tf_op jit(solution)/shard_map/ppermute | solution.py:26
  68.4 87.8 %collective-permute-start.24 = (f32[1,4,64]{2,1,0:T(4,128)S(1)}, f32[1,4,64]{2,1,0:T(4,128)S(1)}, u32[]{:S(2)}, u32[]{:S(2)}) collective-permute-start(f32[1,4,64]{2,1,0:T(4,128)S(1)} %get-tuple-element.104), channel_id=1, source_target_pairs={{4,0},{8,4},{12,8},{16,12},{20,16},{24,20},{28,24},{32,28},{36,32}... | collective-permute-start | bytes 3080 | tf_op jit(solution)/shard_map/ppermute | solution.py:27
  85.8 12.1 %collective-permute-start.10 = (f32[2,16,1,256]{3,1,2,0:T(8,128)S(1)}, f32[2,16,1,256]{3,1,2,0:T(8,128)S(1)}, u32[]{:S(2)}, u32[]{:S(2)}) collective-permute-start(f32[2,16,1,256]{3,1,2,0:T(8,128)S(1)} %copy.371), channel_id=1, source_target_pairs={{1,0},{2,1},{3,2},{5,4},{6,5},{7,6},{9,8},{10,9},{11,10},{13,12},{... | collective-permute-start | bytes 98312 | tf_op jit(solution)/shard_map/ppermute | solution.py:27
  87.1 13.3 %collective-permute-start.11 = (f32[2,16,1,256]{3,1,2,0:T(8,128)S(1)}, f32[2,16,1,256]{3,1,2,0:T(8,128)S(1)}, u32[]{:S(2)}, u32[]{:S(2)}) collective-permute-start(f32[2,16,1,256]{3,1,2,0:T(8,128)S(1)} %copy.373), channel_id=1, source_target_pairs={{0,1},{1,2},{2,3},{4,5},{5,6},{6,7},{8,9},{9,10},{10,11},{12,13},{... | collective-permute-start | bytes 98312 | tf_op jit(solution)/shard_map/ppermute | solution.py:26
  97.9 60.2 %collective-permute-start.25 = (f32[1,4,64]{2,1,0:T(4,128)S(1)}, f32[1,4,64]{2,1,0:T(4,128)S(1)}, u32[]{:S(2)}, u32[]{:S(2)}) collective-permute-start(f32[1,4,64]{2,1,0:T(4,128)S(1)} %get-tuple-element.103), channel_id=1, source_target_pairs={{0,4},{4,8},{8,12},{12,16},{16,20},{20,24},{24,28},{28,32},{32,36}... | collective-permute-start | bytes 3080 | tf_op jit(solution)/shard_map/ppermute | solution.py:26
  100.4 93.3 %collective-permute-start.36 = (f32[1,2,32]{2,1,0:T(2,128)S(1)}, f32[1,2,32]{2,1,0:T(2,128)S(1)}, u32[]{:S(2)}, u32[]{:S(2)}) collective-permute-start(f32[1,2,32]{2,1,0:T(2,128)S(1)} %get-tuple-element.132), channel_id=1, source_target_pairs={{4,0},{8,4},{12,8},{16,12},{20,16},{24,20},{28,24},{32,28},{36,32}... | collective-permute-start | bytes 776 | tf_op jit(solution)/shard_map/ppermute | solution.py:27
  163.5 12.1 %collective-permute-start.22 = (f32[2,8,1,128]{3,1,2,0:T(8,128)S(1)}, f32[2,8,1,128]{3,1,2,0:T(8,128)S(1)}, u32[]{:S(2)}, u32[]{:S(2)}) collective-permute-start(f32[2,8,1,128]{3,1,2,0:T(8,128)S(1)} %bitcast.133), channel_id=1, source_target_pairs={{1,0},{2,1},{3,2},{5,4},{6,5},{7,6},{9,8},{10,9},{11,10},{13,12},{... | collective-permute-start | bytes 24584 | tf_op jit(solution)/shard_map/ppermute | solution.py:27
  164.8 13.2 %collective-permute-start.23 = (f32[2,8,1,128]{3,1,2,0:T(8,128)S(1)}, f32[2,8,1,128]{3,1,2,0:T(8,128)S(1)}, u32[]{:S(2)}, u32[]{:S(2)}) collective-permute-start(f32[2,8,1,128]{3,1,2,0:T(8,128)S(1)} %bitcast.132), channel_id=1, source_target_pairs={{0,1},{1,2},{2,3},{4,5},{5,6},{6,7},{8,9},{9,10},{10,11},{12,13},{... | collective-permute-start | bytes 24584 | tf_op jit(solution)/shard_map/ppermute | solution.py:26
  175.5 20.1 %collective-permute-start.37 = (f32[1,2,32]{2,1,0:T(2,128)S(1)}, f32[1,2,32]{2,1,0:T(2,128)S(1)}, u32[]{:S(2)}, u32[]{:S(2)}) collective-permute-start(f32[1,2,32]{2,1,0:T(2,128)S(1)} %get-tuple-element.131), channel_id=1, source_target_pairs={{0,4},{4,8},{8,12},{12,16},{16,20},{20,24},{24,28},{28,32},{32,36}... | collective-permute-start | bytes 776 | tf_op jit(solution)/shard_map/ppermute | solution.py:26
  178.0 44.9 %collective-permute-start.48 = (f32[1,1,16]{2,1,0:T(1,128)S(1)}, f32[1,1,16]{2,1,0:T(1,128)S(1)}, u32[]{:S(2)}, u32[]{:S(2)}) collective-permute-start(f32[1,1,16]{2,1,0:T(1,128)S(1)} %multiply_bitcast_fusion), channel_id=1, source_target_pairs={{4,0},{8,4},{12,8},{16,12},{20,16},{24,20},{28,24},{32,28},{36,32}... | collective-permute-start | bytes 200 | tf_op jit(solution)/shard_map/ppermute | solution.py:27
  200.8 12.1 %collective-permute-start.34 = (f32[2,4,1,64]{3,2,1,0:T(1,128)S(1)}, f32[2,4,1,64]{3,2,1,0:T(1,128)S(1)}, u32[]{:S(2)}, u32[]{:S(2)}) collective-permute-start(f32[2,4,1,64]{3,2,1,0:T(1,128)S(1)} %get-tuple-element.96), channel_id=1, source_target_pairs={{1,0},{2,1},{3,2},{5,4},{6,5},{7,6},{9,8},{10,9},{11,10},{13,12},{... | collective-permute-start | bytes 6152 | tf_op jit(solution)/shard_map/ppermute | solution.py:27
  202.1 13.2 %collective-permute-start.35 = (f32[2,4,1,64]{3,2,1,0:T(1,128)S(1)}, f32[2,4,1,64]{3,2,1,0:T(1,128)S(1)}, u32[]{:S(2)}, u32[]{:S(2)}) collective-permute-start(f32[2,4,1,64]{3,2,1,0:T(1,128)S(1)} %get-tuple-element.95), channel_id=1, source_target_pairs={{0,1},{1,2},{2,3},{4,5},{5,6},{6,7},{8,9},{9,10},{10,11},{12,13},{... | collective-permute-start | bytes 6152 | tf_op jit(solution)/shard_map/ppermute | solution.py:26
  208.1 12.6 %collective-permute-start.33 = (f32[2,1,4,64]{3,2,1,0:T(4,128)S(1)}, f32[2,1,4,64]{3,2,1,0:T(4,128)S(1)}, u32[]{:S(2)}, u32[]{:S(2)}) collective-permute-start(f32[2,1,4,64]{3,2,1,0:T(4,128)S(1)} %get-tuple-element.93), channel_id=1, source_target_pairs={{0,4},{4,8},{8,12},{12,16},{16,20},{20,24},{24,28},{28,32},{32,36}... | collective-permute-start | bytes 6152 | tf_op jit(solution)/shard_map/ppermute | solution.py:26
  212.9 14.0 %collective-permute-start.49 = (f32[1,1,16]{2,1,0:T(1,128)S(1)}, f32[1,1,16]{2,1,0:T(1,128)S(1)}, u32[]{:S(2)}, u32[]{:S(2)}) collective-permute-start(f32[1,1,16]{2,1,0:T(1,128)S(1)} %multiply_bitcast_fusion), channel_id=1, source_target_pairs={{0,4},{4,8},{8,12},{12,16},{16,20},{20,24},{24,28},{28,32},{32,36}... | collective-permute-start | bytes 200 | tf_op jit(solution)/shard_map/ppermute | solution.py:26
  215.3 14.6 %collective-permute-start.50 = (f32[1,1,16]{2,1,0:T(1,128)S(1)}, f32[1,1,16]{2,1,0:T(1,128)S(1)}, u32[]{:S(2)}, u32[]{:S(2)}) collective-permute-start(f32[1,1,16]{2,1,0:T(1,128)S(1)} %multiply_bitcast_fusion), channel_id=1, source_target_pairs={{1,0},{2,1},{3,2},{5,4},{6,5},{7,6},{9,8},{10,9},{11,10},{13,12},{... | collective-permute-start | bytes 200 | tf_op jit(solution)/shard_map/ppermute | solution.py:27
  216.7 16.9 %collective-permute-start.51 = (f32[1,1,16]{2,1,0:T(1,128)S(1)}, f32[1,1,16]{2,1,0:T(1,128)S(1)}, u32[]{:S(2)}, u32[]{:S(2)}) collective-permute-start(f32[1,1,16]{2,1,0:T(1,128)S(1)} %multiply_bitcast_fusion), channel_id=1, source_target_pairs={{0,1},{1,2},{2,3},{4,5},{5,6},{6,7},{8,9},{9,10},{10,11},{12,13},{... | collective-permute-start | bytes 200 | tf_op jit(solution)/shard_map/ppermute | solution.py:26
  221.6 12.0 %collective-permute-start.42 = (f32[2,2,1,32]{3,2,1,0:T(1,128)S(1)}, f32[2,2,1,32]{3,2,1,0:T(1,128)S(1)}, u32[]{:S(2)}, u32[]{:S(2)}) collective-permute-start(f32[2,2,1,32]{3,2,1,0:T(1,128)S(1)} %get-tuple-element.125), channel_id=1, source_target_pairs={{1,0},{2,1},{3,2},{5,4},{6,5},{7,6},{9,8},{10,9},{11,10},{13,12},{... | collective-permute-start | bytes 1544 | tf_op jit(solution)/shard_map/ppermute | solution.py:27
  234.4 12.1 %collective-permute-start.46 = (f32[2,2,1,32]{3,2,1,0:T(1,128)S(1)}, f32[2,2,1,32]{3,2,1,0:T(1,128)S(1)}, u32[]{:S(2)}, u32[]{:S(2)}) collective-permute-start(f32[2,2,1,32]{3,2,1,0:T(1,128)S(1)} %get-tuple-element.121), channel_id=1, source_target_pairs={{1,0},{2,1},{3,2},{5,4},{6,5},{7,6},{9,8},{10,9},{11,10},{13,12},{... | collective-permute-start | bytes 1544 | tf_op jit(solution)/shard_map/ppermute | solution.py:27
  259.9 13.5 %collective-permute-start.58 = (f32[2,2,1,32]{3,2,1,0:T(1,128)S(1)}, f32[2,2,1,32]{3,2,1,0:T(1,128)S(1)}, u32[]{:S(2)}, u32[]{:S(2)}) collective-permute-start(f32[2,2,1,32]{3,2,1,0:T(1,128)S(1)} %get-tuple-element.117), channel_id=1, source_target_pairs={{1,0},{2,1},{3,2},{5,4},{6,5},{7,6},{9,8},{10,9},{11,10},{13,12},{... | collective-permute-start | bytes 1544 | tf_op jit(solution)/shard_map/ppermute | solution.py:27
  261.2 12.2 %collective-permute-start.59 = (f32[2,2,1,32]{3,2,1,0:T(1,128)S(1)}, f32[2,2,1,32]{3,2,1,0:T(1,128)S(1)}, u32[]{:S(2)}, u32[]{:S(2)}) collective-permute-start(f32[2,2,1,32]{3,2,1,0:T(1,128)S(1)} %get-tuple-element.116), channel_id=1, source_target_pairs={{0,1},{1,2},{2,3},{4,5},{5,6},{6,7},{8,9},{9,10},{10,11},{12,13},{... | collective-permute-start | bytes 1544 | tf_op jit(solution)/shard_map/ppermute | solution.py:26
  274.3 12.0 %collective-permute-start.62 = (f32[2,2,1,32]{3,2,1,0:T(1,128)S(1)}, f32[2,2,1,32]{3,2,1,0:T(1,128)S(1)}, u32[]{:S(2)}, u32[]{:S(2)}) collective-permute-start(f32[2,2,1,32]{3,2,1,0:T(1,128)S(1)} %get-tuple-element.113), channel_id=1, source_target_pairs={{1,0},{2,1},{3,2},{5,4},{6,5},{7,6},{9,8},{10,9},{11,10},{13,12},{... | collective-permute-start | bytes 1544 | tf_op jit(solution)/shard_map/ppermute | solution.py:27
  287.6 12.0 %collective-permute-start.66 = (f32[2,4,1,64]{3,2,1,0:T(1,128)S(1)}, f32[2,4,1,64]{3,2,1,0:T(1,128)S(1)}, u32[]{:S(2)}, u32[]{:S(2)}) collective-permute-start(f32[2,4,1,64]{3,2,1,0:T(1,128)S(1)} %get-tuple-element.92), channel_id=1, source_target_pairs={{1,0},{2,1},{3,2},{5,4},{6,5},{7,6},{9,8},{10,9},{11,10},{13,12},{... | collective-permute-start | bytes 6152 | tf_op jit(solution)/shard_map/ppermute | solution.py:27
  300.6 12.0 %collective-permute-start.70 = (f32[2,4,1,64]{3,2,1,0:T(1,128)S(1)}, f32[2,4,1,64]{3,2,1,0:T(1,128)S(1)}, u32[]{:S(2)}, u32[]{:S(2)}) collective-permute-start(f32[2,4,1,64]{3,2,1,0:T(1,128)S(1)} %get-tuple-element.88), channel_id=1, source_target_pairs={{1,0},{2,1},{3,2},{5,4},{6,5},{7,6},{9,8},{10,9},{11,10},{13,12},{... | collective-permute-start | bytes 6152 | tf_op jit(solution)/shard_map/ppermute | solution.py:27
  314.2 12.0 %collective-permute-start.74 = (f32[2,8,1,128]{3,1,2,0:T(8,128)S(1)}, f32[2,8,1,128]{3,1,2,0:T(8,128)S(1)}, u32[]{:S(2)}, u32[]{:S(2)}) collective-permute-start(f32[2,8,1,128]{3,1,2,0:T(8,128)S(1)} %bitcast.138), channel_id=1, source_target_pairs={{1,0},{2,1},{3,2},{5,4},{6,5},{7,6},{9,8},{10,9},{11,10},{13,12},{... | collective-permute-start | bytes 24584 | tf_op jit(solution)/shard_map/ppermute | solution.py:27
  327.4 12.0 %collective-permute-start.78 = (f32[2,8,1,128]{3,1,2,0:T(8,128)S(1)}, f32[2,8,1,128]{3,1,2,0:T(8,128)S(1)}, u32[]{:S(2)}, u32[]{:S(2)}) collective-permute-start(f32[2,8,1,128]{3,1,2,0:T(8,128)S(1)} %bitcast.139), channel_id=1, source_target_pairs={{1,0},{2,1},{3,2},{5,4},{6,5},{7,6},{9,8},{10,9},{11,10},{13,12},{... | collective-permute-start | bytes 24584 | tf_op jit(solution)/shard_map/ppermute | solution.py:27
  349.2 12.4 %collective-permute-start.82 = (f32[2,16,1,256]{3,1,2,0:T(8,128)S(1)}, f32[2,16,1,256]{3,1,2,0:T(8,128)S(1)}, u32[]{:S(2)}, u32[]{:S(2)}) collective-permute-start(f32[2,16,1,256]{3,1,2,0:T(8,128)S(1)} %copy.399), channel_id=1, source_target_pairs={{1,0},{2,1},{3,2},{5,4},{6,5},{7,6},{9,8},{10,9},{11,10},{13,12},{... | collective-permute-start | bytes 98312 | tf_op jit(solution)/shard_map/ppermute | solution.py:27
  363.8 12.0 %collective-permute-start.86 = (f32[2,16,1,256]{3,1,2,0:T(8,128)S(1)}, f32[2,16,1,256]{3,1,2,0:T(8,128)S(1)}, u32[]{:S(2)}, u32[]{:S(2)}) collective-permute-start(f32[2,16,1,256]{3,1,2,0:T(8,128)S(1)} %copy.403), channel_id=1, source_target_pairs={{1,0},{2,1},{3,2},{5,4},{6,5},{7,6},{9,8},{10,9},{11,10},{13,12},{... | collective-permute-start | bytes 98312 | tf_op jit(solution)/shard_map/ppermute | solution.py:27
  (71 other events, 734.8 us)
where the time goes:
time: 475 us; the launch traced here: 471 us
  starting transfers between devices  260 us (55%)
  blocking collectives  90.2 us (19%)
  local copies, waits for them, and re-layouts  74.6 us (16%)
  other arithmetic  33.6 us (7%)
  waiting for transfers between devices  9.22 us (2%)
    ppermute x44, starting transfers between devices, with_halo(): lax.ppermute(last, axis, up)  183 us
    psum x4, blocking collectives, by_axis(): return functools.reduce(lax.psum, axes, shard)  90.2 us
    ppermute x44, starting transfers between devices, with_halo(): lax.ppermute(initial, axis, [(b, a) for a, b in up])  76.9 us
    reshape x3, local copies, waits for them, and re-layouts, coarsen(): values.reshape(count, size_x // 2, 2, size_y // 2, 2, size_z // 2, 2)  40.9 us
    reduce_sum x10, other arithmetic, coarsen(): return blocks.mean(axis=(2, 4, 6))  22.5 us
    another operation x1, local copies, waits for them, and re-layouts, coarsen(): values.reshape(count, size_x // 2, 2, size_y // 2, 2, size_z // 2, 2)  18.9 us
  transfers between devices with their start and end apart: 88, of which 14 were waited for; matrix products, arithmetic and copies ran while one was open for 19% of the time, Pallas kernels for 0%

commit v1 on v0

v1 whole, which is shorter than its diff:
```python
import functools

import jax
import jax.numpy as jnp
from jax import lax
from jax.experimental import pallas as pl
from jax.experimental.pallas import tpu as pltpu
from jax.sharding import PartitionSpec as P

f32 = jnp.float32
HALO = 4
DAMPING = 0.8
BASE_TAU = 16.0
VMEM = pl.BlockSpec(memory_space=pltpu.VMEM)


def half_tau(level):
    return 0.5 * BASE_TAU / 4.0**level


def iota(shape, dim):
    return lax.broadcasted_iota(jnp.int32, shape, dim)


def dot(a, b):
    return jnp.dot(a, b, precision=lax.Precision.HIGHEST, preferred_element_type=f32)


def rounded(x):
    return x.astype(jnp.bfloat16).astype(f32)


def ahead(x, axis):
    return pltpu.roll(x, x.shape[axis] - 1, axis)


def behind(x, axis):
    return pltpu.roll(x, 1, axis)


def coefficients(level, m, cx, cy, cz, dg, wt, rows, y_len, z_len, z_fields):
    shape = m.shape[1:]
    tau = half_tau(level)
    lane = iota(shape, 1)
    z_last = lax.rem(lane, z_len) == z_len - 1
    z_first = lax.rem(lane, z_len) == 0
    sub = iota(shape, 0)

    def couple_x(i):
        return rounded(tau * (m[i] + m[i + 1]))

    cx[0] = couple_x(0)

    def body(i, _):
        here = m[i]
        edge = rounded(tau * here)
        x_up = couple_x(i)
        cx[i] = x_up
        y_up = rounded(tau * (here + ahead(here, 0)))
        if y_len is None:
            y_down = behind(y_up, 0)
            cy[i] = y_up
        else:
            inner = jnp.where(sub >= y_len - 1, 0.0, y_up)
            y_up = jnp.where(sub == y_len - 1, edge, y_up)
            y_down = jnp.where(sub == 0, edge, behind(inner, 0))
            cy[i] = inner
        inner = jnp.where(z_last, 0.0, rounded(tau * (here + ahead(here, 1))))
        cz[i] = inner
        z_up = jnp.where(z_last, edge, inner)
        z_down = jnp.where(z_first, edge, behind(inner, 1))
        diagonal = 1.0 + x_up + cx[i - 1] + y_up + y_down + z_up + z_down
        dg[i] = diagonal
        wt[i] = jnp.where(here > 0.0, DAMPING / diagonal, 0.0)
        return 0

    lax.fori_loop(1, rows - 1, body, 0)


def residual_row(i, r, v, cx, cy, cz, dg):
    here = v[i]
    up = cy[i]
    side = cz[i]
    total = cx[i] * v[i + 1] + cx[i - 1] * v[i - 1]
    total = total + (up * ahead(here, 0) + behind(up * here, 0))
    total = total + (side * ahead(here, 1) + behind(side * here, 1))
    return r - dg[i] * here + total


def sweep(lo, hi, source, v, out, coefs, wt, offset=0):
    def body(i, _):
        for s, a, o in zip(source, v, out):
            o[i] = a[i] + wt[i] * residual_row(i, s[i - offset], a, *coefs)
        return 0

    lax.fori_loop(lo, hi, body, 0)


def coarse_z(z_in, lanes_in, z_out, lanes_out, fields, shift=0, single=False):
    src = iota((lanes_in, lanes_out), 0)
    dst = iota((lanes_in, lanes_out), 1)
    target = lax.div(src, z_in) * z_out + lax.div(lax.rem(src, z_in), 2) + shift
    return jnp.where((target == dst) & (src < fields * z_in), 0.125, 0.0).astype(f32)


def fine_z(z_in, lanes_in, z_out, lanes_out, fields, shift=0):
    src = iota((lanes_in, lanes_out), 0)
    dst = iota((lanes_in, lanes_out), 1)
    wanted = lax.div(dst, z_out) * z_in + lax.div(lax.rem(dst, z_out), 2) + shift
    return jnp.where((wanted == src) & (dst < fields * z_out), 1.0, 0.0).astype(f32)


def down0(own, xlo, xhi, out, vs, vc, cx, cy, cz, dg, wt, ss, cc, m, us, uc, pair, thin):
    for index, ref in enumerate((m, ss, cc)):

        def copy_edge(i, _, index=index, ref=ref):
            ref[i] = xlo[index, i]
            ref[i + 20] = xhi[index, i]
            return 0

        def copy_own(i, _, index=index, ref=ref):
            ref[i + 4] = own[index, i]
            return 0

        lax.fori_loop(0, 4, copy_edge, 0)
        lax.fori_loop(0, 16, copy_own, 0)
    coefficients(0, m, cx, cy, cz, dg, wt, 24, None, 256, 1)
    coefs = (cx, cy, cz, dg)

    def first(i, _):
        us[i] = wt[i] * ss[i]
        uc[i] = wt[i] * cc[i]
        return 0

    lax.fori_loop(1, 23, first, 0)
    sweep(2, 22, (ss, cc), (us, uc), (vs, vc), coefs, wt)
    for ref in (vs, vc):
        for row in (0, 1, 22, 23):
            ref[row] = jnp.zeros((24, 256), f32)

    def rest(k, sums):
        num, den = sums
        folded = [0.0, 0.0]
        for half in range(2):
            i = 4 + 2 * k + half
            res_s = residual_row(i, ss[i], vs, *coefs)
            res_c = residual_row(i, cc[i], vc, *coefs)
            num = num + (vs[i] * cc[i] + res_s * vc[i])
            den = den + (vs[i] * ss[i] + res_s * vs[i])
            folded[0] = folded[0] + res_s
            folded[1] = folded[1] + res_c
        pair[k] = folded[0]
        pair[k + 8] = folded[1]
        pair[k + 16] = m[4 + 2 * k] + m[5 + 2 * k]
        return num, den

    zero = jnp.zeros((24, 256), f32)
    num, den = lax.fori_loop(0, 8, rest, (zero, zero))
    thin[...] = dot(pair[...].reshape(576, 256), coarse_z(256, 256, 128, 128, 1))

    def fold(k, _):
        value = thin[pl.ds(k * 24 + 4, 8, stride=2), :] + thin[pl.ds(k * 24 + 5, 8, stride=2), :]
        for j in range(4):
            out[j, k] = value
        return 0

    lax.fori_loop(0, 24, fold, 0)
    sub = iota((24, 256), 0)
    inside = (sub >= 4) & (sub < 20)
    num = jnp.sum(jnp.where(inside, num, 0.0))
    den = jnp.sum(jnp.where(inside, den, 0.0))
    lane = iota((8, 128), 1)
    both = jnp.where(lane == 0, num, jnp.where(lane == 1, den, 0.0))
    for j in range(4):
        out[j, 24] = both


def down1(lo, own, hi, to_up, to_down, mine, sums, vs, vc, cx, cy, cz, dg, wt, ss, cc, m, us, uc, pair, thin):
    for part, ref in enumerate((lo, own, hi)):

        def copy(i, _, part=part, ref=ref):
            for j in range(4):
                for index, target in enumerate((ss, cc, m)):
                    target[2 + part * 8 + i, pl.ds(8 * j, 8), :] = ref[j, index * 8 + i]
            return 0

        lax.fori_loop(0, 8, copy, 0)
    for ref in (ss, cc, m, vs, vc):
        for row in (0, 1, 26, 27):
            ref[row] = jnp.zeros((32, 128), f32)
    coefficients(1, m, cx, cy, cz, dg, wt, 28, 32, 128, 1)
    coefs = (cx, cy, cz, dg)

    def first(i, _):
        us[i] = wt[i] * ss[i]
        uc[i] = wt[i] * cc[i]
        return 0

    lax.fori_loop(1, 27, first, 0)
    sweep(2, 26, (ss, cc), (us, uc), (vs, vc), coefs, wt)

    def rest(k, sums):
        num, den = sums
        folded = [0.0, 0.0]
        mask = jnp.where((k >= 4) & (k < 8), 1.0, 0.0)
        for half in range(2):
            i = 2 + 2 * k + half
            res_s = residual_row(i, ss[i], vs, *coefs)
            res_c = residual_row(i, cc[i], vc, *coefs)
            num = num + mask * (vs[i] * cc[i] + res_s * vc[i])
            den = den + mask * (vs[i] * ss[i] + res_s * vs[i])
            folded[0] = folded[0] + res_s
            folded[1] = folded[1] + res_c
        pair[k, :, 0:128] = folded[0]
        pair[k, :, 128:256] = folded[1]
        return num, den

    zero = jnp.zeros((32, 128), f32)
    num, den = lax.fori_loop(0, 12, rest, (zero, zero))

    def rest_m(k, _):
        both = m[2 * k + 2] + m[2 * k + 3]
        pair[k + 12, :, 0:128] = both
        pair[k + 12, :, 128:256] = both
        return 0

    lax.fori_loop(0, 12, rest_m, 0)
    thin[...] = dot(pair[...].reshape(768, 256), coarse_z(128, 256, 64, 128, 2))

    def folded_row(k):
        return thin[pl.ds(k * 32, 16, stride=2), :] + thin[pl.ds(k * 32 + 1, 16, stride=2), :]

    place = lax.axis_index("wide")
    for k in range(12):
        value = folded_row(k)
        if k < 2:
            value = jnp.where(place == 1, value, 0.0)
        elif k >= 10:
            value = jnp.where(place == lax.axis_size("wide") - 2, value, 0.0)
        mine[k] = value
        if k < 10:
            to_up[k] = value
        if k >= 2:
            to_down[k - 2] = value

    def fold_m(k, _):
        mine[k + 12] = folded_row(k + 12)
        return 0

    lax.fori_loop(0, 12, fold_m, 0)
    lane = iota((16, 128), 1)
    for k in range(4):
        to_up[10 + k] = jnp.where(lane < 64, mine[12 + k], mine[16 + k])
        to_down[10 + k] = jnp.where(lane < 64, mine[16 + k], mine[20 + k])
    lane = iota((8, 128), 1)
    num = jnp.sum(num) * 8.0
    den = jnp.sum(den) * 8.0
    finer = own[0, 24] + own[1, 24] + own[2, 24] + own[3, 24]
    sums[...] = finer + jnp.where(lane == 0, num, jnp.where(lane == 1, den, 0.0))


def bottom(
    dn4, dn2, mine, up2, up4, finer, e2, sums,
    m2, r2, u2, v2, cx2, cy2, cz2, dg2, wt2,
    m3, r3, u3, v3, cx3, cy3, cz3, dg3, wt3,
    m4, r4, u4, v4, cx4, cy4, cz4, dg4, wt4,
    pair, thin, wide, add,
):
    lane16 = iota((16, 128), 1)

    def unpack(ref, first, r_at, m_at):
        def body(k, _):
            r2[r_at + k] = ref[first + k]
            return 0

        lax.fori_loop(0, 8, body, 0)

        def body_m(k, _):
            packed = ref[10 + k]
            other = pltpu.roll(packed, 64, 1)
            m2[m_at + k] = jnp.where(lane16 < 64, packed, other)
            m2[m_at + 4 + k] = jnp.where(lane16 < 64, other, packed)
            return 0

        lax.fori_loop(0, 4, body_m, 0)

    unpack(dn4, 2, 2, 0)
    unpack(dn2, 2, 10, 8)
    unpack(up2, 0, 26, 28)
    unpack(up4, 0, 34, 36)
    for k in range(2):
        r2[8 + k] = r2[8 + k] + dn2[k]
        r2[16 + k] = r2[16 + k] + mine[k]
        r2[26 + k] = r2[26 + k] + mine[10 + k]
        r2[34 + k] = r2[34 + k] + up2[8 + k]

    def body_own(k, _):
        r2[18 + k] = mine[2 + k]
        return 0

    lax.fori_loop(0, 8, body_own, 0)

    def body_own_m(k, _):
        m2[16 + k] = mine[12 + k]
        return 0

    lax.fori_loop(0, 12, body_own_m, 0)

    def relax(level, m, r, u, v, cx, cy, cz, dg, wt, rows, y_len, z_len, r_lo, r_hi):
        coefficients(level, m, cx, cy, cz, dg, wt, rows, y_len, z_len, 2)

        def first(i, _):
            u[i] = wt[i] * r[i]
            return 0

        lax.fori_loop(r_lo, r_hi, first, 0)
        sweep(r_lo + 1, r_hi - 1, (r,), (u,), (v,), (cx, cy, cz, dg), wt)

    def products(i, r, v, res, z_len):
        num = v * pltpu.roll(r, 128 - z_len, 1)
        den = v * r
        if res is not None:
            num = num + res * pltpu.roll(v, 128 - z_len, 1)
            den = den + res * v
        lane = iota(v.shape, 1)
        return jnp.where(lane < z_len, num, 0.0), jnp.where(lane < z_len, den, 0.0)

    def restrict(m, r, v, coefs, k_count, m_count, y_in, m_next, r_next, r_at, z_len, own_lo, own_hi):
        shape = r.shape[1:]

        def rest(k, sums):
            num, den = sums
            total = 0.0
            mask = jnp.where((k >= own_lo) & (k < own_hi), 1.0, 0.0)
            for half in range(2):
                i = 4 + 2 * k + half
                res = residual_row(i, r[i], v, *coefs)
                a, b = products(i, r[i], v[i], res, z_len)
                num = num + mask * a
                den = den + mask * b
                total = total + res
            pair[pl.ds(pl.multiple_of(k * y_in, 8), y_in), :] = total
            return num, den

        zero = jnp.zeros(shape, f32)
        num, den = lax.fori_loop(0, k_count, rest, (zero, zero))

        def rest_m(k, _):
            pair[pl.ds(pl.multiple_of((k_count + k) * y_in, 8), y_in), :] = m[2 * k] + m[2 * k + 1]
            return 0

        lax.fori_loop(0, m_count, rest_m, 0)
        n = (k_count + m_count) * y_in
        thin[0:n, :] = dot(pair[0:n, :], coarse_z(z_len, 128, z_len // 2, 128, 2))
        y_out = y_in // 2

        def folded(k):
            return (
                thin[pl.ds(k * y_in, y_out, stride=2), :] + thin[pl.ds(k * y_in + 1, y_out, stride=2), :]
            )

        def fold(k, _):
            r_next[r_at + k, 0:y_out, :] = folded(k)
            return 0

        def fold_m(k, _):
            m_next[k, 0:y_out, :] = folded(k_count + k)
            return 0

        lax.fori_loop(0, k_count, fold, 0)
        lax.fori_loop(0, m_count, fold_m, 0)
        return jnp.sum(num), jnp.sum(den)

    c2 = (cx2, cy2, cz2, dg2)
    c3 = (cx3, cy3, cz3, dg3)
    c4 = (cx4, cy4, cz4, dg4)
    relax(2, m2, r2, u2, v2, *c2, wt2, 44, 16, 64, 2, 42)
    num2, den2 = restrict(m2, r2, v2, c2, 18, 22, 16, m3, r3, 2, 64, 8, 10)
    relax(3, m3, r3, u3, v3, *c3, wt3, 22, 8, 32, 2, 20)
    m4[...] = jnp.zeros((11, 8, 128), f32)
    r4[...] = jnp.zeros((11, 8, 128), f32)
    num3, den3 = restrict(m3, r3, v3, c3, 7, 11, 8, m4, r4, 2, 32, 3, 4)
    relax(4, m4, r4, u4, v4, *c4, wt4, 11, 4, 16, 2, 9)
    a4, b4 = products(5, r4[5], v4[5], None, 16)
    num = 64.0 * num2 + 512.0 * num3 + 4096.0 * jnp.sum(a4)
    den = 64.0 * den2 + 512.0 * den3 + 4096.0 * jnp.sum(b4)
    lane = iota((8, 128), 1)
    total = finer[...] + jnp.where(lane == 0, num, jnp.where(lane == 1, den, 0.0))
    sums[...] = jnp.broadcast_to(total[0:1].reshape(1, 1, 128), sums.shape)

    def correct(k_lo, k_hi, coarse, y_in, v, at, z_len):
        y_out = 2 * y_in

        def body(k, _):
            value = coarse[k, 0:y_in, :]
            base = pl.multiple_of((k - k_lo) * y_out, 8)
            wide[pl.ds(base, y_in, stride=2), :] = value
            wide[pl.ds(base + 1, y_in, stride=2), :] = value
            return 0

        lax.fori_loop(k_lo, k_hi, body, 0)
        n = (k_hi - k_lo) * y_out
        add[0:n, :] = dot(wide[0:n, :], fine_z(z_len // 2, 128, z_len, 128, 2))

        def body_add(k, _):
            value = add[pl.ds(pl.multiple_of(k * y_out, 8), y_out), :]
            v[at + 2 * k] = v[at + 2 * k] + value
            v[at + 2 * k + 1] = v[at + 2 * k + 1] + value
            return 0

        lax.fori_loop(0, k_hi - k_lo, body_add, 0)

    correct(3, 8, v4, 4, v3, 6, 32)
    sweep(7, 15, (r3,), (v3,), (u3,), c3, wt3)
    sweep(8, 14, (r3,), (u3,), (v3,), c3, wt3)
    correct(8, 14, v3, 8, v2, 16, 64)
    sweep(17, 27, (r2,), (v2,), (u2,), c2, wt2)

    def last(i, _):
        e2[i - 18] = u2[i] + wt2[i] * residual_row(i, r2[i], u2, *c2)
        return 0

    lax.fori_loop(18, 26, last, 0)


def up(
    e2, vs1, vc1, cx1, cy1, cz1, dg1, wt1, ss1, cc1, vs0, vc0, cx0, cy0, cz0, dg0, wt0, ss0, cc0,
    out_s, out_c, as1, ac1, bs1, bc1, as0, ac0, bs0, bc0, wide, add, block, thick, full,
):
    c1 = (cx1, cy1, cz1, dg1)
    c0 = (cx0, cy0, cz0, dg0)

    def widen(k, _):
        value = e2[k]
        wide[pl.ds(k * 32, 16, stride=2), :] = value
        wide[pl.ds(k * 32 + 1, 16, stride=2), :] = value
        return 0

    lax.fori_loop(0, 8, widen, 0)
    add[...] = dot(wide[...], fine_z(64, 128, 128, 256, 2))

    def correct1(k, _):
        both = add[pl.ds(pl.multiple_of(k * 32, 8), 32), :]
        for half in range(2):
            i = 6 + 2 * k + half
            as1[i] = vs1[i] + both[:, 0:128]
            ac1[i] = vc1[i] + both[:, 128:256]
        return 0

    lax.fori_loop(0, 8, correct1, 0)
    sweep(8, 20, (ss1, cc1), (as1, ac1), (bs1, bc1), c1, wt1)
    place = lax.axis_index("narrow")
    block[...] = jnp.zeros((960, 128), f32)

    def last1(i, _):
        for index, (r, v) in enumerate(((ss1, bs1), (cc1, bc1))):
            value = v[i] + wt1[i] * residual_row(i, r[i], v, *c1)
            block[pl.ds(pl.multiple_of((index * 10 + i - 9) * 48 + 8, 8), 32), :] = value
        return 0

    lax.fori_loop(9, 19, last1, 0)

    def take(k, _):
        value = block[pl.ds(pl.multiple_of(k * 48 + 8 * place, 8), 24), :][6:18, :]
        thick[pl.ds(k * 24, 12, stride=2), :] = value
        thick[pl.ds(k * 24 + 1, 12, stride=2), :] = value
        return 0

    lax.fori_loop(0, 20, take, 0)
    full[...] = dot(thick[...], fine_z(128, 128, 256, 256, 1)).reshape(20, 24, 256)

    def correct0(k, _):
        for half in range(2):
            i = 2 + 2 * k + half
            as0[i] = vs0[i] + full[k]
            ac0[i] = vc0[i] + full[10 + k]
        return 0

    lax.fori_loop(0, 10, correct0, 0)
    sweep(3, 21, (ss0, cc0), (as0, ac0), (bs0, bc0), c0, wt0)

    def last0(i, _):
        for r, v, o in ((ss0, bs0, out_s), (cc0, bc0, out_c)):
            value = v[i] + wt0[i] * residual_row(i, r[i], v, *c0)
            o[i - 4] = value[4:20, :]
        return 0

    lax.fori_loop(4, 20, last0, 0)


def call(kernel, ins, outs, scratch, name):
    return pl.pallas_call(
        kernel,
        out_shape=[jax.ShapeDtypeStruct(s, f32) for s in outs],
        in_specs=[VMEM] * len(ins),
        out_specs=[VMEM] * len(outs),
        scratch_shapes=[pltpu.VMEM(s, f32) for s in scratch],
        compiler_params=pltpu.CompilerParams(vmem_limit_bytes=40 * 2**20),
        name=name,
    )(*ins)


def shifted(value, axis, by):
    size = lax.axis_size(axis)
    return lax.ppermute(value, axis, [(i, i + by) for i in range(size) if 0 <= i + by < size])


def per_device(mobility, sav_vector, cotangent):
    own = jnp.stack([mobility, sav_vector, cotangent])
    y_lo = shifted(own[:, :, -HALO:], "narrow", 1)
    y_hi = shifted(own[:, :, :HALO], "narrow", -1)
    own = jnp.concatenate([y_lo, own, y_hi], axis=2)
    x_lo = shifted(own[:, -HALO:], "wide", 1)
    x_hi = shifted(own[:, :HALO], "wide", -1)
    a0 = (24, 24, 256)
    chunk, *state0 = call(
        down0,
        (own, x_lo, x_hi),
        [(4, 25, 8, 128)] + [a0] * 9,
        [a0] * 4 + [(576, 128)],
        "down0",
    )
    gathered = lax.all_to_all(chunk, "narrow", 0, 0)
    lo = shifted(gathered, "wide", 1)
    hi = shifted(gathered, "wide", -1)
    a1 = (28, 32, 128)
    to_up, to_down, mine, finer, *state1 = call(
        down1,
        (lo, gathered, hi),
        [(14, 16, 128), (14, 16, 128), (24, 16, 128), (8, 128)] + [a1] * 9,
        [a1] * 3 + [(24, 32, 256), (768, 128)],
        "down1",
    )
    dn2 = shifted(to_up, "wide", 2)
    up2 = shifted(to_down, "wide", -2)
    dn4 = shifted(to_up, "wide", 4)
    up4 = shifted(to_down, "wide", -4)
    wide = lax.axis_size("wide")
    e2, sums = call(
        bottom,
        (dn4, dn2, mine, up2, up4, finer),
        [(8, 16, 128), (wide, 1, 128)],
        [(44, 16, 128)] * 9
        + [(22, 8, 128)] * 9
        + [(11, 8, 128)] * 9
        + [(640, 128), (640, 128), (96, 128), (96, 128)],
        "bottom",
    )
    every = lax.all_to_all(sums, "wide", 0, 0)
    out_s, out_c = call(
        up,
        (e2, *state1, *state0),
        [(16, 16, 256)] * 2,
        [a1] * 4 + [a0] * 4 + [(256, 128), (256, 256), (960, 128), (480, 128), (20, 24, 256)],
        "up",
    )
    totals = jnp.sum(every, axis=(0, 1))
    ratio = totals[0] / (1.0 + totals[1])
    return out_c - ratio * out_s


def solution(mesh):
    spec = P("wide", "narrow", None)
    return jax.shard_map(
        per_device, mesh=mesh, in_specs=(spec, spec, spec), out_specs=spec, check_vma=False
    )
```

time: 475 us -> 165 us (0.35)
  starting transfers between devices: 260 us -> 55.8 us
  blocking collectives: 90.2 us -> 9.36 us
  local copies, waits for them, and re-layouts: 74.6 us -> 25.2 us
  Pallas kernels: 0 us -> 48.3 us
  other arithmetic: 33.6 us -> 4.28 us
  waiting for transfers between devices: 9.22 us -> 19.6 us
    ppermute x88 -> x10, starting transfers between devices: 260 us -> 35 us  [shifted(): lax.ppermute(value, axis, [(i, i + by) for i in range(size) if 0 <= i + b...]
    psum x4 -> x0, blocking collectives: 90.2 us -> none  [by_axis(): return functools.reduce(lax.psum, axes, shard)]
    pallas_call x0 -> x4, Pallas kernels: none -> 48.3 us  [call(): pl.pallas_call(kernel, out_shape=[jax.ShapeDtypeStruct(s, f32) for s in o...]
    reshape x9 -> x0, local copies, waits for them, and re-layouts: 47.1 us -> none  [the longest x3 40.9 us: coarsen(): values.reshape(count, size_x // 2, 2, size_y // 2, 2, size_z // 2, 2)]
    unnamed x32 -> x64, local copies, waits for them, and re-layouts: 0.71 us -> 24.5 us
    reduce_sum x11 -> x1, other arithmetic: 23.3 us -> 0.99 us  [per_device(): totals = jnp.sum(every, axis=(0, 1))]
    all_to_all x0 -> x1, starting transfers between devices: none -> 20.8 us  [per_device(): every = lax.all_to_all(sums, 'wide', 0, 0)]
    another operation x1 -> x0, local copies, waits for them, and re-layouts: 18.9 us -> none  [coarsen(): values.reshape(count, size_x // 2, 2, size_y // 2, 2, size_z // 2, 2)]
  transfers between devices with their start and end apart: 88 -> 11, of which waited for: 14 -> 8; matrix products, arithmetic and copies ran while one was open for 19% -> 0% of each run, Pallas kernels for 0% -> 4%
where the time goes in v1:
time: 165 us; the launch traced here: 164 us
  starting transfers between devices  55.8 us (34%)
  Pallas kernels  48.3 us (29%)
  local copies, waits for them, and re-layouts  25.2 us (15%)
  waiting for transfers between devices  19.6 us (12%)
  blocking collectives  9.36 us (6%)
  other arithmetic  4.28 us (3%)
    pallas_call x4, Pallas kernels, call(): pl.pallas_call(kernel, out_shape=[jax.ShapeDtypeStruct(s, f32) for s in o...  48.3 us
    ppermute x10, starting transfers between devices, shifted(): lax.ppermute(value, axis, [(i, i + by) for i in range(size) if 0 <= i + b...  35 us
    unnamed x64, local copies, waits for them, and re-layouts  24.5 us
    all_to_all x1, starting transfers between devices, per_device(): every = lax.all_to_all(sums, 'wide', 0, 0)  20.8 us
    ppermute x10, waiting for transfers between devices, shifted(): lax.ppermute(value, axis, [(i, i + by) for i in range(size) if 0 <= i + b...  19.6 us
    all_to_all x1, blocking collectives, per_device(): gathered = lax.all_to_all(chunk, 'narrow', 0, 0)  9.36 us
  transfers between devices with their start and end apart: 11, of which 8 were waited for; matrix products, arithmetic and copies ran while one was open for 0% of the time, Pallas kernels for 4%

profile of v1, /device:TPU:1, one launch (start us, length us, event | category | flops | bytes accessed | tf_op | source)
XLA Modules:
  0.0 163.9 jit_solution(13767515131080871503)
XLA Ops:
  0.0 1.3 pad_maximum_fusion.3
  1.4 4.0 %collective-permute-start = (f32[3,16,4,256]{3,2,1,0:T(4,128)S(1)}, f32[3,16,4,256]{3,2,1,0:T(4,128)S(1)}, u32[]{:S(2)}, u32[]{:S(2)}) collective-permute-start(f32[3,16,4,256]{3,2,1,0:T(4,128)S(1)} %get-tuple-element.61), channel_id=1, source_target_pairs={{0,1},{1,2},{2,3},{4,5},{5,6},{6,7},{8,9},{9,10},{10,11},{12,13},{... | collective-permute-start | bytes 589832 | tf_op jit(solution)/shard_map/ppermute | solution.py:505
  5.3 1.3 collective-permute-start.1
  6.6 1.3 collective-permute-done
  7.9 3.8 %collective-permute-done.1 = f32[3,16,4,256]{3,2,1,0:T(4,128)S(1)} collective-permute-done((f32[3,16,4,256]{3,2,1,0:T(4,128)S(1)}, f32[3,16,4,256]{3,2,1,0:T(4,128)S(1)}, u32[]{:S(2)}, u32[]{:S(2)}) %collective-permute-start.1) | collective-permute-done | bytes 196640 | tf_op jit(solution)/shard_map/ppermute | solution.py:505
  12.0 7.3 %collective-permute-start.3 = (f32[3,4,24,256]{3,2,1,0:T(8,128)S(1)}, f32[3,4,24,256]{3,2,1,0:T(8,128)S(1)}, u32[]{:S(2)}, u32[]{:S(2)}) collective-permute-start(f32[3,4,24,256]{3,2,1,0:T(8,128)S(1)} %get-tuple-element.59), channel_id=1, source_target_pairs={{4,0},{8,4},{12,8},{16,12},{20,16},{24,20},{28,24},{32,28},{36,32}... | collective-permute-start | bytes 884744 | tf_op jit(solution)/shard_map/ppermute | solution.py:505
  19.3 1.9 %collective-permute-start.2 = (f32[3,4,24,256]{3,2,1,0:T(8,128)S(1)}, f32[3,4,24,256]{3,2,1,0:T(8,128)S(1)}, u32[]{:S(2)}, u32[]{:S(2)}) collective-permute-start(f32[3,4,24,256]{3,2,1,0:T(8,128)S(1)} %get-tuple-element.60), channel_id=1, source_target_pairs={{0,4},{4,8},{8,12},{12,16},{16,20},{20,24},{24,28},{28,32},{32,36}... | collective-permute-start | bytes 884744 | tf_op jit(solution)/shard_map/ppermute | solution.py:505
  21.2 1.4 collective-permute-done.3.xhi
  22.6 2.2 %collective-permute-done.2.xlo = f32[3,4,24,256]{3,2,1,0:T(8,128)S(1)} collective-permute-done((f32[3,4,24,256]{3,2,1,0:T(8,128)S(1)}, f32[3,4,24,256]{3,2,1,0:T(8,128)S(1)}, u32[]{:S(2)}, u32[]{:S(2)}) %collective-permute-start.2) | collective-permute-done | bytes 294944 | tf_op jit(solution)/shard_map/ppermute | solution.py:505
  24.8 8.0 %down0.1 = (f32[4,25,8,128]{3,2,1,0:T(8,128)S(1)}, f32[24,24,256]{2,1,0:T(8,128)S(1)}, f32[24,24,256]{2,1,0:T(8,128)S(1)}, f32[24,24,256]{2,1,0:T(8,128)S(1)}, f...) custom-call(f32[3,16,24,256]{3,2,1,0:T(8,128)S(1)} %pad_maximum_fusi, ...), custom_call_target="tpu_custom_call" | custom-call | tf_op jit(solution)/shard_map/down0/pallas_call | solution.py:492
  34.5 9.4 %all_to_all.10.own = f32[4,25,8,128]{3,2,1,0:T(8,128)S(1)} all-to-all(f32[4,25,8,128]{3,2,1,0:T(8,128)S(1)} %get-tuple-element.32), channel_id=1, replica_groups=mesh['wide'=128,'narrow'=4] {'narrow'}, dimensions={0} | all-to-all | bytes 819200 | tf_op jit(solution)/shard_map/all_to_all | solution.py:523
  43.9 1.9 %collective-permute-start.5 = (f32[4,25,8,128]{3,2,1,0:T(8,128)S(1)}, f32[4,25,8,128]{3,2,1,0:T(8,128)S(1)}, u32[]{:S(2)}, u32[]{:S(2)}) collective-permute-start(f32[4,25,8,128]{3,2,1,0:T(8,128)S(1)} %all_to_all.10.own), channel_id=1, source_target_pairs={{4,0},{8,4},{12,8},{16,12},{20,16},{24,20},{28,24},{32,28},{36,32}... | collective-permute-start | bytes 1228808 | tf_op jit(solution)/shard_map/ppermute | solution.py:505
  45.8 5.7 %collective-permute-start.4 = (f32[4,25,8,128]{3,2,1,0:T(8,128)S(1)}, f32[4,25,8,128]{3,2,1,0:T(8,128)S(1)}, u32[]{:S(2)}, u32[]{:S(2)}) collective-permute-start(f32[4,25,8,128]{3,2,1,0:T(8,128)S(1)} %all_to_all.10.own), channel_id=1, source_target_pairs={{0,4},{4,8},{8,12},{12,16},{16,20},{20,24},{24,28},{28,32},{32,36}... | collective-permute-start | bytes 1228808 | tf_op jit(solution)/shard_map/ppermute | solution.py:505
  51.5 3.7 %collective-permute-done.5.hi = f32[4,25,8,128]{3,2,1,0:T(8,128)S(1)} collective-permute-done((f32[4,25,8,128]{3,2,1,0:T(8,128)S(1)}, f32[4,25,8,128]{3,2,1,0:T(8,128)S(1)}, u32[]{:S(2)}, u32[]{:S(2)}) %collective-permute-start.5) | collective-permute-done | bytes 409632 | tf_op jit(solution)/shard_map/ppermute | solution.py:505
  55.2 1.2 collective-permute-done.4.lo
  56.4 8.9 %down1.1 = (f32[14,16,128]{2,1,0:T(8,128)S(1)}, f32[14,16,128]{2,1,0:T(8,128)S(1)}, f32[24,16,128]{2,1,0:T(8,128)S(1)}, f32[8,128]{1,0:T(8,128)S(1)}, f32[28,32,...) custom-call(f32[4,25,8,128]{3,2,1,0:T(8,128)S(1)} %collective-permut, ...), custom_call_target="tpu_custom_call" | custom-call | tf_op jit(solution)/shard_map/down1/pallas_call | solution.py:492
  72.3 3.5 %collective-permute-start.7 = (f32[14,16,128]{2,1,0:T(8,128)S(1)}, f32[14,16,128]{2,1,0:T(8,128)S(1)}, u32[]{:S(2)}, u32[]{:S(2)}) collective-permute-start(f32[14,16,128]{2,1,0:T(8,128)S(1)} %get-tuple-element.33), channel_id=1, source_target_pairs={{0,8},{4,12},{8,16},{12,20},{16,24},{20,28},{24,32},{28,36},{32,40... | collective-permute-start | bytes 344072 | tf_op jit(solution)/shard_map/ppermute | solution.py:505
  75.9 6.8 %collective-permute-start.6 = (f32[14,16,128]{2,1,0:T(8,128)S(1)}, f32[14,16,128]{2,1,0:T(8,128)S(1)}, u32[]{:S(2)}, u32[]{:S(2)}) collective-permute-start(f32[14,16,128]{2,1,0:T(8,128)S(1)} %get-tuple-element.33), channel_id=1, source_target_pairs={{0,16},{4,20},{8,24},{12,28},{16,32},{20,36},{24,40},{28,44},{32,4... | collective-permute-start | bytes 344072 | tf_op jit(solution)/shard_map/ppermute | solution.py:505
  82.7 1.3 collective-permute-start.9
  84.0 1.3 collective-permute-start.8
  85.3 3.9 %collective-permute-done.9.up4 = f32[14,16,128]{2,1,0:T(8,128)S(1)} collective-permute-done((f32[14,16,128]{2,1,0:T(8,128)S(1)}, f32[14,16,128]{2,1,0:T(8,128)S(1)}, u32[]{:S(2)}, u32[]{:S(2)}) %collective-permute-start.9) | collective-permute-done | bytes 114720 | tf_op jit(solution)/shard_map/ppermute | solution.py:505
  89.2 2.0 %collective-permute-done.8.up2 = f32[14,16,128]{2,1,0:T(8,128)S(1)} collective-permute-done((f32[14,16,128]{2,1,0:T(8,128)S(1)}, f32[14,16,128]{2,1,0:T(8,128)S(1)}, u32[]{:S(2)}, u32[]{:S(2)}) %collective-permute-start.8) | collective-permute-done | bytes 114720 | tf_op jit(solution)/shard_map/ppermute | solution.py:505
  91.3 24.2 %bottom.1 = (f32[8,16,128]{2,1,0:T(8,128)S(1)}, f32[128,1,128]{2,1,0:T(1,128)S(1)}) custom-call(f32[14,16,128]{2,1,0:T(8,128)S(1)} %collective-permute-done.6.dn4, f32[14,16,128]{2,1,0:T(8,128)S(1)} %collective-permute-done.7.dn2, f32[24,16,128]{2,1,0:T(8,128)S(1)} %get-tuple-element.34.mine, f32[14,16,128]{2,1,0:T(8,128)S(1)} %collective-permute-done.8.up2, ...), custom_call_target="tpu_custom_call" | custom-call | tf_op jit(solution)/shard_map/bottom/pallas_call | solution.py:492
  116.8 20.8 %all-to-all-start.1 = ((f32[128,1,128]{2,1,0:T(1,128)}), f32[128,1,128]{2,1,0:T(1,128)}, u32[]{:S(2)}, u32[]{:S(2)}) async-start(f32[128,1,128]{2,1,0:T(1,128)} %copy-done.28), calls=%async_computation.1 | async-start | bytes 131072 | tf_op jit(solution)/shard_map/all_to_all | solution.py:549
  137.6 1.1 copy-done.1
  138.6 1.1 copy-done.3
  139.7 1.1 copy-done.5
  140.7 1.0 copy-done.7
  141.8 1.0 copy-done.9
  142.8 1.0 copy-done.11
  150.7 7.2 %up.1 = (f32[16,16,256]{2,1,0:T(8,128)S(1)}, f32[16,16,256]{2,1,0:T(8,128)S(1)}) custom-call(f32[8,16,128]{2,1,0:T(8,128)S(1)} %copy-done.27, f32[28,32,128]{2,1,0:T(8,128)S(1)} %copy-done.7, f32[28,32,128]{2,1,0:T(8,128)S(1)} %copy-done.9, f32[28,32,128]{2,1,0:T(8,128)S(1)} %copy-done.11, f32[28,32,128]{2,1,0:T(8,128)S(1)} %copy-done.13, ...), custom_call_target="tpu_custom_call" | custom-call | tf_op jit(solution)/shard_map/up/pallas_call | solution.py:492
  162.1 1.8 %multiply_subtract_fusion = f32[16,16,256]{2,1,0:T(8,128)} fusion(f32[16,16,256]{2,1,0:T(8,128)} %copy-done.25, f32[16,16,256]{2,1,0:T(8,128)} %copy-done.24, f32[]{:T(128)} %bitcast.3), kind=kLoop, calls=%fused_computation.1 | loop fusion | flops 131072 | bytes 786436 | tf_op jit(solution)/shard_map/sub | solution.py:559
  (65 shorter events, 20.1 us)
Async XLA Ops:
  0.0 11.7 %copy-start.29 = (f32[16,16,256]{2,1,0:T(8,128)S(1)}, f32[16,16,256]{2,1,0:T(8,128)}, u32[]{:S(2)}) copy-start(f32[16,16,256]{2,1,0:T(8,128)} %param.5) | copy-start | bytes 786436
  0.0 11.7 %copy-start.30 = (f32[16,16,256]{2,1,0:T(8,128)S(1)}, f32[16,16,256]{2,1,0:T(8,128)}, u32[]{:S(2)}) copy-start(f32[16,16,256]{2,1,0:T(8,128)} %param.4) | copy-start | bytes 786436
  0.0 11.7 %copy-start.31 = (f32[16,16,256]{2,1,0:T(8,128)S(1)}, f32[16,16,256]{2,1,0:T(8,128)}, u32[]{:S(2)}) copy-start(f32[16,16,256]{2,1,0:T(8,128)} %param.3) | copy-start | bytes 786436
  1.4 6.5 %collective-permute-start = (f32[3,16,4,256]{3,2,1,0:T(4,128)S(1)}, f32[3,16,4,256]{3,2,1,0:T(4,128)S(1)}, u32[]{:S(2)}, u32[]{:S(2)}) collective-permute-start(f32[3,16,4,256]{3,2,1,0:T(4,128)S(1)} %get-tuple-element.61), channel_id=1, source_target_pairs={{0,1},{1,2},{2,3},{4,5},{5,6},{6,7},{8,9},{9,10},{10,11},{12,13},{... | collective-permute-start | bytes 589832 | tf_op jit(solution)/shard_map/ppermute | solution.py:505
  5.3 6.4 %collective-permute-start.1 = (f32[3,16,4,256]{3,2,1,0:T(4,128)S(1)}, f32[3,16,4,256]{3,2,1,0:T(4,128)S(1)}, u32[]{:S(2)}, u32[]{:S(2)}) collective-permute-start(f32[3,16,4,256]{3,2,1,0:T(4,128)S(1)} %get-tuple-element.62), channel_id=1, source_target_pairs={{1,0},{2,1},{3,2},{5,4},{6,5},{7,6},{9,8},{10,9},{11,10},{13,12},{... | collective-permute-start | bytes 589832 | tf_op jit(solution)/shard_map/ppermute | solution.py:505
  12.0 10.6 %collective-permute-start.3 = (f32[3,4,24,256]{3,2,1,0:T(8,128)S(1)}, f32[3,4,24,256]{3,2,1,0:T(8,128)S(1)}, u32[]{:S(2)}, u32[]{:S(2)}) collective-permute-start(f32[3,4,24,256]{3,2,1,0:T(8,128)S(1)} %get-tuple-element.59), channel_id=1, source_target_pairs={{4,0},{8,4},{12,8},{16,12},{20,16},{24,20},{28,24},{32,28},{36,32}... | collective-permute-start | bytes 884744 | tf_op jit(solution)/shard_map/ppermute | solution.py:505
  19.3 5.6 %collective-permute-start.2 = (f32[3,4,24,256]{3,2,1,0:T(8,128)S(1)}, f32[3,4,24,256]{3,2,1,0:T(8,128)S(1)}, u32[]{:S(2)}, u32[]{:S(2)}) collective-permute-start(f32[3,4,24,256]{3,2,1,0:T(8,128)S(1)} %get-tuple-element.60), channel_id=1, source_target_pairs={{0,4},{4,8},{8,12},{12,16},{16,20},{20,24},{24,28},{28,32},{32,36}... | collective-permute-start | bytes 884744 | tf_op jit(solution)/shard_map/ppermute | solution.py:505
  32.8 0.8 copy-start.2
  33.7 0.8 copy-start.4
  34.5 20.7 %copy-start = (f32[24,24,256]{2,1,0:T(8,128)}, f32[24,24,256]{2,1,0:T(8,128)S(1)}, u32[]{:S(2)}) copy-start(f32[24,24,256]{2,1,0:T(8,128)S(1)} %get-tuple-element.53.wt0) | copy-start | bytes 1769476
  43.9 11.3 %collective-permute-start.5 = (f32[4,25,8,128]{3,2,1,0:T(8,128)S(1)}, f32[4,25,8,128]{3,2,1,0:T(8,128)S(1)}, u32[]{:S(2)}, u32[]{:S(2)}) collective-permute-start(f32[4,25,8,128]{3,2,1,0:T(8,128)S(1)} %all_to_all.10.own), channel_id=1, source_target_pairs={{4,0},{8,4},{12,8},{16,12},{20,16},{24,20},{28,24},{32,28},{36,32}... | collective-permute-start | bytes 1228808 | tf_op jit(solution)/shard_map/ppermute | solution.py:505
  45.8 10.6 %collective-permute-start.4 = (f32[4,25,8,128]{3,2,1,0:T(8,128)S(1)}, f32[4,25,8,128]{3,2,1,0:T(8,128)S(1)}, u32[]{:S(2)}, u32[]{:S(2)}) collective-permute-start(f32[4,25,8,128]{3,2,1,0:T(8,128)S(1)} %all_to_all.10.own), channel_id=1, source_target_pairs={{0,4},{4,8},{8,12},{12,16},{16,20},{20,24},{24,28},{28,32},{32,36}... | collective-permute-start | bytes 1228808 | tf_op jit(solution)/shard_map/ppermute | solution.py:505
  68.4 0.8 copy-start.14
  71.5 0.8 copy-start.22
  72.3 13.0 %collective-permute-start.7 = (f32[14,16,128]{2,1,0:T(8,128)S(1)}, f32[14,16,128]{2,1,0:T(8,128)S(1)}, u32[]{:S(2)}, u32[]{:S(2)}) collective-permute-start(f32[14,16,128]{2,1,0:T(8,128)S(1)} %get-tuple-element.33), channel_id=1, source_target_pairs={{0,8},{4,12},{8,16},{12,20},{16,24},{20,28},{24,32},{28,36},{32,40... | collective-permute-start | bytes 344072 | tf_op jit(solution)/shard_map/ppermute | solution.py:505
  75.9 9.4 %collective-permute-start.6 = (f32[14,16,128]{2,1,0:T(8,128)S(1)}, f32[14,16,128]{2,1,0:T(8,128)S(1)}, u32[]{:S(2)}, u32[]{:S(2)}) collective-permute-start(f32[14,16,128]{2,1,0:T(8,128)S(1)} %get-tuple-element.33), channel_id=1, source_target_pairs={{0,16},{4,20},{8,24},{12,28},{16,32},{20,36},{24,40},{28,44},{32,4... | collective-permute-start | bytes 344072 | tf_op jit(solution)/shard_map/ppermute | solution.py:505
  82.7 6.5 %collective-permute-start.9 = (f32[14,16,128]{2,1,0:T(8,128)S(1)}, f32[14,16,128]{2,1,0:T(8,128)S(1)}, u32[]{:S(2)}, u32[]{:S(2)}) collective-permute-start(f32[14,16,128]{2,1,0:T(8,128)S(1)} %get-tuple-element.35), channel_id=1, source_target_pairs={{16,0},{20,4},{24,8},{28,12},{32,16},{36,20},{40,24},{44,28},{48,3... | collective-permute-start | bytes 344072 | tf_op jit(solution)/shard_map/ppermute | solution.py:505
  84.0 7.3 %collective-permute-start.8 = (f32[14,16,128]{2,1,0:T(8,128)S(1)}, f32[14,16,128]{2,1,0:T(8,128)S(1)}, u32[]{:S(2)}, u32[]{:S(2)}) collective-permute-start(f32[14,16,128]{2,1,0:T(8,128)S(1)} %get-tuple-element.35), channel_id=1, source_target_pairs={{8,0},{12,4},{16,8},{20,12},{24,16},{28,20},{32,24},{36,28},{40,32... | collective-permute-start | bytes 344072 | tf_op jit(solution)/shard_map/ppermute | solution.py:505
  116.8 42.6 %all-to-all-start.1 = ((f32[128,1,128]{2,1,0:T(1,128)}), f32[128,1,128]{2,1,0:T(1,128)}, u32[]{:S(2)}, u32[]{:S(2)}) async-start(f32[128,1,128]{2,1,0:T(1,128)} %copy-done.28), calls=%async_computation.1 | async-start | bytes 131072 | tf_op jit(solution)/shard_map/all_to_all | solution.py:549
  137.5 1.1 copy-start.1
  138.6 1.1 copy-start.3
  139.7 1.1 copy-start.5
  140.7 1.0 copy-start.7
  141.8 1.0 copy-start.9
  142.8 1.0 copy-start.11
  143.8 1.0 copy-start.13
  144.8 1.0 copy-start.15
  145.8 1.0 copy-start.17
  146.8 1.0 copy-start.19
  147.9 1.0 copy-start.21
  148.9 1.0 copy-start.23
  149.9 0.8 copy-start.27
  (11 other events, 8.1 us)

commit v2 on v0

v2 whole, which is shorter than its diff:
```python
import functools

import jax
import jax.numpy as jnp
from jax import lax
from jax.experimental import pallas as pl
from jax.experimental.pallas import tpu as pltpu
from jax.sharding import PartitionSpec as P

f32 = jnp.float32
HALO = 4
LIMIT = 24
DAMPING = 0.8
BASE_TAU = 16.0
VMEM = pl.BlockSpec(memory_space=pltpu.VMEM)
HBM = pl.BlockSpec(memory_space=pltpu.HBM)


def half_tau(level):
    return 0.5 * BASE_TAU / 4.0**level


def iota(shape, dim):
    return lax.broadcasted_iota(jnp.int32, shape, dim)


def dot(a, b):
    return jnp.dot(a, b, precision=lax.Precision.HIGHEST, preferred_element_type=f32)


def rounded(x):
    return x.astype(jnp.bfloat16).astype(f32)


def ahead(x, axis):
    return pltpu.roll(x, x.shape[axis] - 1, axis)


def behind(x, axis):
    return pltpu.roll(x, 1, axis)


def at(i, n):
    return pl.ds(i, n) if n > 1 or not isinstance(i, int) else slice(i, i + 1)


def by_rows(lo, hi, n, fn, carry=None):
    count = (hi - lo) // n
    if count > 1:
        carry = lax.fori_loop(0, count, lambda t, c: fn(lo + t * n, n, c), carry)
    elif count == 1:
        carry = fn(lo, n, carry)
    rest = hi - lo - count * n
    if rest:
        carry = fn(lo + count * n, rest, carry)
    return carry


def coefficients(level, m, cx, cy, cz, dg, wt, lo, hi, n, y_len, z_len):
    tau = half_tau(level)
    cx[lo - 1] = rounded(tau * (m[lo - 1] + m[lo]))

    def body(i, n, carry):
        here = m[at(i, n)]
        shape = here.shape
        lane = lax.rem(iota(shape, 2), z_len)
        z_last = lane == z_len - 1
        z_first = lane == 0
        edge = rounded(tau * here)
        x_up = rounded(tau * (here + m[at(i + 1, n)]))
        cx[at(i, n)] = x_up
        y_up = rounded(tau * (here + ahead(here, 1)))
        if y_len is None:
            y_down = behind(y_up, 1)
            cy[at(i, n)] = y_up
        else:
            sub = iota(shape, 1)
            inner = jnp.where(sub >= y_len - 1, 0.0, y_up)
            y_up = jnp.where(sub == y_len - 1, edge, y_up)
            y_down = jnp.where(sub == 0, edge, behind(inner, 1))
            cy[at(i, n)] = inner
        inner = jnp.where(z_last, 0.0, rounded(tau * (here + ahead(here, 2))))
        cz[at(i, n)] = inner
        z_up = jnp.where(z_last, edge, inner)
        z_down = jnp.where(z_first, edge, behind(inner, 2))
        diagonal = 1.0 + x_up + cx[at(i - 1, n)] + y_up + y_down + z_up + z_down
        if dg is not None:
            dg[at(i, n)] = diagonal
        wt[at(i, n)] = jnp.where(here > 0.0, DAMPING / diagonal, 0.0)
        return carry

    by_rows(lo, hi, n, body, 0)


def coupled(i, n, v, cx, cy, cz):
    here = v[at(i, n)]
    up = cy[at(i, n)]
    side = cz[at(i, n)]
    total = cx[at(i, n)] * v[at(i + 1, n)] + cx[at(i - 1, n)] * v[at(i - 1, n)]
    total = total + (up * ahead(here, 1) + behind(up * here, 1))
    return total + (side * ahead(here, 2) + behind(side * here, 2))


def residual(i, n, r, v, cx, cy, cz, dg):
    return r - dg[at(i, n)] * v[at(i, n)] + coupled(i, n, v, cx, cy, cz)


def relaxed(i, n, r, v, wt, cx, cy, cz, *_):
    return (1.0 - DAMPING) * v[at(i, n)] + wt[at(i, n)] * (r[at(i, n)] + coupled(i, n, v, cx, cy, cz))


def start(lo, hi, n, source, out, wt):
    def body(i, n, carry):
        for s, o in zip(source, out):
            o[at(i, n)] = wt[at(i, n)] * s[at(i, n)]
        return carry

    by_rows(lo, hi, n, body, 0)


def sweep(lo, hi, n, source, v, out, coefs, wt):
    def body(i, n, carry):
        for s, a, o in zip(source, v, out):
            o[at(i, n)] = relaxed(i, n, s, a, wt, *coefs)
        return carry

    by_rows(lo, hi, n, body, 0)


def pairs(x):
    x = x.reshape(x.shape[0] // 2, 2, *x.shape[1:])
    return x[:, 0] + x[:, 1]


def doubled(x):
    x = jnp.broadcast_to(x[:, None], (x.shape[0], 2, *x.shape[1:]))
    return x.reshape(x.shape[0] * 2, *x.shape[2:])


def flat_dot(x, matrix):
    n = x.shape[0] * x.shape[1]
    return dot(x.reshape(n, x.shape[2]), matrix).reshape(x.shape[0], x.shape[1], matrix.shape[1])


def fold_y(ref, k, n, first, count):
    return ref[k : k + n, pl.ds(first, count, stride=2), :] + ref[k : k + n, pl.ds(first + 1, count, stride=2), :]


def coarse_z(z_in, lanes_in, z_out, lanes_out, fields):
    src = iota((lanes_in, lanes_out), 0)
    dst = iota((lanes_in, lanes_out), 1)
    target = lax.div(src, z_in) * z_out + lax.div(lax.rem(src, z_in), 2)
    return jnp.where((target == dst) & (src < fields * z_in), 0.125, 0.0).astype(f32)


def fine_z(z_in, lanes_in, z_out, lanes_out, fields):
    src = iota((lanes_in, lanes_out), 0)
    dst = iota((lanes_in, lanes_out), 1)
    wanted = lax.div(dst, z_out) * z_in + lax.div(lax.rem(dst, z_out), 2)
    return jnp.where((wanted == src) & (dst < fields * z_out), 1.0, 0.0).astype(f32)


def products(i, n, s, c, us, uc, coefs, sums):
    num, den = sums
    v_s, v_c = us[at(i, n)], uc[at(i, n)]
    r_s, r_c = s[at(i, n)], c[at(i, n)]
    res_s = residual(i, n, r_s, us, *coefs)
    res_c = residual(i, n, r_c, uc, *coefs)
    num = num + jnp.sum(v_s * r_c + res_s * v_c, axis=0)
    den = den + jnp.sum(v_s * r_s + res_s * v_s, axis=0)
    return res_s, res_c, (num, den)


def fetch(sources, targets, sems):
    copies = [pltpu.make_async_copy(a, b, sems.at[k]) for k, (a, b) in enumerate(zip(sources, targets))]
    for copy in copies:
        copy.start()
    return copies


def wait(copies):
    for copy in copies:
        copy.wait()


def fetch0(own, xlo, xhi, fields, sems):
    sources, targets = [], []
    for index, ref in enumerate(fields):
        for part, lo, hi in ((xlo, 0, 4), (own, 4, 20), (xhi, 20, 24)):
            sources.append(part.at[index])
            targets.append(ref.at[pl.ds(lo, hi - lo)])
    return fetch(sources, targets, sems)


def fetch1(lo, own, hi, fields, sems):
    sources, targets = [], []
    for index, ref in fields:
        for part, source in enumerate((lo, own, hi)):
            for j in range(4):
                sources.append(source.at[j, pl.ds(index * 8, 8)])
                targets.append(ref.at[pl.ds(2 + part * 8, 8), pl.ds(8 * j, 8), :])
    return fetch(sources, targets, sems)


def down0(own, xlo, xhi, out, vs, vc, cx, cy, cz, dg, wt, ss, cc, m, us, uc, pair, thin, sems):
    copies = fetch0(own, xlo, xhi, (m, ss, cc), sems)
    wait(copies[:3])
    coefficients(0, m, cx, cy, cz, dg, wt, 1, 23, 2, None, 256)
    coefs = (cx, cy, cz, dg)
    wait(copies[3:])
    start(1, 23, 2, (ss, cc), (us, uc), wt)
    sweep(2, 22, 2, (ss, cc), (us, uc), (vs, vc), coefs, wt)

    def rest(i, n, sums):
        res_s, res_c, sums = products(i, n, ss, cc, vs, vc, coefs, sums)
        k = lax.div(i - 4, 2)
        pair[at(k, n // 2)] = pairs(res_s)
        pair[at(k + 8, n // 2)] = pairs(res_c)
        pair[at(k + 16, n // 2)] = pairs(m[at(i, n)])
        return sums

    zero = jnp.zeros((24, 256), f32)
    num, den = by_rows(4, 20, 2, rest, (zero, zero))
    thin[...] = flat_dot(pair[...], coarse_z(256, 256, 128, 128, 1))
    value = fold_y(thin, 0, 24, 4, 8)
    sub = iota((24, 256), 0)
    inside = (sub >= 4) & (sub < 20)
    num = jnp.sum(jnp.where(inside, num, 0.0))
    den = jnp.sum(jnp.where(inside, den, 0.0))
    lane = iota((8, 128), 1)
    both = jnp.where(lane == 0, num, jnp.where(lane == 1, den, 0.0))
    for j in range(4):
        out[j, 0:24] = value
        out[j, 24] = both


def down1(
    lo, own, hi, to_up, to_down, mine, sums,
    vs, vc, cx, cy, cz, dg, wt, ss, cc, m, us, uc, pair, thin, inner, sems,
):
    copies = fetch1(lo, own, hi, ((2, m), (0, ss), (1, cc)), sems)
    partial = fetch([own.at[j, 24] for j in range(4)], [inner.at[j] for j in range(4)], sems.at[pl.ds(36, 4)])
    for ref in (ss, cc, m, vs, vc):
        ref[0:2] = jnp.zeros((2, 32, 128), f32)
        ref[26:28] = jnp.zeros((2, 32, 128), f32)
    wait(copies[:12])
    coefficients(1, m, cx, cy, cz, dg, wt, 1, 27, 2, 32, 128)
    coefs = (cx, cy, cz, dg)
    wait(copies[12:])
    wait(partial)
    start(1, 27, 2, (ss, cc), (us, uc), wt)
    sweep(2, 26, 4, (ss, cc), (us, uc), (vs, vc), coefs, wt)

    def rest(i, n, sums):
        res_s, res_c, sums = products(i, n, ss, cc, vs, vc, coefs, sums)
        k = lax.div(i - 2, 2)
        pair[at(k, n // 2), :, 0:128] = pairs(res_s)
        pair[at(k, n // 2), :, 128:256] = pairs(res_c)
        both = pairs(m[at(i, n)])
        pair[at(k + 12, n // 2), :, 0:128] = both
        pair[at(k + 12, n // 2), :, 128:256] = both
        return sums

    zero = jnp.zeros((32, 128), f32)
    by_rows(2, 10, 4, rest, (zero, zero))
    num, den = by_rows(10, 18, 4, rest, (zero, zero))
    by_rows(18, 26, 4, rest, (zero, zero))
    thin[...] = flat_dot(pair[...], coarse_z(128, 256, 64, 128, 2))
    place = lax.axis_index("wide")
    low = jnp.where(place == 1, fold_y(thin, 0, 2, 0, 16), 0.0)
    mid = fold_y(thin, 2, 8, 0, 16)
    high = jnp.where(place == lax.axis_size("wide") - 2, fold_y(thin, 10, 2, 0, 16), 0.0)
    mob = fold_y(thin, 12, 12, 0, 16)
    mine[0:2] = low
    mine[2:10] = mid
    mine[10:12] = high
    mine[12:24] = mob
    to_up[0:2] = low
    to_up[2:10] = mid
    to_down[0:8] = mid
    to_down[8:10] = high
    left = iota((4, 16, 128), 2) < 64
    to_up[10:14] = jnp.where(left, mob[0:4], mob[4:8])
    to_down[10:14] = jnp.where(left, mob[4:8], mob[8:12])
    lane = iota((8, 128), 1)
    num = jnp.sum(num) * 8.0
    den = jnp.sum(den) * 8.0
    finer = inner[0] + inner[1] + inner[2] + inner[3]
    sums[...] = finer + jnp.where(lane == 0, num, jnp.where(lane == 1, den, 0.0))


def bottom(
    dn4, dn2, mine, up2, up4, finer, e2, sums,
    m2, r2, u2, v2, cx2, cy2, cz2, dg2, wt2,
    m3, r3, u3, v3, cx3, cy3, cz3, dg3, wt3,
    m4, r4, u4, v4, cx4, cy4, cz4, dg4, wt4,
    pair2, thin2, pair3, thin3, wide3, wide2,
):
    left = iota((4, 16, 128), 2) < 64

    def unpack(ref, first, r_at, m_at):
        r2[r_at : r_at + 8] = ref[first : first + 8]
        packed = ref[10:14]
        other = pltpu.roll(packed, 64, 2)
        m2[m_at : m_at + 4] = jnp.where(left, packed, other)
        m2[m_at + 4 : m_at + 8] = jnp.where(left, other, packed)

    unpack(dn4, 2, 2, 0)
    unpack(dn2, 2, 10, 8)
    unpack(up2, 0, 26, 28)
    unpack(up4, 0, 34, 36)
    r2[18:26] = mine[2:10]
    m2[16:28] = mine[12:24]
    r2[8:10] = r2[8:10] + dn2[0:2]
    r2[16:18] = r2[16:18] + mine[0:2]
    r2[26:28] = r2[26:28] + mine[10:12]
    r2[34:36] = r2[34:36] + up2[8:10]

    def both_products(r, v, res, z_len):
        num = v * pltpu.roll(r, 128 - z_len, 2)
        den = v * r
        if res is not None:
            num = num + res * pltpu.roll(v, 128 - z_len, 2)
            den = den + res * v
        mask = iota(v.shape, 2) < z_len
        return jnp.sum(jnp.where(mask, num, 0.0)), jnp.sum(jnp.where(mask, den, 0.0))

    c2 = (cx2, cy2, cz2, dg2)
    c3 = (cx3, cy3, cz3, dg3)
    c4 = (cx4, cy4, cz4, dg4)
    coefficients(2, m2, *c2, wt2, 1, 43, 6, 16, 64)
    start(2, 42, 8, (r2,), (u2,), wt2)
    sweep(3, 41, 8, (r2,), (u2,), (v2,), c2, wt2)

    def rest2(i, n, sums):
        res = residual(i, n, r2[at(i, n)], v2, *c2)
        pair2[at(lax.div(i - 4, 2), n // 2)] = pairs(res)
        return sums

    by_rows(4, 40, 6, rest2, 0)
    own = slice(20, 24)
    num2, den2 = both_products(r2[own], v2[own], residual(20, 4, r2[own], v2, *c2), 64)
    pair2[18:40] = pairs(m2[...])
    thin2[...] = flat_dot(pair2[...], coarse_z(64, 128, 32, 128, 2))
    r3[2:20] = fold_y(thin2, 0, 18, 0, 8)
    m3[...] = fold_y(thin2, 18, 22, 0, 8)

    coefficients(3, m3, *c3, wt3, 1, 21, 10, 8, 32)
    start(2, 20, 18, (r3,), (u3,), wt3)
    sweep(3, 19, 16, (r3,), (u3,), (v3,), c3, wt3)
    res = residual(4, 14, r3[4:18], v3, *c3)
    num3, den3 = both_products(r3[10:12], v3[10:12], res[6:8], 32)
    pair3[0:7] = pairs(res)
    pair3[7:18] = pairs(m3[...])
    thin3[...] = flat_dot(pair3[...], coarse_z(32, 128, 16, 128, 2))
    m4[...] = jnp.zeros((11, 8, 128), f32)
    r4[...] = jnp.zeros((11, 8, 128), f32)
    r4[2:9, 0:4, :] = fold_y(thin3, 0, 7, 0, 4)
    m4[:, 0:4, :] = fold_y(thin3, 7, 11, 0, 4)

    coefficients(4, m4, *c4, wt4, 1, 10, 9, 4, 16)
    start(2, 9, 7, (r4,), (u4,), wt4)
    sweep(3, 8, 5, (r4,), (u4,), (v4,), c4, wt4)
    num4, den4 = both_products(r4[5:6], v4[5:6], None, 16)
    num = 64.0 * num2 + 512.0 * num3 + 4096.0 * num4
    den = 64.0 * den2 + 512.0 * den3 + 4096.0 * den4
    lane = iota((8, 128), 1)
    total = finer[...] + jnp.where(lane == 0, num, jnp.where(lane == 1, den, 0.0))
    sums[...] = jnp.broadcast_to(total[0:1].reshape(1, 1, 128), sums.shape)

    wide3[:, pl.ds(0, 4, stride=2), :] = v4[3:8, 0:4, :]
    wide3[:, pl.ds(1, 4, stride=2), :] = v4[3:8, 0:4, :]
    v3[6:16] = v3[6:16] + doubled(flat_dot(wide3[...], fine_z(16, 128, 32, 128, 2)))
    sweep(7, 15, 8, (r3,), (v3,), (u3,), c3, wt3)
    sweep(8, 14, 6, (r3,), (u3,), (v3,), c3, wt3)
    wide2[:, pl.ds(0, 8, stride=2), :] = v3[8:14]
    wide2[:, pl.ds(1, 8, stride=2), :] = v3[8:14]
    v2[16:28] = v2[16:28] + doubled(flat_dot(wide2[...], fine_z(32, 128, 64, 128, 2)))
    sweep(17, 27, 10, (r2,), (v2,), (u2,), c2, wt2)
    e2[...] = relaxed(18, 8, r2, u2, wt2, *c2)


def up(
    e2, lo1, own1, hi1, own0, xlo0, xhi0, out_s, out_c,
    vs1, vc1, cx1, cy1, cz1, wt1, ss1, cc1, m1, as1, ac1, bs1, bc1,
    vs0, vc0, cx0, cy0, cz0, wt0, ss0, cc0, m0, as0, ac0, bs0, bc0,
    wide, add, block, thick, full, sems,
):
    copies1 = fetch1(lo1, own1, hi1, ((2, m1), (0, ss1), (1, cc1)), sems)
    copies0 = fetch0(own0, xlo0, xhi0, (m0, ss0, cc0), sems.at[pl.ds(36, 9)])
    c1 = (cx1, cy1, cz1)
    c0 = (cx0, cy0, cz0)
    wait(copies1)
    coefficients(1, m1, cx1, cy1, cz1, None, wt1, 5, 23, 2, 32, 128)
    start(5, 23, 2, (ss1, cc1), (as1, ac1), wt1)
    sweep(6, 22, 4, (ss1, cc1), (as1, ac1), (vs1, vc1), c1, wt1)
    wait(copies0)
    coefficients(0, m0, cx0, cy0, cz0, None, wt0, 1, 23, 2, None, 256)
    start(1, 23, 2, (ss0, cc0), (as0, ac0), wt0)
    sweep(2, 22, 2, (ss0, cc0), (as0, ac0), (vs0, vc0), c0, wt0)
    wide[:, pl.ds(0, 16, stride=2), :] = e2[...]
    wide[:, pl.ds(1, 16, stride=2), :] = e2[...]
    add[...] = flat_dot(wide[...], fine_z(64, 128, 128, 256, 2))

    def correct1(i, n, carry):
        k = lax.div(i - 6, 2)
        both = add[at(k, n // 2)]
        as1[at(i, n)] = vs1[at(i, n)] + doubled(both[:, :, 0:128])
        ac1[at(i, n)] = vc1[at(i, n)] + doubled(both[:, :, 128:256])
        return carry

    by_rows(6, 22, 4, correct1, 0)
    sweep(8, 20, 4, (ss1, cc1), (as1, ac1), (bs1, bc1), c1, wt1)
    place = lax.axis_index("narrow")
    block[:, 0:8, :] = jnp.zeros((20, 8, 128), f32)
    block[:, 40:48, :] = jnp.zeros((20, 8, 128), f32)

    def last1(i, n, carry):
        for index, (r, v) in enumerate(((ss1, bs1), (cc1, bc1))):
            value = relaxed(i, n, r, v, wt1, *c1)
            block[at(index * 10 + i - 9, n), 8:40, :] = value
        return carry

    by_rows(9, 19, 5, last1, 0)
    value = block[:, pl.ds(pl.multiple_of(8 * place, 8), 24), :][:, 6:18, :]
    thick[:, pl.ds(0, 12, stride=2), :] = value
    thick[:, pl.ds(1, 12, stride=2), :] = value
    full[...] = flat_dot(thick[...], fine_z(128, 128, 256, 256, 1))

    def correct0(i, n, carry):
        k = lax.div(i - 2, 2)
        as0[at(i, n)] = vs0[at(i, n)] + doubled(full[at(k, n // 2)])
        ac0[at(i, n)] = vc0[at(i, n)] + doubled(full[at(10 + k, n // 2)])
        return carry

    by_rows(2, 22, 2, correct0, 0)
    sweep(3, 21, 2, (ss0, cc0), (as0, ac0), (bs0, bc0), c0, wt0)

    def last0(i, n, carry):
        for r, v, o in ((ss0, bs0, out_s), (cc0, bc0, out_c)):
            o[at(i - 4, n)] = relaxed(i, n, r, v, wt0, *c0)[:, 4:20, :]
        return carry

    by_rows(4, 20, 2, last0, 0)


def final(every, out_s, out_c, out):
    total = jnp.sum(every[...], axis=0)
    lane = iota((1, 128), 1)
    num = jnp.sum(jnp.where(lane == 0, total, 0.0), axis=1, keepdims=True)
    den = jnp.sum(jnp.where(lane == 1, total, 0.0), axis=1, keepdims=True)
    ratio = (num / (1.0 + den))[0, 0]
    out[...] = out_c[...] - ratio * out_s[...]


def call(kernel, ins, outs, scratch, name, sems=0, specs=None):
    scratch = [pltpu.VMEM(s, f32) for s in scratch]
    if sems:
        scratch.append(pltpu.SemaphoreType.DMA((sems,)))
    return pl.pallas_call(
        kernel,
        out_shape=[jax.ShapeDtypeStruct(s, f32) for s in outs],
        in_specs=specs or [VMEM] * len(ins),
        out_specs=[VMEM] * len(outs),
        scratch_shapes=scratch,
        compiler_params=pltpu.CompilerParams(vmem_limit_bytes=LIMIT * 2**20),
        name=name,
    )(*ins)


def shifted(value, axis, by):
    size = lax.axis_size(axis)
    return lax.ppermute(value, axis, [(i, i + by) for i in range(size) if 0 <= i + by < size])


def per_device(mobility, sav_vector, cotangent):
    own = jnp.stack([mobility, sav_vector, cotangent])
    y_lo = shifted(own[:, :, -HALO:], "narrow", 1)
    y_hi = shifted(own[:, :, :HALO], "narrow", -1)
    own = jnp.concatenate([y_lo, own, y_hi], axis=2)
    x_lo = shifted(own[:, -HALO:], "wide", 1)
    x_hi = shifted(own[:, :HALO], "wide", -1)
    a0 = (24, 24, 256)
    (chunk,) = call(
        down0,
        (own, x_lo, x_hi),
        [(4, 25, 8, 128)],
        [a0] * 13 + [(24, 24, 128)],
        "down0",
        9,
        [HBM] * 3,
    )
    gathered = lax.all_to_all(chunk, "narrow", 0, 0)
    lo = shifted(gathered, "wide", 1)
    hi = shifted(gathered, "wide", -1)
    a1 = (28, 32, 128)
    to_up, to_down, mine, finer = call(
        down1,
        (lo, gathered, hi),
        [(14, 16, 128), (14, 16, 128), (24, 16, 128), (8, 128)],
        [a1] * 12 + [(24, 32, 256), (24, 32, 128), (4, 8, 128)],
        "down1",
        40,
        [HBM] * 3,
    )
    dn2 = shifted(to_up, "wide", 2)
    up2 = shifted(to_down, "wide", -2)
    dn4 = shifted(to_up, "wide", 4)
    up4 = shifted(to_down, "wide", -4)
    wide = lax.axis_size("wide")
    e2, sums = call(
        bottom,
        (dn4, dn2, mine, up2, up4, finer),
        [(8, 16, 128), (wide, 1, 128)],
        [(44, 16, 128)] * 9
        + [(22, 8, 128)] * 9
        + [(11, 8, 128)] * 9
        + [(40, 16, 128)] * 2
        + [(18, 8, 128)] * 2
        + [(5, 8, 128), (6, 16, 128)],
        "bottom",
    )
    every = lax.all_to_all(sums, "wide", 0, 0)
    out_s, out_c = call(
        up,
        (e2, lo, gathered, hi, own, x_lo, x_hi),
        [(16, 16, 256)] * 2,
        [a1] * 13
        + [a0] * 13
        + [(8, 32, 128), (8, 32, 256), (20, 48, 128), (20, 24, 128), (20, 24, 256)],
        "up",
        45,
        [VMEM] + [HBM] * 6,
    )
    return call(final, (every, out_s, out_c), [(16, 16, 256)], [], "final")[0]


def solution(mesh):
    spec = P("wide", "narrow", None)
    return jax.shard_map(
        per_device, mesh=mesh, in_specs=(spec, spec, spec), out_specs=spec, check_vma=False
    )
```

time: 475 us -> 121 us (0.25)
  starting transfers between devices: 260 us -> 55.8 us
  blocking collectives: 90.2 us -> 9.37 us
  local copies, waits for them, and re-layouts: 74.6 us -> 1.5 us
  other arithmetic: 33.6 us -> 1.52 us
  Pallas kernels: 0 us -> 30.9 us
  waiting for transfers between devices: 9.22 us -> 21.2 us
    ppermute x88 -> x10, starting transfers between devices: 260 us -> 35 us  [shifted(): lax.ppermute(value, axis, [(i, i + by) for i in range(size) if 0 <= i + b...]
    psum x4 -> x0, blocking collectives: 90.2 us -> none  [by_axis(): return functools.reduce(lax.psum, axes, shard)]
    reshape x9 -> x0, local copies, waits for them, and re-layouts: 47.1 us -> none  [the longest x3 40.9 us: coarsen(): values.reshape(count, size_x // 2, 2, size_y // 2, 2, size_z // 2, 2)]
    pallas_call x0 -> x5, Pallas kernels: none -> 30.9 us  [call(): pl.pallas_call(kernel, out_shape=[jax.ShapeDtypeStruct(s, f32) for s in o...]
    reduce_sum x11 -> x0, other arithmetic: 23.3 us -> none  [the longest x10 22.5 us: coarsen(): return blocks.mean(axis=(2, 4, 6))]
    all_to_all x0 -> x1, starting transfers between devices: none -> 20.8 us  [per_device(): every = lax.all_to_all(sums, 'wide', 0, 0)]
    another operation x1 -> x0, local copies, waits for them, and re-layouts: 18.9 us -> none  [coarsen(): values.reshape(count, size_x // 2, 2, size_y // 2, 2, size_z // 2, 2)]
    ppermute x88 -> x10, waiting for transfers between devices: 9.22 us -> 19.6 us  [shifted(): lax.ppermute(value, axis, [(i, i + by) for i in range(size) if 0 <= i + b...]
  transfers between devices with their start and end apart: 88 -> 11, of which waited for: 14 -> 9; matrix products, arithmetic and copies ran while one was open for 19% -> 0% of each run, Pallas kernels for 0% -> 10%
where the time goes in v2:
time: 121 us
  starting transfers between devices  55.8 us (46%)
  Pallas kernels  30.9 us (26%)
  waiting for transfers between devices  21.2 us (18%)
  blocking collectives  9.37 us (8%)
  other arithmetic  1.52 us (1%)
  local copies, waits for them, and re-layouts  1.5 us (1%)
    ppermute x10, starting transfers between devices, shifted(): lax.ppermute(value, axis, [(i, i + by) for i in range(size) if 0 <= i + b...  35 us
    pallas_call x5, Pallas kernels, call(): pl.pallas_call(kernel, out_shape=[jax.ShapeDtypeStruct(s, f32) for s in o...  30.9 us
    all_to_all x1, starting transfers between devices, per_device(): every = lax.all_to_all(sums, 'wide', 0, 0)  20.8 us
    ppermute x10, waiting for transfers between devices, shifted(): lax.ppermute(value, axis, [(i, i + by) for i in range(size) if 0 <= i + b...  19.6 us
    all_to_all x1, blocking collectives, per_device(): gathered = lax.all_to_all(chunk, 'narrow', 0, 0)  9.37 us
  transfers between devices with their start and end apart: 11, of which 9 were waited for; matrix products, arithmetic and copies ran while one was open for 0% of the time, Pallas kernels for 10%

profile of v2, /device:TPU:1, one launch (start us, length us, event | category | flops | bytes accessed | tf_op | source)
XLA Modules:
  0.0 120.5 jit_solution(8892552588165545136)
XLA Ops:
  0.0 1.3 %pad_maximum_fusion.3 = (f32[3,16,4,256]{3,2,1,0:T(4,128)S(1)}, f32[3,16,4,256]{3,2,1,0:T(4,128)S(1)}) fusion(f32[1,16,16,256]{3,2,1,0:T(8,128)} %bitcast.3, f32[1,16,16,256]{3,2,1,0:T(8,128)} %bitcast.5, f32[1,16,16,256]{3,2,1,0:T(8,128)} %bitcast.7), kind=kLoop, calls=%fused_computation.3 | loop fusion | flops 196608 | bytes 1179648 | tf_op jit(solution)/shard_map/slice | solution.py:478
  1.4 4.0 %collective-permute-start = (f32[3,16,4,256]{3,2,1,0:T(4,128)S(1)}, f32[3,16,4,256]{3,2,1,0:T(4,128)S(1)}, u32[]{:S(2)}, u32[]{:S(2)}) collective-permute-start(f32[3,16,4,256]{3,2,1,0:T(4,128)S(1)} %get-tuple-element.23), channel_id=1, source_target_pairs={{0,1},{1,2},{2,3},{4,5},{5,6},{6,7},{8,9},{9,10},{10,11},{12,13},{... | collective-permute-start | bytes 589832 | tf_op jit(solution)/shard_map/ppermute | solution.py:473
  5.3 1.3 %collective-permute-start.1 = (f32[3,16,4,256]{3,2,1,0:T(4,128)S(1)}, f32[3,16,4,256]{3,2,1,0:T(4,128)S(1)}, u32[]{:S(2)}, u32[]{:S(2)}) collective-permute-start(f32[3,16,4,256]{3,2,1,0:T(4,128)S(1)} %get-tuple-element.24), channel_id=1, source_target_pairs={{1,0},{2,1},{3,2},{5,4},{6,5},{7,6},{9,8},{10,9},{11,10},{13,12},{... | collective-permute-start | bytes 589832 | tf_op jit(solution)/shard_map/ppermute | solution.py:473
  6.6 1.3 %collective-permute-done = f32[3,16,4,256]{3,2,1,0:T(4,128)S(1)} collective-permute-done((f32[3,16,4,256]{3,2,1,0:T(4,128)S(1)}, f32[3,16,4,256]{3,2,1,0:T(4,128)S(1)}, u32[]{:S(2)}, u32[]{:S(2)}) %collective-permute-start) | collective-permute-done | bytes 196640 | tf_op jit(solution)/shard_map/ppermute | solution.py:473
  7.9 3.8 %collective-permute-done.1 = f32[3,16,4,256]{3,2,1,0:T(4,128)S(1)} collective-permute-done((f32[3,16,4,256]{3,2,1,0:T(4,128)S(1)}, f32[3,16,4,256]{3,2,1,0:T(4,128)S(1)}, u32[]{:S(2)}, u32[]{:S(2)}) %collective-permute-start.1) | collective-permute-done | bytes 196640 | tf_op jit(solution)/shard_map/ppermute | solution.py:473
  11.7 0.2 pad_maximum_fusion.own.own0
  12.0 7.3 %collective-permute-start.3 = (f32[3,4,24,256]{3,2,1,0:T(8,128)S(1)}, f32[3,4,24,256]{3,2,1,0:T(8,128)S(1)}, u32[]{:S(2)}, u32[]{:S(2)}) collective-permute-start(f32[3,4,24,256]{3,2,1,0:T(8,128)S(1)} %get-tuple-element.21), channel_id=1, source_target_pairs={{4,0},{8,4},{12,8},{16,12},{20,16},{24,20},{28,24},{32,28},{36,32}... | collective-permute-start | bytes 884744 | tf_op jit(solution)/shard_map/ppermute | solution.py:473
  19.3 1.9 %collective-permute-start.2 = (f32[3,4,24,256]{3,2,1,0:T(8,128)S(1)}, f32[3,4,24,256]{3,2,1,0:T(8,128)S(1)}, u32[]{:S(2)}, u32[]{:S(2)}) collective-permute-start(f32[3,4,24,256]{3,2,1,0:T(8,128)S(1)} %get-tuple-element.22), channel_id=1, source_target_pairs={{0,4},{4,8},{8,12},{12,16},{16,20},{20,24},{24,28},{28,32},{32,36}... | collective-permute-start | bytes 884744 | tf_op jit(solution)/shard_map/ppermute | solution.py:473
  21.2 1.4 %collective-permute-done.3.xhi.xhi0 = f32[3,4,24,256]{3,2,1,0:T(8,128)S(1)} collective-permute-done((f32[3,4,24,256]{3,2,1,0:T(8,128)S(1)}, f32[3,4,24,256]{3,2,1,0:T(8,128)S(1)}, u32[]{:S(2)}, u32[]{:S(2)}) %collective-permute-start.3) | collective-permute-done | bytes 294944 | tf_op jit(solution)/shard_map/ppermute | solution.py:473
  22.6 2.2 %collective-permute-done.2.xlo.xlo0 = f32[3,4,24,256]{3,2,1,0:T(8,128)S(1)} collective-permute-done((f32[3,4,24,256]{3,2,1,0:T(8,128)S(1)}, f32[3,4,24,256]{3,2,1,0:T(8,128)S(1)}, u32[]{:S(2)}, u32[]{:S(2)}) %collective-permute-start.2) | collective-permute-done | bytes 294944 | tf_op jit(solution)/shard_map/ppermute | solution.py:473
  24.8 6.4 %down0.1 = f32[4,25,8,128]{3,2,1,0:T(8,128)S(1)} custom-call(f32[3,16,24,256]{3,2,1,0:T(8,128)S(1)} %pad_maximum_fusion.own.own0, f32[3,4,24,256]{3,2,1,0:T(8,128)S(1)} %collective-permute-done.2.xlo.xlo0, f32[3,4,24,256]{3,2,1,0:T(8,128)S(1)} %collective-permute-done.3.xhi.xhi0), custom_call_target="tpu_custom_call" | custom-call | tf_op jit(solution)/shard_map/down0/pallas_call | solution.py:460
  31.3 9.4 %all_to_all.10.own.own1 = f32[4,25,8,128]{3,2,1,0:T(8,128)S(1)} all-to-all(f32[4,25,8,128]{3,2,1,0:T(8,128)S(1)} %down0.1), channel_id=1, replica_groups=mesh['wide'=128,'narrow'=4] {'narrow'}, dimensions={0} | all-to-all | bytes 819200 | tf_op jit(solution)/shard_map/all_to_all | solution.py:493
  40.6 1.9 %collective-permute-start.5 = (f32[4,25,8,128]{3,2,1,0:T(8,128)S(1)}, f32[4,25,8,128]{3,2,1,0:T(8,128)S(1)}, u32[]{:S(2)}, u32[]{:S(2)}) collective-permute-start(f32[4,25,8,128]{3,2,1,0:T(8,128)S(1)} %all_to_all.10.own.own1), channel_id=1, source_target_pairs={{4,0},{8,4},{12,8},{16,12},{20,16},{24,20},{28,24},{32,28},{36,32}... | collective-permute-start | bytes 1228808 | tf_op jit(solution)/shard_map/ppermute | solution.py:473
  42.5 5.7 %collective-permute-start.4 = (f32[4,25,8,128]{3,2,1,0:T(8,128)S(1)}, f32[4,25,8,128]{3,2,1,0:T(8,128)S(1)}, u32[]{:S(2)}, u32[]{:S(2)}) collective-permute-start(f32[4,25,8,128]{3,2,1,0:T(8,128)S(1)} %all_to_all.10.own.own1), channel_id=1, source_target_pairs={{0,4},{4,8},{8,12},{12,16},{16,20},{20,24},{24,28},{28,32},{32,36}... | collective-permute-start | bytes 1228808 | tf_op jit(solution)/shard_map/ppermute | solution.py:473
  48.3 3.7 %collective-permute-done.5.hi.hi1 = f32[4,25,8,128]{3,2,1,0:T(8,128)S(1)} collective-permute-done((f32[4,25,8,128]{3,2,1,0:T(8,128)S(1)}, f32[4,25,8,128]{3,2,1,0:T(8,128)S(1)}, u32[]{:S(2)}, u32[]{:S(2)}) %collective-permute-start.5) | collective-permute-done | bytes 409632 | tf_op jit(solution)/shard_map/ppermute | solution.py:473
  52.0 1.2 collective-permute-done.4.lo.lo1
  53.2 5.4 %down1.1 = (f32[14,16,128]{2,1,0:T(8,128)S(1)}, f32[14,16,128]{2,1,0:T(8,128)S(1)}, f32[24,16,128]{2,1,0:T(8,128)S(1)}, f32[8,128]{1,0:T(8,128)S(1)}) custom-call(f32[4,25,8,128]{3,2,1,0:T(8,128)S(1)} %collective-permute-done.4.lo.lo1, f32[4,25,8,128]{3,2,1,0:T(8,128)S(1)} %all_to_all.10.own.own1, f32[4,25,8,128]{3,2,1,0:T(8,128)S(1)} %collective-permute-done.5.hi.hi1), custom_call_target="tpu_custom_call" | custom-call | tf_op jit(solution)/shard_map/down1/pallas_call | solution.py:460
  58.5 3.6 %collective-permute-start.7 = (f32[14,16,128]{2,1,0:T(8,128)S(1)}, f32[14,16,128]{2,1,0:T(8,128)S(1)}, u32[]{:S(2)}, u32[]{:S(2)}) collective-permute-start(f32[14,16,128]{2,1,0:T(8,128)S(1)} %get-tuple-element.13), channel_id=1, source_target_pairs={{0,8},{4,12},{8,16},{12,20},{16,24},{20,28},{24,32},{28,36},{32,40... | collective-permute-start | bytes 344072 | tf_op jit(solution)/shard_map/ppermute | solution.py:473
  62.1 6.8 %collective-permute-start.6 = (f32[14,16,128]{2,1,0:T(8,128)S(1)}, f32[14,16,128]{2,1,0:T(8,128)S(1)}, u32[]{:S(2)}, u32[]{:S(2)}) collective-permute-start(f32[14,16,128]{2,1,0:T(8,128)S(1)} %get-tuple-element.13), channel_id=1, source_target_pairs={{0,16},{4,20},{8,24},{12,28},{16,32},{20,36},{24,40},{28,44},{32,4... | collective-permute-start | bytes 344072 | tf_op jit(solution)/shard_map/ppermute | solution.py:473
  68.9 1.3 %collective-permute-start.9 = (f32[14,16,128]{2,1,0:T(8,128)S(1)}, f32[14,16,128]{2,1,0:T(8,128)S(1)}, u32[]{:S(2)}, u32[]{:S(2)}) collective-permute-start(f32[14,16,128]{2,1,0:T(8,128)S(1)} %get-tuple-element.15), channel_id=1, source_target_pairs={{16,0},{20,4},{24,8},{28,12},{32,16},{36,20},{40,24},{44,28},{48,3... | collective-permute-start | bytes 344072 | tf_op jit(solution)/shard_map/ppermute | solution.py:473
  70.2 1.3 %collective-permute-start.8 = (f32[14,16,128]{2,1,0:T(8,128)S(1)}, f32[14,16,128]{2,1,0:T(8,128)S(1)}, u32[]{:S(2)}, u32[]{:S(2)}) collective-permute-start(f32[14,16,128]{2,1,0:T(8,128)S(1)} %get-tuple-element.15), channel_id=1, source_target_pairs={{8,0},{12,4},{16,8},{20,12},{24,16},{28,20},{32,24},{36,28},{40,32... | collective-permute-start | bytes 344072 | tf_op jit(solution)/shard_map/ppermute | solution.py:473
  71.5 0.0 collective-permute-done.7.dn2
  71.5 0.0 collective-permute-done.6.dn4
  71.6 3.9 %collective-permute-done.9.up4 = f32[14,16,128]{2,1,0:T(8,128)S(1)} collective-permute-done((f32[14,16,128]{2,1,0:T(8,128)S(1)}, f32[14,16,128]{2,1,0:T(8,128)S(1)}, u32[]{:S(2)}, u32[]{:S(2)}) %collective-permute-start.9) | collective-permute-done | bytes 114720 | tf_op jit(solution)/shard_map/ppermute | solution.py:473
  75.5 2.0 %collective-permute-done.8.up2 = f32[14,16,128]{2,1,0:T(8,128)S(1)} collective-permute-done((f32[14,16,128]{2,1,0:T(8,128)S(1)}, f32[14,16,128]{2,1,0:T(8,128)S(1)}, u32[]{:S(2)}, u32[]{:S(2)}) %collective-permute-start.8) | collective-permute-done | bytes 114720 | tf_op jit(solution)/shard_map/ppermute | solution.py:473
  77.5 5.3 %bottom.1 = (f32[8,16,128]{2,1,0:T(8,128)S(1)}, f32[128,1,128]{2,1,0:T(1,128)}) custom-call(f32[14,16,128]{2,1,0:T(8,128)S(1)} %collective-permute-done.6.dn4, f32[14,16,128]{2,1,0:T(8,128)S(1)} %collective-permute-done.7.dn2, f32[24,16,128]{2,1,0:T(8,128)S(1)} %get-tuple-element.14.mine, f32[14,16,128]{2,1,0:T(8,128)S(1)} %collective-permute-done.8.up2, ...), custom_call_target="tpu_custom_call" | custom-call | tf_op jit(solution)/shard_map/bottom/pallas_call | solution.py:460
  82.8 0.6 copy-done
  83.4 20.8 %all-to-all-start.1 = ((f32[128,1,128]{2,1,0:T(1,128)}), f32[128,1,128]{2,1,0:T(1,128)}, u32[]{:S(2)}, u32[]{:S(2)}) async-start(f32[128,1,128]{2,1,0:T(1,128)} %get-tuple-element.17), calls=%async_computation.1 | async-start | bytes 131072 | tf_op jit(solution)/shard_map/all_to_all | solution.py:523
  104.2 0.8 copy-done.1
  105.1 12.0 %up.1 = (f32[16,16,256]{2,1,0:T(8,128)S(1)}, f32[16,16,256]{2,1,0:T(8,128)S(1)}) custom-call(f32[8,16,128]{2,1,0:T(8,128)S(1)} %copy-done.1, f32[4,25,8,128]{3,2,1,0:T(8,128)S(1)} %collective-permute-done.4.lo.lo1, f32[4,25,8,128]{3,2,1,0:T(8,128)S(1)} %all_to_all.10.own.own1, f32[4,25,8,128]{3,2,1,0:T(8,128)S(1)} %collective-permute-done.5.hi.hi1, ...), custom_call_target="tpu_custom_call" | custom-call | tf_op jit(solution)/shard_map/up/pallas_call | solution.py:460
  117.1 1.6 %all-to-all-done.1.every = f32[128,1,128]{2,1,0:T(1,128)} async-done(((f32[128,1,128]{2,1,0:T(1,128)}), f32[128,1,128]{2,1,0:T(1,128)}, u32[]{:S(2)}, u32[]{:S(2)}) %all-to-all-start.1) | async-done | bytes 65568 | tf_op jit(solution)/shard_map/all_to_all | solution.py:523
  118.7 1.8 %final.1 = f32[16,16,256]{2,1,0:T(8,128)} custom-call(f32[128,1,128]{2,1,0:T(1,128)} %all-to-all-done.1.every, f32[16,16,256]{2,1,0:T(8,128)S(1)} %get-tuple-element.19.out_s, f32[16,16,256]{2,1,0:T(8,128)S(1)} %get-tuple-element.20.out_c), custom_call_target="tpu_custom_call" | custom-call | tf_op jit(solution)/shard_map/final/pallas_call | solution.py:460
  (9 shorter events, 0.1 us)
Async XLA Ops:
  0.0 11.7 %copy-start.2 = (f32[16,16,256]{2,1,0:T(8,128)S(1)}, f32[16,16,256]{2,1,0:T(8,128)}, u32[]{:S(2)}) copy-start(f32[16,16,256]{2,1,0:T(8,128)} %param.5) | copy-start | bytes 786436
  0.0 11.7 %copy-start.3 = (f32[16,16,256]{2,1,0:T(8,128)S(1)}, f32[16,16,256]{2,1,0:T(8,128)}, u32[]{:S(2)}) copy-start(f32[16,16,256]{2,1,0:T(8,128)} %param.4) | copy-start | bytes 786436
  0.0 11.7 %copy-start.4 = (f32[16,16,256]{2,1,0:T(8,128)S(1)}, f32[16,16,256]{2,1,0:T(8,128)}, u32[]{:S(2)}) copy-start(f32[16,16,256]{2,1,0:T(8,128)} %param.3) | copy-start | bytes 786436
  1.4 6.5 %collective-permute-start = (f32[3,16,4,256]{3,2,1,0:T(4,128)S(1)}, f32[3,16,4,256]{3,2,1,0:T(4,128)S(1)}, u32[]{:S(2)}, u32[]{:S(2)}) collective-permute-start(f32[3,16,4,256]{3,2,1,0:T(4,128)S(1)} %get-tuple-element.23), channel_id=1, source_target_pairs={{0,1},{1,2},{2,3},{4,5},{5,6},{6,7},{8,9},{9,10},{10,11},{12,13},{... | collective-permute-start | bytes 589832 | tf_op jit(solution)/shard_map/ppermute | solution.py:473
  5.3 6.4 %collective-permute-start.1 = (f32[3,16,4,256]{3,2,1,0:T(4,128)S(1)}, f32[3,16,4,256]{3,2,1,0:T(4,128)S(1)}, u32[]{:S(2)}, u32[]{:S(2)}) collective-permute-start(f32[3,16,4,256]{3,2,1,0:T(4,128)S(1)} %get-tuple-element.24), channel_id=1, source_target_pairs={{1,0},{2,1},{3,2},{5,4},{6,5},{7,6},{9,8},{10,9},{11,10},{13,12},{... | collective-permute-start | bytes 589832 | tf_op jit(solution)/shard_map/ppermute | solution.py:473
  12.0 10.6 %collective-permute-start.3 = (f32[3,4,24,256]{3,2,1,0:T(8,128)S(1)}, f32[3,4,24,256]{3,2,1,0:T(8,128)S(1)}, u32[]{:S(2)}, u32[]{:S(2)}) collective-permute-start(f32[3,4,24,256]{3,2,1,0:T(8,128)S(1)} %get-tuple-element.21), channel_id=1, source_target_pairs={{4,0},{8,4},{12,8},{16,12},{20,16},{24,20},{28,24},{32,28},{36,32}... | collective-permute-start | bytes 884744 | tf_op jit(solution)/shard_map/ppermute | solution.py:473
  19.3 5.6 %collective-permute-start.2 = (f32[3,4,24,256]{3,2,1,0:T(8,128)S(1)}, f32[3,4,24,256]{3,2,1,0:T(8,128)S(1)}, u32[]{:S(2)}, u32[]{:S(2)}) collective-permute-start(f32[3,4,24,256]{3,2,1,0:T(8,128)S(1)} %get-tuple-element.22), channel_id=1, source_target_pairs={{0,4},{4,8},{8,12},{12,16},{16,20},{20,24},{24,28},{28,32},{32,36}... | collective-permute-start | bytes 884744 | tf_op jit(solution)/shard_map/ppermute | solution.py:473
  40.6 11.3 %collective-permute-start.5 = (f32[4,25,8,128]{3,2,1,0:T(8,128)S(1)}, f32[4,25,8,128]{3,2,1,0:T(8,128)S(1)}, u32[]{:S(2)}, u32[]{:S(2)}) collective-permute-start(f32[4,25,8,128]{3,2,1,0:T(8,128)S(1)} %all_to_all.10.own.own1), channel_id=1, source_target_pairs={{4,0},{8,4},{12,8},{16,12},{20,16},{24,20},{28,24},{32,28},{36,32}... | collective-permute-start | bytes 1228808 | tf_op jit(solution)/shard_map/ppermute | solution.py:473
  42.5 10.6 %collective-permute-start.4 = (f32[4,25,8,128]{3,2,1,0:T(8,128)S(1)}, f32[4,25,8,128]{3,2,1,0:T(8,128)S(1)}, u32[]{:S(2)}, u32[]{:S(2)}) collective-permute-start(f32[4,25,8,128]{3,2,1,0:T(8,128)S(1)} %all_to_all.10.own.own1), channel_id=1, source_target_pairs={{0,4},{4,8},{8,12},{12,16},{16,20},{20,24},{24,28},{28,32},{32,36}... | collective-permute-start | bytes 1228808 | tf_op jit(solution)/shard_map/ppermute | solution.py:473
  58.5 13.0 %collective-permute-start.7 = (f32[14,16,128]{2,1,0:T(8,128)S(1)}, f32[14,16,128]{2,1,0:T(8,128)S(1)}, u32[]{:S(2)}, u32[]{:S(2)}) collective-permute-start(f32[14,16,128]{2,1,0:T(8,128)S(1)} %get-tuple-element.13), channel_id=1, source_target_pairs={{0,8},{4,12},{8,16},{12,20},{16,24},{20,28},{24,32},{28,36},{32,40... | collective-permute-start | bytes 344072 | tf_op jit(solution)/shard_map/ppermute | solution.py:473
  62.1 9.4 %collective-permute-start.6 = (f32[14,16,128]{2,1,0:T(8,128)S(1)}, f32[14,16,128]{2,1,0:T(8,128)S(1)}, u32[]{:S(2)}, u32[]{:S(2)}) collective-permute-start(f32[14,16,128]{2,1,0:T(8,128)S(1)} %get-tuple-element.13), channel_id=1, source_target_pairs={{0,16},{4,20},{8,24},{12,28},{16,32},{20,36},{24,40},{28,44},{32,4... | collective-permute-start | bytes 344072 | tf_op jit(solution)/shard_map/ppermute | solution.py:473
  68.9 6.5 %collective-permute-start.9 = (f32[14,16,128]{2,1,0:T(8,128)S(1)}, f32[14,16,128]{2,1,0:T(8,128)S(1)}, u32[]{:S(2)}, u32[]{:S(2)}) collective-permute-start(f32[14,16,128]{2,1,0:T(8,128)S(1)} %get-tuple-element.15), channel_id=1, source_target_pairs={{16,0},{20,4},{24,8},{28,12},{32,16},{36,20},{40,24},{44,28},{48,3... | collective-permute-start | bytes 344072 | tf_op jit(solution)/shard_map/ppermute | solution.py:473
  70.2 7.3 %collective-permute-start.8 = (f32[14,16,128]{2,1,0:T(8,128)S(1)}, f32[14,16,128]{2,1,0:T(8,128)S(1)}, u32[]{:S(2)}, u32[]{:S(2)}) collective-permute-start(f32[14,16,128]{2,1,0:T(8,128)S(1)} %get-tuple-element.15), channel_id=1, source_target_pairs={{8,0},{12,4},{16,8},{20,12},{24,16},{28,20},{32,24},{36,28},{40,32... | collective-permute-start | bytes 344072 | tf_op jit(solution)/shard_map/ppermute | solution.py:473
  82.8 0.6 copy-start
  83.4 35.3 %all-to-all-start.1 = ((f32[128,1,128]{2,1,0:T(1,128)}), f32[128,1,128]{2,1,0:T(1,128)}, u32[]{:S(2)}, u32[]{:S(2)}) async-start(f32[128,1,128]{2,1,0:T(1,128)} %get-tuple-element.17), calls=%async_computation.1 | async-start | bytes 131072 | tf_op jit(solution)/shard_map/all_to_all | solution.py:523
  104.2 0.8 copy-start.1

commit v3 on v2

--- a/solution.py
+++ b/solution.py
@@ -10,6 +10,9 @@
 f32 = jnp.float32
 HALO = 4
 LIMIT = 24
+C0, S0, W0, R0 = 22, 22, 20, 16
+C1, S1, W1, R1 = 26, 26, 24, 8
+C2, S2, W2, R2 = 42, 40, 38, 36
 DAMPING = 0.8
 BASE_TAU = 16.0
 VMEM = pl.BlockSpec(memory_space=pltpu.VMEM)
@@ -24,8 +27,15 @@
     return lax.broadcasted_iota(jnp.int32, shape, dim)
 
 
-def dot(a, b):
-    return jnp.dot(a, b, precision=lax.Precision.HIGHEST, preferred_element_type=f32)
+def dot(x, matrix):
+    matrix = matrix.astype(jnp.bfloat16)
+    total = None
+    for _ in range(3):
+        part = x.astype(jnp.bfloat16)
+        x = x - part.astype(f32)
+        term = jnp.dot(part, matrix, preferred_element_type=f32)
+        total = term if total is None else total + term
+    return total
 
 
 def rounded(x):
@@ -183,33 +193,40 @@
         copy.wait()
 
 
-def fetch0(own, xlo, xhi, fields, sems):
+def sides(low, high):
+    even = lax.rem(lax.axis_index("wide"), 2) == 0
+    return jnp.where(even, high, low), jnp.where(even, low, high)
+
+
+def fetch0(own, inner, outer, fields, sems):
+    inner_at, outer_at = sides(0, 20)
     sources, targets = [], []
     for index, ref in enumerate(fields):
-        for part, lo, hi in ((xlo, 0, 4), (own, 4, 20), (xhi, 20, 24)):
+        for part, lo, n in ((own, 4, 16), (inner, inner_at, 4), (outer, outer_at, 4)):
             sources.append(part.at[index])
-            targets.append(ref.at[pl.ds(lo, hi - lo)])
+            targets.append(ref.at[pl.ds(lo, n)])
     return fetch(sources, targets, sems)
 
 
-def fetch1(lo, own, hi, fields, sems):
+def fetch1(own, inner, outer, fields, sems):
+    inner_at, outer_at = sides(2, 18)
     sources, targets = [], []
     for index, ref in fields:
-        for part, source in enumerate((lo, own, hi)):
+        for source, lo in ((own, 10), (inner, inner_at), (outer, outer_at)):
             for j in range(4):
                 sources.append(source.at[j, pl.ds(index * 8, 8)])
-                targets.append(ref.at[pl.ds(2 + part * 8, 8), pl.ds(8 * j, 8), :])
+                targets.append(ref.at[pl.ds(lo, 8), pl.ds(8 * j, 8), :])
     return fetch(sources, targets, sems)
 
 
-def down0(own, xlo, xhi, out, vs, vc, cx, cy, cz, dg, wt, ss, cc, m, us, uc, pair, thin, sems):
-    copies = fetch0(own, xlo, xhi, (m, ss, cc), sems)
+def down0(own, inner, outer, out, vs, vc, cx, cy, cz, dg, wt, ss, cc, m, us, uc, pair, thin, sems):
+    copies = fetch0(own, inner, outer, (m, ss, cc), sems)
     wait(copies[:3])
-    coefficients(0, m, cx, cy, cz, dg, wt, 1, 23, 2, None, 256)
+    coefficients(0, m, cx, cy, cz, dg, wt, 1, 23, C0, None, 256)
     coefs = (cx, cy, cz, dg)
     wait(copies[3:])
-    start(1, 23, 2, (ss, cc), (us, uc), wt)
-    sweep(2, 22, 2, (ss, cc), (us, uc), (vs, vc), coefs, wt)
+    start(1, 23, S0, (ss, cc), (us, uc), wt)
+    sweep(2, 22, W0, (ss, cc), (us, uc), (vs, vc), coefs, wt)
 
     def rest(i, n, sums):
         res_s, res_c, sums = products(i, n, ss, cc, vs, vc, coefs, sums)
@@ -220,7 +237,7 @@
         return sums
 
     zero = jnp.zeros((24, 256), f32)
-    num, den = by_rows(4, 20, 2, rest, (zero, zero))
+    num, den = by_rows(4, 20, R0, rest, (zero, zero))
     thin[...] = flat_dot(pair[...], coarse_z(256, 256, 128, 128, 1))
     value = fold_y(thin, 0, 24, 4, 8)
     sub = iota((24, 256), 0)
@@ -235,21 +252,21 @@
 
 
 def down1(
-    lo, own, hi, to_up, to_down, mine, sums,
-    vs, vc, cx, cy, cz, dg, wt, ss, cc, m, us, uc, pair, thin, inner, sems,
+    own, inner, outer, to_up, to_down, mine, sums,
+    vs, vc, cx, cy, cz, dg, wt, ss, cc, m, us, uc, pair, thin, parts, sems,
 ):
-    copies = fetch1(lo, own, hi, ((2, m), (0, ss), (1, cc)), sems)
-    partial = fetch([own.at[j, 24] for j in range(4)], [inner.at[j] for j in range(4)], sems.at[pl.ds(36, 4)])
+    copies = fetch1(own, inner, outer, ((2, m), (0, ss), (1, cc)), sems)
+    partial = fetch([own.at[j, 24] for j in range(4)], [parts.at[j] for j in range(4)], sems.at[pl.ds(36, 4)])
     for ref in (ss, cc, m, vs, vc):
         ref[0:2] = jnp.zeros((2, 32, 128), f32)
         ref[26:28] = jnp.zeros((2, 32, 128), f32)
     wait(copies[:12])
-    coefficients(1, m, cx, cy, cz, dg, wt, 1, 27, 2, 32, 128)
+    coefficients(1, m, cx, cy, cz, dg, wt, 1, 27, C1, 32, 128)
     coefs = (cx, cy, cz, dg)
     wait(copies[12:])
     wait(partial)
-    start(1, 27, 2, (ss, cc), (us, uc), wt)
-    sweep(2, 26, 4, (ss, cc), (us, uc), (vs, vc), coefs, wt)
+    start(1, 27, S1, (ss, cc), (us, uc), wt)
+    sweep(2, 26, W1, (ss, cc), (us, uc), (vs, vc), coefs, wt)
 
     def rest(i, n, sums):
         res_s, res_c, sums = products(i, n, ss, cc, vs, vc, coefs, sums)
@@ -262,9 +279,9 @@
         return sums
 
     zero = jnp.zeros((32, 128), f32)
-    by_rows(2, 10, 4, rest, (zero, zero))
-    num, den = by_rows(10, 18, 4, rest, (zero, zero))
-    by_rows(18, 26, 4, rest, (zero, zero))
+    by_rows(2, 10, R1, rest, (zero, zero))
+    num, den = by_rows(10, 18, R1, rest, (zero, zero))
+    by_rows(18, 26, R1, rest, (zero, zero))
     thin[...] = flat_dot(pair[...], coarse_z(128, 256, 64, 128, 2))
     place = lax.axis_index("wide")
     low = jnp.where(place == 1, fold_y(thin, 0, 2, 0, 16), 0.0)
@@ -285,7 +302,7 @@
     lane = iota((8, 128), 1)
     num = jnp.sum(num) * 8.0
     den = jnp.sum(den) * 8.0
-    finer = inner[0] + inner[1] + inner[2] + inner[3]
+    finer = parts[0] + parts[1] + parts[2] + parts[3]
     sums[...] = finer + jnp.where(lane == 0, num, jnp.where(lane == 1, den, 0.0))
 
 
@@ -328,16 +345,16 @@
     c2 = (cx2, cy2, cz2, dg2)
     c3 = (cx3, cy3, cz3, dg3)
     c4 = (cx4, cy4, cz4, dg4)
-    coefficients(2, m2, *c2, wt2, 1, 43, 6, 16, 64)
-    start(2, 42, 8, (r2,), (u2,), wt2)
-    sweep(3, 41, 8, (r2,), (u2,), (v2,), c2, wt2)
+    coefficients(2, m2, *c2, wt2, 1, 43, C2, 16, 64)
+    start(2, 42, S2, (r2,), (u2,), wt2)
+    sweep(3, 41, W2, (r2,), (u2,), (v2,), c2, wt2)
 
     def rest2(i, n, sums):
         res = residual(i, n, r2[at(i, n)], v2, *c2)
         pair2[at(lax.div(i - 4, 2), n // 2)] = pairs(res)
         return sums
 
-    by_rows(4, 40, 6, rest2, 0)
+    by_rows(4, 40, R2, rest2, 0)
     own = slice(20, 24)
     num2, den2 = both_products(r2[own], v2[own], residual(20, 4, r2[own], v2, *c2), 64)
     pair2[18:40] = pairs(m2[...])
@@ -381,23 +398,23 @@
 
 
 def up(
-    e2, lo1, own1, hi1, own0, xlo0, xhi0, out_s, out_c,
+    e2, own1, inner1, outer1, own0, inner0, outer0, out_s, out_c,
     vs1, vc1, cx1, cy1, cz1, wt1, ss1, cc1, m1, as1, ac1, bs1, bc1,
     vs0, vc0, cx0, cy0, cz0, wt0, ss0, cc0, m0, as0, ac0, bs0, bc0,
     wide, add, block, thick, full, sems,
 ):
-    copies1 = fetch1(lo1, own1, hi1, ((2, m1), (0, ss1), (1, cc1)), sems)
-    copies0 = fetch0(own0, xlo0, xhi0, (m0, ss0, cc0), sems.at[pl.ds(36, 9)])
+    copies1 = fetch1(own1, inner1, outer1, ((2, m1), (0, ss1), (1, cc1)), sems)
+    copies0 = fetch0(own0, inner0, outer0, (m0, ss0, cc0), sems.at[pl.ds(36, 9)])
     c1 = (cx1, cy1, cz1)
     c0 = (cx0, cy0, cz0)
     wait(copies1)
-    coefficients(1, m1, cx1, cy1, cz1, None, wt1, 5, 23, 2, 32, 128)
-    start(5, 23, 2, (ss1, cc1), (as1, ac1), wt1)
-    sweep(6, 22, 4, (ss1, cc1), (as1, ac1), (vs1, vc1), c1, wt1)
+    coefficients(1, m1, cx1, cy1, cz1, None, wt1, 5, 23, C1, 32, 128)
+    start(5, 23, S1, (ss1, cc1), (as1, ac1), wt1)
+    sweep(6, 22, W1, (ss1, cc1), (as1, ac1), (vs1, vc1), c1, wt1)
     wait(copies0)
-    coefficients(0, m0, cx0, cy0, cz0, None, wt0, 1, 23, 2, None, 256)
-    start(1, 23, 2, (ss0, cc0), (as0, ac0), wt0)
-    sweep(2, 22, 2, (ss0, cc0), (as0, ac0), (vs0, vc0), c0, wt0)
+    coefficients(0, m0, cx0, cy0, cz0, None, wt0, 1, 23, C0, None, 256)
+    start(1, 23, S0, (ss0, cc0), (as0, ac0), wt0)
+    sweep(2, 22, W0, (ss0, cc0), (as0, ac0), (vs0, vc0), c0, wt0)
     wide[:, pl.ds(0, 16, stride=2), :] = e2[...]
     wide[:, pl.ds(1, 16, stride=2), :] = e2[...]
     add[...] = flat_dot(wide[...], fine_z(64, 128, 128, 256, 2))
@@ -409,8 +426,8 @@
         ac1[at(i, n)] = vc1[at(i, n)] + doubled(both[:, :, 128:256])
         return carry
 
-    by_rows(6, 22, 4, correct1, 0)
-    sweep(8, 20, 4, (ss1, cc1), (as1, ac1), (bs1, bc1), c1, wt1)
+    by_rows(6, 22, R1, correct1, 0)
+    sweep(8, 20, W1, (ss1, cc1), (as1, ac1), (bs1, bc1), c1, wt1)
     place = lax.axis_index("narrow")
     block[:, 0:8, :] = jnp.zeros((20, 8, 128), f32)
     block[:, 40:48, :] = jnp.zeros((20, 8, 128), f32)
@@ -433,15 +450,15 @@
         ac0[at(i, n)] = vc0[at(i, n)] + doubled(full[at(10 + k, n // 2)])
         return carry
 
-    by_rows(2, 22, 2, correct0, 0)
-    sweep(3, 21, 2, (ss0, cc0), (as0, ac0), (bs0, bc0), c0, wt0)
+    by_rows(2, 22, R0, correct0, 0)
+    sweep(3, 21, W0, (ss0, cc0), (as0, ac0), (bs0, bc0), c0, wt0)
 
     def last0(i, n, carry):
         for r, v, o in ((ss0, bs0, out_s), (cc0, bc0, out_c)):
             o[at(i - 4, n)] = relaxed(i, n, r, v, wt0, *c0)[:, 4:20, :]
         return carry
 
-    by_rows(4, 20, 2, last0, 0)
+    by_rows(4, 20, W0, last0, 0)
 
 
 def final(every, out_s, out_c, out):
@@ -473,17 +490,24 @@
     return lax.ppermute(value, axis, [(i, i + by) for i in range(size) if 0 <= i + by < size])
 
 
+def swapped(value, first):
+    pairs = [(i, i + 1) for i in range(first, lax.axis_size("wide") - 1, 2)]
+    return lax.ppermute(value, "wide", pairs + [(b, a) for a, b in pairs])
+
+
 def per_device(mobility, sav_vector, cotangent):
     own = jnp.stack([mobility, sav_vector, cotangent])
     y_lo = shifted(own[:, :, -HALO:], "narrow", 1)
     y_hi = shifted(own[:, :, :HALO], "narrow", -1)
     own = jnp.concatenate([y_lo, own, y_hi], axis=2)
-    x_lo = shifted(own[:, -HALO:], "wide", 1)
-    x_hi = shifted(own[:, :HALO], "wide", -1)
+    last = own.shape[1] - HALO
+    odd = lax.rem(lax.axis_index("wide"), 2)
+    x_outer = swapped(lax.dynamic_slice_in_dim(own, odd * last, HALO, axis=1), 1)
+    x_inner = swapped(lax.dynamic_slice_in_dim(own, (1 - odd) * last, HALO, axis=1), 0)
     a0 = (24, 24, 256)
     (chunk,) = call(
         down0,
-        (own, x_lo, x_hi),
+        (own, x_inner, x_outer),
         [(4, 25, 8, 128)],
         [a0] * 13 + [(24, 24, 128)],
         "down0",
@@ -491,12 +515,12 @@
         [HBM] * 3,
     )
     gathered = lax.all_to_all(chunk, "narrow", 0, 0)
-    lo = shifted(gathered, "wide", 1)
-    hi = shifted(gathered, "wide", -1)
+    outer = swapped(gathered, 1)
+    inner = swapped(gathered, 0)
     a1 = (28, 32, 128)
     to_up, to_down, mine, finer = call(
         down1,
-        (lo, gathered, hi),
+        (gathered, inner, outer),
         [(14, 16, 128), (14, 16, 128), (24, 16, 128), (8, 128)],
         [a1] * 12 + [(24, 32, 256), (24, 32, 128), (4, 8, 128)],
         "down1",
@@ -523,7 +547,7 @@
     every = lax.all_to_all(sums, "wide", 0, 0)
     out_s, out_c = call(
         up,
-        (e2, lo, gathered, hi, own, x_lo, x_hi),
+        (e2, gathered, inner, outer, own, x_inner, x_outer),
         [(16, 16, 256)] * 2,
         [a1] * 13
         + [a0] * 13

time: 121 us -> 110 us (0.909)
  Pallas kernels: 30.9 us -> 19.3 us
  starting transfers between devices: 55.8 us -> 49.8 us
  waiting for transfers between devices: 21.2 us -> 25.3 us
  blocking collectives: 9.37 us -> 12.2 us
    ppermute x10 -> x6, starting transfers between devices: 35 us -> 18.4 us  [shifted(): lax.ppermute(value, axis, [(i, i + by) for i in range(size) if 0 <= i + b...]
    ppermute x0 -> x4, starting transfers between devices: none -> 14 us  [swapped(): return lax.ppermute(value, 'wide', pairs + [(b, a) for a, b in pairs])]
    pallas_call x5, Pallas kernels: 30.9 us -> 19.3 us  [call(): pl.pallas_call(kernel, out_shape=[jax.ShapeDtypeStruct(s, f32) for s in o...]
    ppermute x10 -> x6, waiting for transfers between devices: 19.6 us -> 12.6 us  [shifted(): lax.ppermute(value, axis, [(i, i + by) for i in range(size) if 0 <= i + b...]
    ppermute x0 -> x4, waiting for transfers between devices: none -> 6.16 us  [swapped(): return lax.ppermute(value, 'wide', pairs + [(b, a) for a, b in pairs])]
    all_to_all x1, waiting for transfers between devices: 1.64 us -> 6.54 us  [per_device(): every = lax.all_to_all(sums, 'wide', 0, 0)]
    all_to_all x1, starting transfers between devices: 20.8 us -> 17.4 us  [per_device(): every = lax.all_to_all(sums, 'wide', 0, 0)]
    all_to_all x1, blocking collectives: 9.37 us -> 12.2 us  [per_device(): gathered = lax.all_to_all(chunk, 'narrow', 0, 0)]
  transfers between devices with their start and end apart: 11 -> 11, of which waited for: 9 -> 8; matrix products, arithmetic and copies ran while one was open for 0% -> 0% of each run, Pallas kernels for 10% -> 6%
where the time goes in v3:
time: 110 us
  starting transfers between devices  49.8 us (45%)
  waiting for transfers between devices  25.3 us (23%)
  Pallas kernels  19.3 us (18%)
  blocking collectives  12.2 us (11%)
  other arithmetic  1.52 us (1%)
  local copies, waits for them, and re-layouts  1.51 us (1%)
    pallas_call x5, Pallas kernels, call(): pl.pallas_call(kernel, out_shape=[jax.ShapeDtypeStruct(s, f32) for s in o...  19.3 us
    ppermute x6, starting transfers between devices, shifted(): lax.ppermute(value, axis, [(i, i + by) for i in range(size) if 0 <= i + b...  18.4 us
    all_to_all x1, starting transfers between devices, per_device(): every = lax.all_to_all(sums, 'wide', 0, 0)  17.4 us
    ppermute x4, starting transfers between devices, swapped(): return lax.ppermute(value, 'wide', pairs + [(b, a) for a, b in pairs])  14 us
    ppermute x6, waiting for transfers between devices, shifted(): lax.ppermute(value, axis, [(i, i + by) for i in range(size) if 0 <= i + b...  12.6 us
    all_to_all x1, blocking collectives, per_device(): gathered = lax.all_to_all(chunk, 'narrow', 0, 0)  12.2 us
    all_to_all x1, waiting for transfers between devices, per_device(): every = lax.all_to_all(sums, 'wide', 0, 0)  6.54 us
    ppermute x4, waiting for transfers between devices, swapped(): return lax.ppermute(value, 'wide', pairs + [(b, a) for a, b in pairs])  6.16 us
  transfers between devices with their start and end apart: 11, of which 8 were waited for; matrix products, arithmetic and copies ran while one was open for 0% of the time, Pallas kernels for 6%

profile of v3, /device:TPU:1, one launch (start us, length us, event | category | flops | bytes accessed | tf_op | source)
XLA Modules:
  0.0 109.8 jit_solution(815611471026904250)
XLA Ops:
  0.0 1.3 %pad_maximum_fusion.3 = (f32[3,16,4,256]{3,2,1,0:T(4,128)S(1)}, f32[3,16,4,256]{3,2,1,0:T(4,128)S(1)}) fusion(f32[1,16,16,256]{3,2,1,0:T(8,128)} %bitcast.3, f32[1,16,16,256]{3,2,1,0:T(8,128)} %bitcast.5, f32[1,16,16,256]{3,2,1,0:T(8,128)} %bitcast.7), kind=kLoop, calls=%fused_computation.3 | loop fusion | flops 196608 | bytes 1179648 | tf_op jit(solution)/shard_map/slice | solution.py:500
  1.4 4.0 %collective-permute-start = (f32[3,16,4,256]{3,2,1,0:T(4,128)S(1)}, f32[3,16,4,256]{3,2,1,0:T(4,128)S(1)}, u32[]{:S(2)}, u32[]{:S(2)}) collective-permute-start(f32[3,16,4,256]{3,2,1,0:T(4,128)S(1)} %get-tuple-element.23), channel_id=1, source_target_pairs={{0,1},{1,2},{2,3},{4,5},{5,6},{6,7},{8,9},{9,10},{10,11},{12,13},{... | collective-permute-start | bytes 589832 | tf_op jit(solution)/shard_map/ppermute | solution.py:490
  5.3 1.3 %collective-permute-start.1 = (f32[3,16,4,256]{3,2,1,0:T(4,128)S(1)}, f32[3,16,4,256]{3,2,1,0:T(4,128)S(1)}, u32[]{:S(2)}, u32[]{:S(2)}) collective-permute-start(f32[3,16,4,256]{3,2,1,0:T(4,128)S(1)} %get-tuple-element.24), channel_id=1, source_target_pairs={{1,0},{2,1},{3,2},{5,4},{6,5},{7,6},{9,8},{10,9},{11,10},{13,12},{... | collective-permute-start | bytes 589832 | tf_op jit(solution)/shard_map/ppermute | solution.py:490
  6.6 1.3 %collective-permute-done = f32[3,16,4,256]{3,2,1,0:T(4,128)S(1)} collective-permute-done((f32[3,16,4,256]{3,2,1,0:T(4,128)S(1)}, f32[3,16,4,256]{3,2,1,0:T(4,128)S(1)}, u32[]{:S(2)}, u32[]{:S(2)}) %collective-permute-start) | collective-permute-done | bytes 196640 | tf_op jit(solution)/shard_map/ppermute | solution.py:490
  7.9 3.8 %collective-permute-done.1 = f32[3,16,4,256]{3,2,1,0:T(4,128)S(1)} collective-permute-done((f32[3,16,4,256]{3,2,1,0:T(4,128)S(1)}, f32[3,16,4,256]{3,2,1,0:T(4,128)S(1)}, u32[]{:S(2)}, u32[]{:S(2)}) %collective-permute-start.1) | collective-permute-done | bytes 196640 | tf_op jit(solution)/shard_map/ppermute | solution.py:490
  11.7 0.2 pad_maximum_fusion.own.own0
  11.9 0.1 constant_dynamic-slice_fusion
  12.0 6.2 %collective-permute-start.3 = (f32[3,4,24,256]{3,2,1,0:T(8,128)S(1)}, f32[3,4,24,256]{3,2,1,0:T(8,128)S(1)}, u32[]{:S(2)}, u32[]{:S(2)}) collective-permute-start(f32[3,4,24,256]{3,2,1,0:T(8,128)S(1)} %get-tuple-element.21), channel_id=1, source_target_pairs={{4,8},{12,16},{20,24},{28,32},{36,40},{44,48},{52,56},{60,64},{68,... | collective-permute-start | bytes 884744 | tf_op jit(solution)/shard_map/ppermute | solution.py:495
  18.2 1.9 %collective-permute-start.2 = (f32[3,4,24,256]{3,2,1,0:T(8,128)S(1)}, f32[3,4,24,256]{3,2,1,0:T(8,128)S(1)}, u32[]{:S(2)}, u32[]{:S(2)}) collective-permute-start(f32[3,4,24,256]{3,2,1,0:T(8,128)S(1)} %get-tuple-element.22), channel_id=1, source_target_pairs={{0,4},{8,12},{16,20},{24,28},{32,36},{40,44},{48,52},{56,60},{64,6... | collective-permute-start | bytes 884744 | tf_op jit(solution)/shard_map/ppermute | solution.py:495
  20.2 2.5 %collective-permute-done.3.outer.outer0 = f32[3,4,24,256]{3,2,1,0:T(8,128)S(1)} collective-permute-done((f32[3,4,24,256]{3,2,1,0:T(8,128)S(1)}, f32[3,4,24,256]{3,2,1,0:T(8,128)S(1)}, u32[]{:S(2)}, u32[]{:S(2)}) %collective-permute-start.3) | collective-permute-done | bytes 294944 | tf_op jit(solution)/shard_map/ppermute | solution.py:495
  22.6 0.0 collective-permute-done.2.inner.inner0
  22.6 4.0 %down0.1 = f32[4,25,8,128]{3,2,1,0:T(8,128)S(1)} custom-call(f32[3,16,24,256]{3,2,1,0:T(8,128)S(1)} %pad_maximum_fusion.own.own0, f32[3,4,24,256]{3,2,1,0:T(8,128)S(1)} %collective-permute-done.2.inner.inner0, f32[3,4,24,256]{3,2,1,0:T(8,128)S(1)} %collective-permute-done.3.outer.outer0), custom_call_target="tpu_custom_call" | custom-call | tf_op jit(solution)/shard_map/down0/pallas_call | solution.py:477
  26.6 12.2 %all_to_all.10.own.own1 = f32[4,25,8,128]{3,2,1,0:T(8,128)S(1)} all-to-all(f32[4,25,8,128]{3,2,1,0:T(8,128)S(1)} %down0.1), channel_id=1, replica_groups=mesh['wide'=128,'narrow'=4] {'narrow'}, dimensions={0} | all-to-all | bytes 819200 | tf_op jit(solution)/shard_map/all_to_all | solution.py:517
  38.9 3.9 %collective-permute-start.5 = (f32[4,25,8,128]{3,2,1,0:T(8,128)S(1)}, f32[4,25,8,128]{3,2,1,0:T(8,128)S(1)}, u32[]{:S(2)}, u32[]{:S(2)}) collective-permute-start(f32[4,25,8,128]{3,2,1,0:T(8,128)S(1)} %all_to_all.10.own.own1), channel_id=1, source_target_pairs={{4,8},{12,16},{20,24},{28,32},{36,40},{44,48},{52,56},{60,64},{68,... | collective-permute-start | bytes 1228808 | tf_op jit(solution)/shard_map/ppermute | solution.py:495
  42.8 1.9 %collective-permute-start.4 = (f32[4,25,8,128]{3,2,1,0:T(8,128)S(1)}, f32[4,25,8,128]{3,2,1,0:T(8,128)S(1)}, u32[]{:S(2)}, u32[]{:S(2)}) collective-permute-start(f32[4,25,8,128]{3,2,1,0:T(8,128)S(1)} %all_to_all.10.own.own1), channel_id=1, source_target_pairs={{0,4},{8,12},{16,20},{24,28},{32,36},{40,44},{48,52},{56,60},{64,6... | collective-permute-start | bytes 1228808 | tf_op jit(solution)/shard_map/ppermute | solution.py:495
  44.7 3.7 %collective-permute-done.5.outer.outer1 = f32[4,25,8,128]{3,2,1,0:T(8,128)S(1)} collective-permute-done((f32[4,25,8,128]{3,2,1,0:T(8,128)S(1)}, f32[4,25,8,128]{3,2,1,0:T(8,128)S(1)}, u32[]{:S(2)}, u32[]{:S(2)}) %collective-permute-start.5) | collective-permute-done | bytes 409632 | tf_op jit(solution)/shard_map/ppermute | solution.py:495
  48.4 0.0 collective-permute-done.4.inner.inner1
  48.4 2.8 %down1.1 = (f32[14,16,128]{2,1,0:T(8,128)S(1)}, f32[14,16,128]{2,1,0:T(8,128)S(1)}, f32[24,16,128]{2,1,0:T(8,128)S(1)}, f32[8,128]{1,0:T(8,128)S(1)}) custom-call(f32[4,25,8,128]{3,2,1,0:T(8,128)S(1)} %all_to_all.10.own.own1, f32[4,25,8,128]{3,2,1,0:T(8,128)S(1)} %collective-permute-done.4.inner.inner1, f32[4,25,8,128]{3,2,1,0:T(8,128)S(1)} %collective-permute-done.5.outer.outer1), custom_call_target="tpu_custom_call" | custom-call | tf_op jit(solution)/shard_map/down1/pallas_call | solution.py:477
  51.2 3.5 %collective-permute-start.7 = (f32[14,16,128]{2,1,0:T(8,128)S(1)}, f32[14,16,128]{2,1,0:T(8,128)S(1)}, u32[]{:S(2)}, u32[]{:S(2)}) collective-permute-start(f32[14,16,128]{2,1,0:T(8,128)S(1)} %get-tuple-element.13), channel_id=1, source_target_pairs={{0,8},{4,12},{8,16},{12,20},{16,24},{20,28},{24,32},{28,36},{32,40... | collective-permute-start | bytes 344072 | tf_op jit(solution)/shard_map/ppermute | solution.py:490
  54.8 7.0 %collective-permute-start.6 = (f32[14,16,128]{2,1,0:T(8,128)S(1)}, f32[14,16,128]{2,1,0:T(8,128)S(1)}, u32[]{:S(2)}, u32[]{:S(2)}) collective-permute-start(f32[14,16,128]{2,1,0:T(8,128)S(1)} %get-tuple-element.13), channel_id=1, source_target_pairs={{0,16},{4,20},{8,24},{12,28},{16,32},{20,36},{24,40},{28,44},{32,4... | collective-permute-start | bytes 344072 | tf_op jit(solution)/shard_map/ppermute | solution.py:490
  61.8 1.3 %collective-permute-start.9 = (f32[14,16,128]{2,1,0:T(8,128)S(1)}, f32[14,16,128]{2,1,0:T(8,128)S(1)}, u32[]{:S(2)}, u32[]{:S(2)}) collective-permute-start(f32[14,16,128]{2,1,0:T(8,128)S(1)} %get-tuple-element.15), channel_id=1, source_target_pairs={{16,0},{20,4},{24,8},{28,12},{32,16},{36,20},{40,24},{44,28},{48,3... | collective-permute-start | bytes 344072 | tf_op jit(solution)/shard_map/ppermute | solution.py:490
  63.1 1.3 %collective-permute-start.8 = (f32[14,16,128]{2,1,0:T(8,128)S(1)}, f32[14,16,128]{2,1,0:T(8,128)S(1)}, u32[]{:S(2)}, u32[]{:S(2)}) collective-permute-start(f32[14,16,128]{2,1,0:T(8,128)S(1)} %get-tuple-element.15), channel_id=1, source_target_pairs={{8,0},{12,4},{16,8},{20,12},{24,16},{28,20},{32,24},{36,28},{40,32... | collective-permute-start | bytes 344072 | tf_op jit(solution)/shard_map/ppermute | solution.py:490
  64.5 0.4 collective-permute-done.6.dn4
  64.8 4.4 %collective-permute-done.9.up4 = f32[14,16,128]{2,1,0:T(8,128)S(1)} collective-permute-done((f32[14,16,128]{2,1,0:T(8,128)S(1)}, f32[14,16,128]{2,1,0:T(8,128)S(1)}, u32[]{:S(2)}, u32[]{:S(2)}) %collective-permute-start.9) | collective-permute-done | bytes 114720 | tf_op jit(solution)/shard_map/ppermute | solution.py:490
  69.2 2.7 %collective-permute-done.8.up2 = f32[14,16,128]{2,1,0:T(8,128)S(1)} collective-permute-done((f32[14,16,128]{2,1,0:T(8,128)S(1)}, f32[14,16,128]{2,1,0:T(8,128)S(1)}, u32[]{:S(2)}, u32[]{:S(2)}) %collective-permute-start.8) | collective-permute-done | bytes 114720 | tf_op jit(solution)/shard_map/ppermute | solution.py:490
  71.9 3.5 %bottom.1 = (f32[8,16,128]{2,1,0:T(8,128)S(1)}, f32[128,1,128]{2,1,0:T(1,128)}) custom-call(f32[14,16,128]{2,1,0:T(8,128)S(1)} %collective-permute-done.6.dn4, f32[14,16,128]{2,1,0:T(8,128)S(1)} %collective-permute-done.7.dn2, f32[24,16,128]{2,1,0:T(8,128)S(1)} %get-tuple-element.14.mine, f32[14,16,128]{2,1,0:T(8,128)S(1)} %collective-permute-done.8.up2, ...), custom_call_target="tpu_custom_call" | custom-call | tf_op jit(solution)/shard_map/bottom/pallas_call | solution.py:477
  75.4 0.6 copy-done
  76.0 17.4 %all-to-all-start.1 = ((f32[128,1,128]{2,1,0:T(1,128)}), f32[128,1,128]{2,1,0:T(1,128)}, u32[]{:S(2)}, u32[]{:S(2)}) async-start(f32[128,1,128]{2,1,0:T(1,128)} %get-tuple-element.17), calls=%async_computation.1 | async-start | bytes 131072 | tf_op jit(solution)/shard_map/all_to_all | solution.py:547
  93.5 0.8 copy-done.1
  94.3 7.1 %up.1 = (f32[16,16,256]{2,1,0:T(8,128)S(1)}, f32[16,16,256]{2,1,0:T(8,128)S(1)}) custom-call(f32[8,16,128]{2,1,0:T(8,128)S(1)} %copy-done.1, f32[4,25,8,128]{3,2,1,0:T(8,128)S(1)} %all_to_all.10.own.own1, f32[4,25,8,128]{3,2,1,0:T(8,128)S(1)} %collective-permute-done.4.inner.inner1, f32[4,25,8,128]{3,2,1,0:T(8,128)S(1)} %collective-permute-done.5.outer.outer1, ...), custom_call_target="tpu_custom_call" | custom-call | tf_op jit(solution)/shard_map/up/pallas_call | solution.py:477
  101.4 6.5 %all-to-all-done.1.every = f32[128,1,128]{2,1,0:T(1,128)} async-done(((f32[128,1,128]{2,1,0:T(1,128)}), f32[128,1,128]{2,1,0:T(1,128)}, u32[]{:S(2)}, u32[]{:S(2)}) %all-to-all-start.1) | async-done | bytes 65568 | tf_op jit(solution)/shard_map/all_to_all | solution.py:547
  107.9 1.8 %final.1 = f32[16,16,256]{2,1,0:T(8,128)} custom-call(f32[128,1,128]{2,1,0:T(1,128)} %all-to-all-done.1.every, f32[16,16,256]{2,1,0:T(8,128)S(1)} %get-tuple-element.19.out_s, f32[16,16,256]{2,1,0:T(8,128)S(1)} %get-tuple-element.20.out_c), custom_call_target="tpu_custom_call" | custom-call | tf_op jit(solution)/shard_map/final/pallas_call | solution.py:477
  (9 shorter events, 0.0 us)
Async XLA Ops:
  0.0 11.7 %copy-start.2 = (f32[16,16,256]{2,1,0:T(8,128)S(1)}, f32[16,16,256]{2,1,0:T(8,128)}, u32[]{:S(2)}) copy-start(f32[16,16,256]{2,1,0:T(8,128)} %param.5) | copy-start | bytes 786436
  0.0 11.7 %copy-start.3 = (f32[16,16,256]{2,1,0:T(8,128)S(1)}, f32[16,16,256]{2,1,0:T(8,128)}, u32[]{:S(2)}) copy-start(f32[16,16,256]{2,1,0:T(8,128)} %param.4) | copy-start | bytes 786436
  0.0 11.7 %copy-start.4 = (f32[16,16,256]{2,1,0:T(8,128)S(1)}, f32[16,16,256]{2,1,0:T(8,128)}, u32[]{:S(2)}) copy-start(f32[16,16,256]{2,1,0:T(8,128)} %param.3) | copy-start | bytes 786436
  1.4 6.5 %collective-permute-start = (f32[3,16,4,256]{3,2,1,0:T(4,128)S(1)}, f32[3,16,4,256]{3,2,1,0:T(4,128)S(1)}, u32[]{:S(2)}, u32[]{:S(2)}) collective-permute-start(f32[3,16,4,256]{3,2,1,0:T(4,128)S(1)} %get-tuple-element.23), channel_id=1, source_target_pairs={{0,1},{1,2},{2,3},{4,5},{5,6},{6,7},{8,9},{9,10},{10,11},{12,13},{... | collective-permute-start | bytes 589832 | tf_op jit(solution)/shard_map/ppermute | solution.py:490
  5.3 6.4 %collective-permute-start.1 = (f32[3,16,4,256]{3,2,1,0:T(4,128)S(1)}, f32[3,16,4,256]{3,2,1,0:T(4,128)S(1)}, u32[]{:S(2)}, u32[]{:S(2)}) collective-permute-start(f32[3,16,4,256]{3,2,1,0:T(4,128)S(1)} %get-tuple-element.24), channel_id=1, source_target_pairs={{1,0},{2,1},{3,2},{5,4},{6,5},{7,6},{9,8},{10,9},{11,10},{13,12},{... | collective-permute-start | bytes 589832 | tf_op jit(solution)/shard_map/ppermute | solution.py:490
  12.0 10.6 %collective-permute-start.3 = (f32[3,4,24,256]{3,2,1,0:T(8,128)S(1)}, f32[3,4,24,256]{3,2,1,0:T(8,128)S(1)}, u32[]{:S(2)}, u32[]{:S(2)}) collective-permute-start(f32[3,4,24,256]{3,2,1,0:T(8,128)S(1)} %get-tuple-element.21), channel_id=1, source_target_pairs={{4,8},{12,16},{20,24},{28,32},{36,40},{44,48},{52,56},{60,64},{68,... | collective-permute-start | bytes 884744 | tf_op jit(solution)/shard_map/ppermute | solution.py:495
  18.2 4.4 %collective-permute-start.2 = (f32[3,4,24,256]{3,2,1,0:T(8,128)S(1)}, f32[3,4,24,256]{3,2,1,0:T(8,128)S(1)}, u32[]{:S(2)}, u32[]{:S(2)}) collective-permute-start(f32[3,4,24,256]{3,2,1,0:T(8,128)S(1)} %get-tuple-element.22), channel_id=1, source_target_pairs={{0,4},{8,12},{16,20},{24,28},{32,36},{40,44},{48,52},{56,60},{64,6... | collective-permute-start | bytes 884744 | tf_op jit(solution)/shard_map/ppermute | solution.py:495
  38.9 9.5 %collective-permute-start.5 = (f32[4,25,8,128]{3,2,1,0:T(8,128)S(1)}, f32[4,25,8,128]{3,2,1,0:T(8,128)S(1)}, u32[]{:S(2)}, u32[]{:S(2)}) collective-permute-start(f32[4,25,8,128]{3,2,1,0:T(8,128)S(1)} %all_to_all.10.own.own1), channel_id=1, source_target_pairs={{4,8},{12,16},{20,24},{28,32},{36,40},{44,48},{52,56},{60,64},{68,... | collective-permute-start | bytes 1228808 | tf_op jit(solution)/shard_map/ppermute | solution.py:495
  42.8 5.6 %collective-permute-start.4 = (f32[4,25,8,128]{3,2,1,0:T(8,128)S(1)}, f32[4,25,8,128]{3,2,1,0:T(8,128)S(1)}, u32[]{:S(2)}, u32[]{:S(2)}) collective-permute-start(f32[4,25,8,128]{3,2,1,0:T(8,128)S(1)} %all_to_all.10.own.own1), channel_id=1, source_target_pairs={{0,4},{8,12},{16,20},{24,28},{32,36},{40,44},{48,52},{56,60},{64,6... | collective-permute-start | bytes 1228808 | tf_op jit(solution)/shard_map/ppermute | solution.py:495
  51.2 13.2 %collective-permute-start.7 = (f32[14,16,128]{2,1,0:T(8,128)S(1)}, f32[14,16,128]{2,1,0:T(8,128)S(1)}, u32[]{:S(2)}, u32[]{:S(2)}) collective-permute-start(f32[14,16,128]{2,1,0:T(8,128)S(1)} %get-tuple-element.13), channel_id=1, source_target_pairs={{0,8},{4,12},{8,16},{12,20},{16,24},{20,28},{24,32},{28,36},{32,40... | collective-permute-start | bytes 344072 | tf_op jit(solution)/shard_map/ppermute | solution.py:490
  54.8 10.0 %collective-permute-start.6 = (f32[14,16,128]{2,1,0:T(8,128)S(1)}, f32[14,16,128]{2,1,0:T(8,128)S(1)}, u32[]{:S(2)}, u32[]{:S(2)}) collective-permute-start(f32[14,16,128]{2,1,0:T(8,128)S(1)} %get-tuple-element.13), channel_id=1, source_target_pairs={{0,16},{4,20},{8,24},{12,28},{16,32},{20,36},{24,40},{28,44},{32,4... | collective-permute-start | bytes 344072 | tf_op jit(solution)/shard_map/ppermute | solution.py:490
  61.8 7.4 %collective-permute-start.9 = (f32[14,16,128]{2,1,0:T(8,128)S(1)}, f32[14,16,128]{2,1,0:T(8,128)S(1)}, u32[]{:S(2)}, u32[]{:S(2)}) collective-permute-start(f32[14,16,128]{2,1,0:T(8,128)S(1)} %get-tuple-element.15), channel_id=1, source_target_pairs={{16,0},{20,4},{24,8},{28,12},{32,16},{36,20},{40,24},{44,28},{48,3... | collective-permute-start | bytes 344072 | tf_op jit(solution)/shard_map/ppermute | solution.py:490
  63.1 8.8 %collective-permute-start.8 = (f32[14,16,128]{2,1,0:T(8,128)S(1)}, f32[14,16,128]{2,1,0:T(8,128)S(1)}, u32[]{:S(2)}, u32[]{:S(2)}) collective-permute-start(f32[14,16,128]{2,1,0:T(8,128)S(1)} %get-tuple-element.15), channel_id=1, source_target_pairs={{8,0},{12,4},{16,8},{20,12},{24,16},{28,20},{32,24},{36,28},{40,32... | collective-permute-start | bytes 344072 | tf_op jit(solution)/shard_map/ppermute | solution.py:490
  75.4 0.6 copy-start
  76.0 31.9 %all-to-all-start.1 = ((f32[128,1,128]{2,1,0:T(1,128)}), f32[128,1,128]{2,1,0:T(1,128)}, u32[]{:S(2)}, u32[]{:S(2)}) async-start(f32[128,1,128]{2,1,0:T(1,128)} %get-tuple-element.17), calls=%async_computation.1 | async-start | bytes 131072 | tf_op jit(solution)/shard_map/all_to_all | solution.py:547
  93.4 0.8 copy-start.1

commit v4 on v3

--- a/solution.py
+++ b/solution.py
@@ -10,6 +10,7 @@
 f32 = jnp.float32
 HALO = 4
 LIMIT = 24
+ROOM = 6144
 C0, S0, W0, R0 = 22, 22, 20, 16
 C1, S1, W1, R1 = 26, 26, 24, 8
 C2, S2, W2, R2 = 42, 40, 38, 36
@@ -252,95 +253,109 @@
 
 
 def down1(
-    own, inner, outer, to_up, to_down, mine, sums,
+    own, inner, outer, piece, mine,
     vs, vc, cx, cy, cz, dg, wt, ss, cc, m, us, uc, pair, thin, parts, sems,
 ):
     copies = fetch1(own, inner, outer, ((2, m), (0, ss), (1, cc)), sems)
     partial = fetch([own.at[j, 24] for j in range(4)], [parts.at[j] for j in range(4)], sems.at[pl.ds(36, 4)])
-    for ref in (ss, cc, m, vs, vc):
-        ref[0:2] = jnp.zeros((2, 32, 128), f32)
-        ref[26:28] = jnp.zeros((2, 32, 128), f32)
     wait(copies[:12])
-    coefficients(1, m, cx, cy, cz, dg, wt, 1, 27, C1, 32, 128)
+    coefficients(1, m, cx, cy, cz, dg, wt, 3, 25, C1, 32, 128)
     coefs = (cx, cy, cz, dg)
     wait(copies[12:])
     wait(partial)
-    start(1, 27, S1, (ss, cc), (us, uc), wt)
-    sweep(2, 26, W1, (ss, cc), (us, uc), (vs, vc), coefs, wt)
+    start(3, 25, S1, (ss, cc), (us, uc), wt)
+    sweep(4, 24, W1, (ss, cc), (us, uc), (vs, vc), coefs, wt)
 
     def rest(i, n, sums):
         res_s, res_c, sums = products(i, n, ss, cc, vs, vc, coefs, sums)
-        k = lax.div(i - 2, 2)
+        k = (i - 6) // 2
         pair[at(k, n // 2), :, 0:128] = pairs(res_s)
         pair[at(k, n // 2), :, 128:256] = pairs(res_c)
-        both = pairs(m[at(i, n)])
-        pair[at(k + 12, n // 2), :, 0:128] = both
-        pair[at(k + 12, n // 2), :, 128:256] = both
         return sums
 
     zero = jnp.zeros((32, 128), f32)
-    by_rows(2, 10, R1, rest, (zero, zero))
-    num, den = by_rows(10, 18, R1, rest, (zero, zero))
-    by_rows(18, 26, R1, rest, (zero, zero))
+    rest(6, 4, (zero, zero))
+    num, den = rest(10, 8, (zero, zero))
+    rest(18, 4, (zero, zero))
+    both = pairs(m[2:26])
+    pair[8:20, :, 0:128] = both
+    pair[8:20, :, 128:256] = both
     thin[...] = flat_dot(pair[...], coarse_z(128, 256, 64, 128, 2))
-    place = lax.axis_index("wide")
-    low = jnp.where(place == 1, fold_y(thin, 0, 2, 0, 16), 0.0)
-    mid = fold_y(thin, 2, 8, 0, 16)
-    high = jnp.where(place == lax.axis_size("wide") - 2, fold_y(thin, 10, 2, 0, 16), 0.0)
-    mob = fold_y(thin, 12, 12, 0, 16)
-    mine[0:2] = low
-    mine[2:10] = mid
-    mine[10:12] = high
-    mine[12:24] = mob
-    to_up[0:2] = low
-    to_up[2:10] = mid
-    to_down[0:8] = mid
-    to_down[8:10] = high
+    mid = fold_y(thin, 0, 8, 0, 16)
+    mob = fold_y(thin, 8, 12, 0, 16)
+    even = lax.rem(lax.axis_index("wide"), 2) == 0
+    mine[0:8] = mid
+    mine[8:20] = mob
+    piece[0:8] = mid
     left = iota((4, 16, 128), 2) < 64
-    to_up[10:14] = jnp.where(left, mob[0:4], mob[4:8])
-    to_down[10:14] = jnp.where(left, mob[4:8], mob[8:12])
+    piece[8:12] = jnp.where(
+        left, jnp.where(even, mob[0:4], mob[4:8]), jnp.where(even, mob[4:8], mob[8:12])
+    )
     lane = iota((8, 128), 1)
     num = jnp.sum(num) * 8.0
     den = jnp.sum(den) * 8.0
     finer = parts[0] + parts[1] + parts[2] + parts[3]
-    sums[...] = finer + jnp.where(lane == 0, num, jnp.where(lane == 1, den, 0.0))
+    total = finer + jnp.where(lane == 0, num, jnp.where(lane == 1, den, 0.0))
+    for ref, row in ((piece, 12), (mine, 20)):
+        ref[row] = jnp.concatenate([total, total], axis=0)
 
 
 def bottom(
-    dn4, dn2, mine, up2, up4, finer, e2, sums,
+    mine, near, far, pair_own, pair_near, pair_far, e2_out, sums,
     m2, r2, u2, v2, cx2, cy2, cz2, dg2, wt2,
     m3, r3, u3, v3, cx3, cy3, cz3, dg3, wt3,
     m4, r4, u4, v4, cx4, cy4, cz4, dg4, wt4,
-    pair2, thin2, pair3, thin3, wide3, wide2,
+    pair2, thin2, pair3, thin3, wide3, wide2, e2, sems,
 ):
     left = iota((4, 16, 128), 2) < 64
-
-    def unpack(ref, first, r_at, m_at):
-        r2[r_at : r_at + 8] = ref[first : first + 8]
-        packed = ref[10:14]
+    place = lax.axis_index("wide")
+    size = lax.axis_size("wide")
+
+    even = lax.rem(place, 2) == 0
+
+    def choose(a, b):
+        return jnp.where(even, a, b)
+
+    def held(distance, value):
+        return jnp.where((place + distance >= 0) & (place + distance < size), value, 0.0)
+
+    def unpack(ref, distance):
+        packed = held(distance, ref[8:12])
         other = pltpu.roll(packed, 64, 2)
-        m2[m_at : m_at + 4] = jnp.where(left, packed, other)
-        m2[m_at + 4 : m_at + 8] = jnp.where(left, other, packed)
-
-    unpack(dn4, 2, 2, 0)
-    unpack(dn2, 2, 10, 8)
-    unpack(up2, 0, 26, 28)
-    unpack(up4, 0, 34, 36)
-    r2[18:26] = mine[2:10]
-    m2[16:28] = mine[12:24]
-    r2[8:10] = r2[8:10] + dn2[0:2]
-    r2[16:18] = r2[16:18] + mine[0:2]
-    r2[26:28] = r2[26:28] + mine[10:12]
-    r2[34:36] = r2[34:36] + up2[8:10]
-
-    def both_products(r, v, res, z_len):
+        return held(distance, ref[0:8]), jnp.where(left, packed, other), jnp.where(left, other, packed)
+
+    r2[18:26] = mine[0:8]
+    m2[16:28] = mine[8:20]
+    for ref, distance, r_at, m_at in (
+        (near, choose(-2, 2), choose(10, 26), choose(8, 28)),
+        (far, choose(-4, 4), choose(2, 34), choose(0, 36)),
+        (pair_near, choose(3, -3), choose(30, 6), choose(32, 4)),
+    ):
+        cells, m_low, m_high = unpack(ref, distance)
+        r2[pl.ds(r_at, 8)] = cells
+        m2[pl.ds(m_at, 4)] = m_low
+        m2[pl.ds(m_at + 4, 4)] = m_high
+    cells, m_low, m_high = unpack(pair_own, 0)
+    r2[pl.ds(choose(26, 14), 4)] = choose(cells[4:8], cells[0:4])
+    m2[pl.ds(choose(28, 12), 4)] = choose(m_high, m_low)
+    cells, m_low, m_high = unpack(pair_far, choose(5, -5))
+    r2[pl.ds(choose(38, 2), 4)] = choose(cells[0:4], cells[4:8])
+    m2[pl.ds(choose(40, 0), 4)] = choose(m_low, m_high)
+
+    lo = jnp.where(even, jnp.where(place == 2, -2, 0), jnp.where(place == 3, -3, -2))
+    hi = jnp.where(place == size - 4, 3, 2)
+
+    def both_products(r, v, res, z_len, rows):
         num = v * pltpu.roll(r, 128 - z_len, 2)
         den = v * r
         if res is not None:
             num = num + res * pltpu.roll(v, 128 - z_len, 2)
             den = den + res * v
-        mask = iota(v.shape, 2) < z_len
-        return jnp.sum(jnp.where(mask, num, 0.0)), jnp.sum(jnp.where(mask, den, 0.0))
+        device = lax.div(iota(v.shape, 0), rows) - 3
+        mask = (iota(v.shape, 2) < z_len) & (device >= lo) & (device <= hi)
+        num = jnp.sum(jnp.where(mask, num, 0.0), axis=0)
+        den = jnp.sum(jnp.where(mask, den, 0.0), axis=0)
+        return num, den
 
     c2 = (cx2, cy2, cz2, dg2)
     c3 = (cx3, cy3, cz3, dg3)
@@ -349,14 +364,10 @@
     start(2, 42, S2, (r2,), (u2,), wt2)
     sweep(3, 41, W2, (r2,), (u2,), (v2,), c2, wt2)
 
-    def rest2(i, n, sums):
-        res = residual(i, n, r2[at(i, n)], v2, *c2)
-        pair2[at(lax.div(i - 4, 2), n // 2)] = pairs(res)
-        return sums
-
-    by_rows(4, 40, R2, rest2, 0)
-    own = slice(20, 24)
-    num2, den2 = both_products(r2[own], v2[own], residual(20, 4, r2[own], v2, *c2), 64)
+    res = residual(4, 36, r2[4:40], v2, *c2)
+    pair2[0:18] = pairs(res)
+    kept = slice(8, 36)
+    num2, den2 = both_products(r2[kept], v2[kept], res[4:32], 64, 4)
     pair2[18:40] = pairs(m2[...])
     thin2[...] = flat_dot(pair2[...], coarse_z(64, 128, 32, 128, 2))
     r3[2:20] = fold_y(thin2, 0, 18, 0, 8)
@@ -366,7 +377,8 @@
     start(2, 20, 18, (r3,), (u3,), wt3)
     sweep(3, 19, 16, (r3,), (u3,), (v3,), c3, wt3)
     res = residual(4, 14, r3[4:18], v3, *c3)
-    num3, den3 = both_products(r3[10:12], v3[10:12], res[6:8], 32)
+    kept = slice(4, 18)
+    num3, den3 = both_products(r3[kept], v3[kept], res, 32, 2)
     pair3[0:7] = pairs(res)
     pair3[7:18] = pairs(m3[...])
     thin3[...] = flat_dot(pair3[...], coarse_z(32, 128, 16, 128, 2))
@@ -376,15 +388,10 @@
     m4[:, 0:4, :] = fold_y(thin3, 7, 11, 0, 4)
 
     coefficients(4, m4, *c4, wt4, 1, 10, 9, 4, 16)
+    u4[1] = jnp.zeros((8, 128), f32)
+    u4[9] = jnp.zeros((8, 128), f32)
     start(2, 9, 7, (r4,), (u4,), wt4)
-    sweep(3, 8, 5, (r4,), (u4,), (v4,), c4, wt4)
-    num4, den4 = both_products(r4[5:6], v4[5:6], None, 16)
-    num = 64.0 * num2 + 512.0 * num3 + 4096.0 * num4
-    den = 64.0 * den2 + 512.0 * den3 + 4096.0 * den4
-    lane = iota((8, 128), 1)
-    total = finer[...] + jnp.where(lane == 0, num, jnp.where(lane == 1, den, 0.0))
-    sums[...] = jnp.broadcast_to(total[0:1].reshape(1, 1, 128), sums.shape)
-
+    sweep(2, 9, 7, (r4,), (u4,), (v4,), c4, wt4)
     wide3[:, pl.ds(0, 4, stride=2), :] = v4[3:8, 0:4, :]
     wide3[:, pl.ds(1, 4, stride=2), :] = v4[3:8, 0:4, :]
     v3[6:16] = v3[6:16] + doubled(flat_dot(wide3[...], fine_z(16, 128, 32, 128, 2)))
@@ -395,16 +402,27 @@
     v2[16:28] = v2[16:28] + doubled(flat_dot(wide2[...], fine_z(32, 128, 64, 128, 2)))
     sweep(17, 27, 10, (r2,), (v2,), (u2,), c2, wt2)
     e2[...] = relaxed(18, 8, r2, u2, wt2, *c2)
+    copies = fetch([e2], [e2_out.at[pl.ds(0, 8)]], sems)
+    kept = slice(2, 9)
+    num4, den4 = both_products(r4[kept], v4[kept], None, 16, 1)
+    num = 64.0 * jnp.sum(num2) + 512.0 * jnp.sum(num3) + 4096.0 * jnp.sum(num4)
+    den = 64.0 * jnp.sum(den2) + 512.0 * jnp.sum(den3) + 4096.0 * jnp.sum(den4)
+    lane = iota((8, 128), 1)
+    finer = mine[20, 0:8] + near[12, 0:8] + pair_own[12, 0:8] + pair_near[12, 0:8]
+    total = finer + jnp.where(lane == 0, num, jnp.where(lane == 1, den, 0.0))
+    sums[...] = jnp.broadcast_to(total[0:1].reshape(1, 1, 128), sums.shape)
+    wait(copies)
 
 
 def up(
-    e2, own1, inner1, outer1, own0, inner0, outer0, out_s, out_c,
+    e2_in, own1, inner1, outer1, own0, inner0, outer0, out_s, out_c,
     vs1, vc1, cx1, cy1, cz1, wt1, ss1, cc1, m1, as1, ac1, bs1, bc1,
     vs0, vc0, cx0, cy0, cz0, wt0, ss0, cc0, m0, as0, ac0, bs0, bc0,
-    wide, add, block, thick, full, sems,
+    wide, add, block, thick, full, e2, sems,
 ):
     copies1 = fetch1(own1, inner1, outer1, ((2, m1), (0, ss1), (1, cc1)), sems)
     copies0 = fetch0(own0, inner0, outer0, (m0, ss0, cc0), sems.at[pl.ds(36, 9)])
+    copies2 = fetch([e2_in.at[pl.ds(0, 8)]], [e2], sems.at[pl.ds(45, 1)])
     c1 = (cx1, cy1, cz1)
     c0 = (cx0, cy0, cz0)
     wait(copies1)
@@ -415,6 +433,7 @@
     coefficients(0, m0, cx0, cy0, cz0, None, wt0, 1, 23, C0, None, 256)
     start(1, 23, S0, (ss0, cc0), (as0, ac0), wt0)
     sweep(2, 22, W0, (ss0, cc0), (as0, ac0), (vs0, vc0), c0, wt0)
+    wait(copies2)
     wide[:, pl.ds(0, 16, stride=2), :] = e2[...]
     wide[:, pl.ds(1, 16, stride=2), :] = e2[...]
     add[...] = flat_dot(wide[...], fine_z(64, 128, 128, 256, 2))
@@ -461,16 +480,21 @@
     by_rows(4, 20, W0, last0, 0)
 
 
-def final(every, out_s, out_c, out):
+def final(every, out_s, out_c, out, held, sems):
     total = jnp.sum(every[...], axis=0)
     lane = iota((1, 128), 1)
     num = jnp.sum(jnp.where(lane == 0, total, 0.0), axis=1, keepdims=True)
     den = jnp.sum(jnp.where(lane == 1, total, 0.0), axis=1, keepdims=True)
     ratio = (num / (1.0 + den))[0, 0]
-    out[...] = out_c[...] - ratio * out_s[...]
-
-
-def call(kernel, ins, outs, scratch, name, sems=0, specs=None):
+    copies = []
+    for k in range(4):
+        rows = pl.ds(4 * k, 4)
+        held[rows] = out_c[rows] - ratio * out_s[rows]
+        copies += fetch([held.at[rows]], [out.at[rows]], sems.at[pl.ds(k, 1)])
+    wait(copies)
+
+
+def call(kernel, ins, outs, scratch, name, sems=0, specs=None, out_specs=None):
     scratch = [pltpu.VMEM(s, f32) for s in scratch]
     if sems:
         scratch.append(pltpu.SemaphoreType.DMA((sems,)))
@@ -478,7 +502,7 @@
         kernel,
         out_shape=[jax.ShapeDtypeStruct(s, f32) for s in outs],
         in_specs=specs or [VMEM] * len(ins),
-        out_specs=[VMEM] * len(outs),
+        out_specs=out_specs or [VMEM] * len(outs),
         scratch_shapes=scratch,
         compiler_params=pltpu.CompilerParams(vmem_limit_bytes=LIMIT * 2**20),
         name=name,
@@ -488,6 +512,11 @@
 def shifted(value, axis, by):
     size = lax.axis_size(axis)
     return lax.ppermute(value, axis, [(i, i + by) for i in range(size) if 0 <= i + by < size])
+
+
+def apart(value, by):
+    size = lax.axis_size("wide")
+    return lax.ppermute(value, "wide", [(i, (i + by * (1 - 2 * (i % 2))) % size) for i in range(size)])
 
 
 def swapped(value, first):
@@ -518,45 +547,50 @@
     outer = swapped(gathered, 1)
     inner = swapped(gathered, 0)
     a1 = (28, 32, 128)
-    to_up, to_down, mine, finer = call(
+    piece, mine = call(
         down1,
         (gathered, inner, outer),
-        [(14, 16, 128), (14, 16, 128), (24, 16, 128), (8, 128)],
-        [a1] * 12 + [(24, 32, 256), (24, 32, 128), (4, 8, 128)],
+        [(13, 16, 128), (21, 16, 128)],
+        [a1] * 12 + [(20, 32, 256), (20, 32, 128), (4, 8, 128)],
         "down1",
         40,
         [HBM] * 3,
     )
-    dn2 = shifted(to_up, "wide", 2)
-    up2 = shifted(to_down, "wide", -2)
-    dn4 = shifted(to_up, "wide", 4)
-    up4 = shifted(to_down, "wide", -4)
+    near = apart(piece, 2)
+    far = apart(piece, 4)
+    pair_own = swapped(piece, 0)
+    pair_near = swapped(near, 0)
+    pair_far = swapped(far, 0)
     wide = lax.axis_size("wide")
     e2, sums = call(
         bottom,
-        (dn4, dn2, mine, up2, up4, finer),
-        [(8, 16, 128), (wide, 1, 128)],
+        (mine, near, far, pair_own, pair_near, pair_far),
+        [(ROOM, 16, 128), (wide // 4, 1, 128)],
         [(44, 16, 128)] * 9
         + [(22, 8, 128)] * 9
         + [(11, 8, 128)] * 9
         + [(40, 16, 128)] * 2
         + [(18, 8, 128)] * 2
-        + [(5, 8, 128), (6, 16, 128)],
+        + [(5, 8, 128), (6, 16, 128), (8, 16, 128)],
         "bottom",
+        1,
+        None,
+        [HBM, VMEM],
     )
-    every = lax.all_to_all(sums, "wide", 0, 0)
+    groups = [[i for i in range(wide) if (i // 2 + 2 * (i % 2)) % 4 == s] for s in range(4)]
+    every = lax.all_to_all(sums, "wide", 0, 0, axis_index_groups=groups)
     out_s, out_c = call(
         up,
         (e2, gathered, inner, outer, own, x_inner, x_outer),
         [(16, 16, 256)] * 2,
         [a1] * 13
         + [a0] * 13
-        + [(8, 32, 128), (8, 32, 256), (20, 48, 128), (20, 24, 128), (20, 24, 256)],
+        + [(8, 32, 128), (8, 32, 256), (20, 48, 128), (20, 24, 128), (20, 24, 256), (8, 16, 128)],
         "up",
-        45,
-        [VMEM] + [HBM] * 6,
+        46,
+        [HBM] * 7,
     )
-    return call(final, (every, out_s, out_c), [(16, 16, 256)], [], "final")[0]
+    return call(final, (every, out_s, out_c), [(16, 16, 256)], [(16, 16, 256)], "final", 4, None, [HBM])[0]
 
 
 def solution(mesh):

time: 110 us -> 103 us (0.936)
  waiting for transfers between devices: 25.3 us -> 18.3 us
  local copies, waits for them, and re-layouts: 1.51 us -> 0.06 us
  starting transfers between devices: 49.8 us -> 51.1 us
    ppermute x0 -> x2, starting transfers between devices: none -> 15.4 us  [apart(): lax.ppermute(value, 'wide', [(i, (i + by * (1 - 2 * (i % 2))) % size) for...]
    ppermute x6 -> x2, starting transfers between devices: 18.4 us -> 5.25 us  [shifted(): lax.ppermute(value, axis, [(i, i + by) for i in range(size) if 0 <= i + b...]
    ppermute x6 -> x2, waiting for transfers between devices: 12.6 us -> 5.1 us  [shifted(): lax.ppermute(value, axis, [(i, i + by) for i in range(size) if 0 <= i + b...]
    all_to_all x1, starting transfers between devices: 17.4 us -> 10.2 us  [per_device(): every = lax.all_to_all(sums, 'wide', 0, 0, axis_index_groups=groups)]
    ppermute x4 -> x7, starting transfers between devices: 14 us -> 20.2 us  [swapped(): return lax.ppermute(value, 'wide', pairs + [(b, a) for a, b in pairs])]
    unnamed x10 -> x6, local copies, waits for them, and re-layouts: 1.46 us -> 0.01 us
    ppermute x4 -> x7, waiting for transfers between devices: 6.16 us -> 7.42 us  [swapped(): return lax.ppermute(value, 'wide', pairs + [(b, a) for a, b in pairs])]
  transfers between devices with their start and end apart: 11 -> 12, of which waited for: 8 -> 6; matrix products, arithmetic and copies ran while one was open for 0% -> 0% of each run, Pallas kernels for 6% -> 7%
where the time goes in v4:
time: 103 us
  starting transfers between devices  51.1 us (50%)
  Pallas kernels  18.9 us (18%)
  waiting for transfers between devices  18.3 us (18%)
  blocking collectives  12.2 us (12%)
  other arithmetic  1.52 us (1%)
    ppermute x7, starting transfers between devices, swapped(): return lax.ppermute(value, 'wide', pairs + [(b, a) for a, b in pairs])  20.2 us
    pallas_call x5, Pallas kernels, call(): pl.pallas_call(kernel, out_shape=[jax.ShapeDtypeStruct(s, f32) for s in o...  18.9 us
    ppermute x2, starting transfers between devices, apart(): lax.ppermute(value, 'wide', [(i, (i + by * (1 - 2 * (i % 2))) % size) for...  15.4 us
    all_to_all x1, blocking collectives, per_device(): gathered = lax.all_to_all(chunk, 'narrow', 0, 0)  12.2 us
    all_to_all x1, starting transfers between devices, per_device(): every = lax.all_to_all(sums, 'wide', 0, 0, axis_index_groups=groups)  10.2 us
    ppermute x7, waiting for transfers between devices, swapped(): return lax.ppermute(value, 'wide', pairs + [(b, a) for a, b in pairs])  7.42 us
    all_to_all x1, waiting for transfers between devices, per_device(): every = lax.all_to_all(sums, 'wide', 0, 0, axis_index_groups=groups)  5.79 us
    ppermute x2, starting transfers between devices, shifted(): lax.ppermute(value, axis, [(i, i + by) for i in range(size) if 0 <= i + b...  5.25 us
  transfers between devices with their start and end apart: 12, of which 6 were waited for; matrix products, arithmetic and copies ran while one was open for 0% of the time, Pallas kernels for 7%

profile of v4, /device:TPU:1, one launch (start us, length us, event | category | flops | bytes accessed | tf_op | source)
XLA Modules:
  0.0 102.5 jit_solution(14219038484650023676)
XLA Ops:
  0.0 1.3 %pad_maximum_fusion.3 = (f32[3,16,4,256]{3,2,1,0:T(4,128)S(1)}, f32[3,16,4,256]{3,2,1,0:T(4,128)S(1)}) fusion(f32[1,16,16,256]{3,2,1,0:T(8,128)} %bitcast.3, f32[1,16,16,256]{3,2,1,0:T(8,128)} %bitcast.5, f32[1,16,16,256]{3,2,1,0:T(8,128)} %bitcast.7), kind=kLoop, calls=%fused_computation.3 | loop fusion | flops 196608 | bytes 1179648 | tf_op jit(solution)/shard_map/slice | solution.py:529
  1.4 4.0 %collective-permute-start = (f32[3,16,4,256]{3,2,1,0:T(4,128)S(1)}, f32[3,16,4,256]{3,2,1,0:T(4,128)S(1)}, u32[]{:S(2)}, u32[]{:S(2)}) collective-permute-start(f32[3,16,4,256]{3,2,1,0:T(4,128)S(1)} %get-tuple-element.19), channel_id=1, source_target_pairs={{0,1},{1,2},{2,3},{4,5},{5,6},{6,7},{8,9},{9,10},{10,11},{12,13},{... | collective-permute-start | bytes 589832 | tf_op jit(solution)/shard_map/ppermute | solution.py:514
  5.3 1.3 %collective-permute-start.1 = (f32[3,16,4,256]{3,2,1,0:T(4,128)S(1)}, f32[3,16,4,256]{3,2,1,0:T(4,128)S(1)}, u32[]{:S(2)}, u32[]{:S(2)}) collective-permute-start(f32[3,16,4,256]{3,2,1,0:T(4,128)S(1)} %get-tuple-element.20), channel_id=1, source_target_pairs={{1,0},{2,1},{3,2},{5,4},{6,5},{7,6},{9,8},{10,9},{11,10},{13,12},{... | collective-permute-start | bytes 589832 | tf_op jit(solution)/shard_map/ppermute | solution.py:514
  6.6 1.3 %collective-permute-done = f32[3,16,4,256]{3,2,1,0:T(4,128)S(1)} collective-permute-done((f32[3,16,4,256]{3,2,1,0:T(4,128)S(1)}, f32[3,16,4,256]{3,2,1,0:T(4,128)S(1)}, u32[]{:S(2)}, u32[]{:S(2)}) %collective-permute-start) | collective-permute-done | bytes 196640 | tf_op jit(solution)/shard_map/ppermute | solution.py:514
  7.9 3.8 %collective-permute-done.1 = f32[3,16,4,256]{3,2,1,0:T(4,128)S(1)} collective-permute-done((f32[3,16,4,256]{3,2,1,0:T(4,128)S(1)}, f32[3,16,4,256]{3,2,1,0:T(4,128)S(1)}, u32[]{:S(2)}, u32[]{:S(2)}) %collective-permute-start.1) | collective-permute-done | bytes 196640 | tf_op jit(solution)/shard_map/ppermute | solution.py:514
  11.7 0.2 pad_maximum_fusion.own.own0
  11.9 0.1 constant_dynamic-slice_fusion
  12.0 6.2 %collective-permute-start.3 = (f32[3,4,24,256]{3,2,1,0:T(8,128)S(1)}, f32[3,4,24,256]{3,2,1,0:T(8,128)S(1)}, u32[]{:S(2)}, u32[]{:S(2)}) collective-permute-start(f32[3,4,24,256]{3,2,1,0:T(8,128)S(1)} %get-tuple-element.17), channel_id=1, source_target_pairs={{4,8},{12,16},{20,24},{28,32},{36,40},{44,48},{52,56},{60,64},{68,... | collective-permute-start | bytes 884744 | tf_op jit(solution)/shard_map/ppermute | solution.py:524
  18.2 1.9 %collective-permute-start.2 = (f32[3,4,24,256]{3,2,1,0:T(8,128)S(1)}, f32[3,4,24,256]{3,2,1,0:T(8,128)S(1)}, u32[]{:S(2)}, u32[]{:S(2)}) collective-permute-start(f32[3,4,24,256]{3,2,1,0:T(8,128)S(1)} %get-tuple-element.18), channel_id=1, source_target_pairs={{0,4},{8,12},{16,20},{24,28},{32,36},{40,44},{48,52},{56,60},{64,6... | collective-permute-start | bytes 884744 | tf_op jit(solution)/shard_map/ppermute | solution.py:524
  20.2 2.5 %collective-permute-done.3.outer.outer0 = f32[3,4,24,256]{3,2,1,0:T(8,128)S(1)} collective-permute-done((f32[3,4,24,256]{3,2,1,0:T(8,128)S(1)}, f32[3,4,24,256]{3,2,1,0:T(8,128)S(1)}, u32[]{:S(2)}, u32[]{:S(2)}) %collective-permute-start.3) | collective-permute-done | bytes 294944 | tf_op jit(solution)/shard_map/ppermute | solution.py:524
  22.6 0.0 collective-permute-done.2.inner.inner0
  22.6 4.0 %down0.1 = f32[4,25,8,128]{3,2,1,0:T(8,128)S(1)} custom-call(f32[3,16,24,256]{3,2,1,0:T(8,128)S(1)} %pad_maximum_fusion.own.own0, f32[3,4,24,256]{3,2,1,0:T(8,128)S(1)} %collective-permute-done.2.inner.inner0, f32[3,4,24,256]{3,2,1,0:T(8,128)S(1)} %collective-permute-done.3.outer.outer0), custom_call_target="tpu_custom_call" | custom-call | tf_op jit(solution)/shard_map/down0/pallas_call | solution.py:501
  26.6 12.2 %all_to_all.10.own.own1 = f32[4,25,8,128]{3,2,1,0:T(8,128)S(1)} all-to-all(f32[4,25,8,128]{3,2,1,0:T(8,128)S(1)} %down0.1), channel_id=1, replica_groups=mesh['wide'=128,'narrow'=4] {'narrow'}, dimensions={0} | all-to-all | bytes 819200 | tf_op jit(solution)/shard_map/all_to_all | solution.py:546
  38.9 3.9 %collective-permute-start.5 = (f32[4,25,8,128]{3,2,1,0:T(8,128)S(1)}, f32[4,25,8,128]{3,2,1,0:T(8,128)S(1)}, u32[]{:S(2)}, u32[]{:S(2)}) collective-permute-start(f32[4,25,8,128]{3,2,1,0:T(8,128)S(1)} %all_to_all.10.own.own1), channel_id=1, source_target_pairs={{4,8},{12,16},{20,24},{28,32},{36,40},{44,48},{52,56},{60,64},{68,... | collective-permute-start | bytes 1228808 | tf_op jit(solution)/shard_map/ppermute | solution.py:524
  42.8 1.9 %collective-permute-start.4 = (f32[4,25,8,128]{3,2,1,0:T(8,128)S(1)}, f32[4,25,8,128]{3,2,1,0:T(8,128)S(1)}, u32[]{:S(2)}, u32[]{:S(2)}) collective-permute-start(f32[4,25,8,128]{3,2,1,0:T(8,128)S(1)} %all_to_all.10.own.own1), channel_id=1, source_target_pairs={{0,4},{8,12},{16,20},{24,28},{32,36},{40,44},{48,52},{56,60},{64,6... | collective-permute-start | bytes 1228808 | tf_op jit(solution)/shard_map/ppermute | solution.py:524
  44.7 3.7 %collective-permute-done.5.outer.outer1 = f32[4,25,8,128]{3,2,1,0:T(8,128)S(1)} collective-permute-done((f32[4,25,8,128]{3,2,1,0:T(8,128)S(1)}, f32[4,25,8,128]{3,2,1,0:T(8,128)S(1)}, u32[]{:S(2)}, u32[]{:S(2)}) %collective-permute-start.5) | collective-permute-done | bytes 409632 | tf_op jit(solution)/shard_map/ppermute | solution.py:524
  48.4 0.0 collective-permute-done.4.inner.inner1
  48.4 2.3 %down1.1 = (f32[13,16,128]{2,1,0:T(8,128)S(1)}, f32[21,16,128]{2,1,0:T(8,128)S(1)}) custom-call(f32[4,25,8,128]{3,2,1,0:T(8,128)S(1)} %all_to_all.10.own.own1, f32[4,25,8,128]{3,2,1,0:T(8,128)S(1)} %collective-permute-done.4.inner.inner1, f32[4,25,8,128]{3,2,1,0:T(8,128)S(1)} %collective-permute-done.5.outer.outer1), custom_call_target="tpu_custom_call" | custom-call | tf_op jit(solution)/shard_map/down1/pallas_call | solution.py:501
  50.7 12.2 %collective-permute-start.7 = (f32[13,16,128]{2,1,0:T(8,128)S(1)}, f32[13,16,128]{2,1,0:T(8,128)S(1)}, u32[]{:S(2)}, u32[]{:S(2)}) collective-permute-start(f32[13,16,128]{2,1,0:T(8,128)S(1)} %get-tuple-element.12), channel_id=1, source_target_pairs={{0,16},{4,500},{8,24},{12,508},{16,32},{20,4},{24,40},{28,12},{32,... | collective-permute-start | bytes 319496 | tf_op jit(solution)/shard_map/ppermute | solution.py:519
  62.9 3.3 %collective-permute-start.6 = (f32[13,16,128]{2,1,0:T(8,128)S(1)}, f32[13,16,128]{2,1,0:T(8,128)S(1)}, u32[]{:S(2)}, u32[]{:S(2)}) collective-permute-start(f32[13,16,128]{2,1,0:T(8,128)S(1)} %get-tuple-element.12), channel_id=1, source_target_pairs={{0,8},{4,508},{8,16},{12,4},{16,24},{20,12},{24,32},{28,20},{32,40... | collective-permute-start | bytes 319496 | tf_op jit(solution)/shard_map/ppermute | solution.py:519
  66.2 1.9 %collective-permute-start.8 = (f32[13,16,128]{2,1,0:T(8,128)S(1)}, f32[13,16,128]{2,1,0:T(8,128)S(1)}, u32[]{:S(2)}, u32[]{:S(2)}) collective-permute-start(f32[13,16,128]{2,1,0:T(8,128)S(1)} %get-tuple-element.12), channel_id=1, source_target_pairs={{0,4},{8,12},{16,20},{24,28},{32,36},{40,44},{48,52},{56,60},{64,6... | collective-permute-start | bytes 319496 | tf_op jit(solution)/shard_map/ppermute | solution.py:524
  68.1 0.0 collective-permute-done.7.far
  68.1 2.4 %collective-permute-start.10 = (f32[13,16,128]{2,1,0:T(8,128)S(1)}, f32[13,16,128]{2,1,0:T(8,128)S(1)}, u32[]{:S(2)}, u32[]{:S(2)}) collective-permute-start(f32[13,16,128]{2,1,0:T(8,128)S(1)} %collective-permute-done.7.far), channel_id=1, source_target_pairs={{0,4},{8,12},{16,20},{24,28},{32,36},{40,44},{48,52},{56,60},{64,6... | collective-permute-start | bytes 319496 | tf_op jit(solution)/shard_map/ppermute | solution.py:524
  70.6 0.0 collective-permute-done.6.near
  70.6 1.9 %collective-permute-start.9 = (f32[13,16,128]{2,1,0:T(8,128)S(1)}, f32[13,16,128]{2,1,0:T(8,128)S(1)}, u32[]{:S(2)}, u32[]{:S(2)}) collective-permute-start(f32[13,16,128]{2,1,0:T(8,128)S(1)} %collective-permute-done.6.near), channel_id=1, source_target_pairs={{0,4},{8,12},{16,20},{24,28},{32,36},{40,44},{48,52},{56,60},{64,6... | collective-permute-start | bytes 319496 | tf_op jit(solution)/shard_map/ppermute | solution.py:524
  72.5 0.0 collective-permute-done.10.pair_far
  72.5 1.3 %collective-permute-done.9.pair_near = f32[13,16,128]{2,1,0:T(8,128)S(1)} collective-permute-done((f32[13,16,128]{2,1,0:T(8,128)S(1)}, f32[13,16,128]{2,1,0:T(8,128)S(1)}, u32[]{:S(2)}, u32[]{:S(2)}) %collective-permute-start.9) | collective-permute-done | bytes 106528 | tf_op jit(solution)/shard_map/ppermute | solution.py:524
  73.8 4.3 %bottom.1 = (f32[6144,16,128]{2,1,0:T(8,128)}, f32[32,1,128]{2,1,0:T(1,128)}) custom-call(f32[21,16,128]{2,1,0:T(8,128)S(1)} %get-tuple-element.11.mine, f32[13,16,128]{2,1,0:T(8,128)S(1)} %collective-permute-done.6.near, f32[13,16,128]{2,1,0:T(8,128)S(1)} %collective-permute-done.7.far, f32[13,16,128]{2,1,0:T(8,128)S(1)} %collective-permute-done.8.pair_own, ...), custom_call_target="tpu_custom_call" | custom-call | tf_op jit(solution)/shard_map/bottom/pallas_call | solution.py:501
  78.1 10.2 %all-to-all-start.1 = ((f32[32,1,128]{2,1,0:T(1,128)}), f32[32,1,128]{2,1,0:T(1,128)S(1)}, u32[]{:S(2)}, u32[]{:S(2)}) async-start(f32[32,1,128]{2,1,0:T(1,128)} %get-tuple-element.13), calls=%async_computation.1 | async-start | bytes 32768 | tf_op jit(solution)/shard_map/all_to_all | solution.py:581
  88.3 7.4 %up.1 = (f32[16,16,256]{2,1,0:T(8,128)S(1)}, f32[16,16,256]{2,1,0:T(8,128)S(1)}) custom-call(f32[6144,16,128]{2,1,0:T(8,128)} %get-tuple-element.14.e2_in, f32[4,25,8,128]{3,2,1,0:T(8,128)S(1)} %all_to_all.10.own.own1, f32[4,25,8,128]{3,2,1,0:T(8,128)S(1)} %collective-permute-done.4.inner.inner1, f32[4,25,8,128]{3,2,1,0:T(8,128)S(1)} %collective-permute-done.5.outer.outer1, ...), custom_call_target="tpu_custom_call" | custom-call | tf_op jit(solution)/shard_map/up/pallas_call | solution.py:501
  95.7 5.8 %all-to-all-done.1.every = f32[32,1,128]{2,1,0:T(1,128)S(1)} async-done(((f32[32,1,128]{2,1,0:T(1,128)}), f32[32,1,128]{2,1,0:T(1,128)S(1)}, u32[]{:S(2)}, u32[]{:S(2)}) %all-to-all-start.1) | async-done | bytes 16416 | tf_op jit(solution)/shard_map/all_to_all | solution.py:581
  101.5 0.9 final.1
  (7 shorter events, 0.0 us)
Async XLA Ops:
  0.0 11.7 %copy-start = (f32[16,16,256]{2,1,0:T(8,128)S(1)}, f32[16,16,256]{2,1,0:T(8,128)}, u32[]{:S(2)}) copy-start(f32[16,16,256]{2,1,0:T(8,128)} %param.5) | copy-start | bytes 786436
  0.0 11.7 %copy-start.1 = (f32[16,16,256]{2,1,0:T(8,128)S(1)}, f32[16,16,256]{2,1,0:T(8,128)}, u32[]{:S(2)}) copy-start(f32[16,16,256]{2,1,0:T(8,128)} %param.4) | copy-start | bytes 786436
  0.0 11.7 %copy-start.2 = (f32[16,16,256]{2,1,0:T(8,128)S(1)}, f32[16,16,256]{2,1,0:T(8,128)}, u32[]{:S(2)}) copy-start(f32[16,16,256]{2,1,0:T(8,128)} %param.3) | copy-start | bytes 786436
  1.4 6.5 %collective-permute-start = (f32[3,16,4,256]{3,2,1,0:T(4,128)S(1)}, f32[3,16,4,256]{3,2,1,0:T(4,128)S(1)}, u32[]{:S(2)}, u32[]{:S(2)}) collective-permute-start(f32[3,16,4,256]{3,2,1,0:T(4,128)S(1)} %get-tuple-element.19), channel_id=1, source_target_pairs={{0,1},{1,2},{2,3},{4,5},{5,6},{6,7},{8,9},{9,10},{10,11},{12,13},{... | collective-permute-start | bytes 589832 | tf_op jit(solution)/shard_map/ppermute | solution.py:514
  5.3 6.4 %collective-permute-start.1 = (f32[3,16,4,256]{3,2,1,0:T(4,128)S(1)}, f32[3,16,4,256]{3,2,1,0:T(4,128)S(1)}, u32[]{:S(2)}, u32[]{:S(2)}) collective-permute-start(f32[3,16,4,256]{3,2,1,0:T(4,128)S(1)} %get-tuple-element.20), channel_id=1, source_target_pairs={{1,0},{2,1},{3,2},{5,4},{6,5},{7,6},{9,8},{10,9},{11,10},{13,12},{... | collective-permute-start | bytes 589832 | tf_op jit(solution)/shard_map/ppermute | solution.py:514
  12.0 10.6 %collective-permute-start.3 = (f32[3,4,24,256]{3,2,1,0:T(8,128)S(1)}, f32[3,4,24,256]{3,2,1,0:T(8,128)S(1)}, u32[]{:S(2)}, u32[]{:S(2)}) collective-permute-start(f32[3,4,24,256]{3,2,1,0:T(8,128)S(1)} %get-tuple-element.17), channel_id=1, source_target_pairs={{4,8},{12,16},{20,24},{28,32},{36,40},{44,48},{52,56},{60,64},{68,... | collective-permute-start | bytes 884744 | tf_op jit(solution)/shard_map/ppermute | solution.py:524
  18.2 4.4 %collective-permute-start.2 = (f32[3,4,24,256]{3,2,1,0:T(8,128)S(1)}, f32[3,4,24,256]{3,2,1,0:T(8,128)S(1)}, u32[]{:S(2)}, u32[]{:S(2)}) collective-permute-start(f32[3,4,24,256]{3,2,1,0:T(8,128)S(1)} %get-tuple-element.18), channel_id=1, source_target_pairs={{0,4},{8,12},{16,20},{24,28},{32,36},{40,44},{48,52},{56,60},{64,6... | collective-permute-start | bytes 884744 | tf_op jit(solution)/shard_map/ppermute | solution.py:524
  38.9 9.5 %collective-permute-start.5 = (f32[4,25,8,128]{3,2,1,0:T(8,128)S(1)}, f32[4,25,8,128]{3,2,1,0:T(8,128)S(1)}, u32[]{:S(2)}, u32[]{:S(2)}) collective-permute-start(f32[4,25,8,128]{3,2,1,0:T(8,128)S(1)} %all_to_all.10.own.own1), channel_id=1, source_target_pairs={{4,8},{12,16},{20,24},{28,32},{36,40},{44,48},{52,56},{60,64},{68,... | collective-permute-start | bytes 1228808 | tf_op jit(solution)/shard_map/ppermute | solution.py:524
  42.8 5.6 %collective-permute-start.4 = (f32[4,25,8,128]{3,2,1,0:T(8,128)S(1)}, f32[4,25,8,128]{3,2,1,0:T(8,128)S(1)}, u32[]{:S(2)}, u32[]{:S(2)}) collective-permute-start(f32[4,25,8,128]{3,2,1,0:T(8,128)S(1)} %all_to_all.10.own.own1), channel_id=1, source_target_pairs={{0,4},{8,12},{16,20},{24,28},{32,36},{40,44},{48,52},{56,60},{64,6... | collective-permute-start | bytes 1228808 | tf_op jit(solution)/shard_map/ppermute | solution.py:524
  50.7 17.4 %collective-permute-start.7 = (f32[13,16,128]{2,1,0:T(8,128)S(1)}, f32[13,16,128]{2,1,0:T(8,128)S(1)}, u32[]{:S(2)}, u32[]{:S(2)}) collective-permute-start(f32[13,16,128]{2,1,0:T(8,128)S(1)} %get-tuple-element.12), channel_id=1, source_target_pairs={{0,16},{4,500},{8,24},{12,508},{16,32},{20,4},{24,40},{28,12},{32,... | collective-permute-start | bytes 319496 | tf_op jit(solution)/shard_map/ppermute | solution.py:519
  62.9 7.6 %collective-permute-start.6 = (f32[13,16,128]{2,1,0:T(8,128)S(1)}, f32[13,16,128]{2,1,0:T(8,128)S(1)}, u32[]{:S(2)}, u32[]{:S(2)}) collective-permute-start(f32[13,16,128]{2,1,0:T(8,128)S(1)} %get-tuple-element.12), channel_id=1, source_target_pairs={{0,8},{4,508},{8,16},{12,4},{16,24},{20,12},{24,32},{28,20},{32,40... | collective-permute-start | bytes 319496 | tf_op jit(solution)/shard_map/ppermute | solution.py:519
  66.2 6.3 %collective-permute-start.8 = (f32[13,16,128]{2,1,0:T(8,128)S(1)}, f32[13,16,128]{2,1,0:T(8,128)S(1)}, u32[]{:S(2)}, u32[]{:S(2)}) collective-permute-start(f32[13,16,128]{2,1,0:T(8,128)S(1)} %get-tuple-element.12), channel_id=1, source_target_pairs={{0,4},{8,12},{16,20},{24,28},{32,36},{40,44},{48,52},{56,60},{64,6... | collective-permute-start | bytes 319496 | tf_op jit(solution)/shard_map/ppermute | solution.py:524
  68.1 4.4 %collective-permute-start.10 = (f32[13,16,128]{2,1,0:T(8,128)S(1)}, f32[13,16,128]{2,1,0:T(8,128)S(1)}, u32[]{:S(2)}, u32[]{:S(2)}) collective-permute-start(f32[13,16,128]{2,1,0:T(8,128)S(1)} %collective-permute-done.7.far), channel_id=1, source_target_pairs={{0,4},{8,12},{16,20},{24,28},{32,36},{40,44},{48,52},{56,60},{64,6... | collective-permute-start | bytes 319496 | tf_op jit(solution)/shard_map/ppermute | solution.py:524
  70.6 3.2 %collective-permute-start.9 = (f32[13,16,128]{2,1,0:T(8,128)S(1)}, f32[13,16,128]{2,1,0:T(8,128)S(1)}, u32[]{:S(2)}, u32[]{:S(2)}) collective-permute-start(f32[13,16,128]{2,1,0:T(8,128)S(1)} %collective-permute-done.6.near), channel_id=1, source_target_pairs={{0,4},{8,12},{16,20},{24,28},{32,36},{40,44},{48,52},{56,60},{64,6... | collective-permute-start | bytes 319496 | tf_op jit(solution)/shard_map/ppermute | solution.py:524
  78.1 23.4 %all-to-all-start.1 = ((f32[32,1,128]{2,1,0:T(1,128)}), f32[32,1,128]{2,1,0:T(1,128)S(1)}, u32[]{:S(2)}, u32[]{:S(2)}) async-start(f32[32,1,128]{2,1,0:T(1,128)} %get-tuple-element.13), calls=%async_computation.1 | async-start | bytes 32768 | tf_op jit(solution)/shard_map/all_to_all | solution.py:581

commit v5 on v4

--- a/solution.py
+++ b/solution.py
@@ -200,12 +200,17 @@
 
 
 def fetch0(own, inner, outer, fields, sems):
-    inner_at, outer_at = sides(0, 20)
     sources, targets = [], []
     for index, ref in enumerate(fields):
-        for part, lo, n in ((own, 4, 16), (inner, inner_at, 4), (outer, outer_at, 4)):
-            sources.append(part.at[index])
-            targets.append(ref.at[pl.ds(lo, n)])
+        n = 3 if index else 4
+        first = 4 + 3 * (index - 1) if index else 0
+        inner_at, outer_at = sides(4 - n, 20)
+        edges = ((inner, inner_at), (outer, outer_at))
+        sources += [part.at[pl.ds(first, n)] for part, _ in edges]
+        targets += [ref.at[pl.ds(lo, n)] for _, lo in edges]
+        if own is not None:
+            sources.append(own.at[index])
+            targets.append(ref.at[pl.ds(4, 16)])
     return fetch(sources, targets, sems)
 
 
@@ -220,12 +225,14 @@
     return fetch(sources, targets, sems)
 
 
-def down0(own, inner, outer, out, vs, vc, cx, cy, cz, dg, wt, ss, cc, m, us, uc, pair, thin, sems):
-    copies = fetch0(own, inner, outer, (m, ss, cc), sems)
-    wait(copies[:3])
+def down0(own, outer, inner, out, vs, vc, cx, cy, cz, dg, wt, ss, cc, m, us, uc, pair, thin, sems):
+    copies = fetch0(None, inner, outer, (m, ss, cc), sems)
+    for index, ref in enumerate((m, ss, cc)):
+        ref[4:20] = own[index]
+    wait(copies[:2])
     coefficients(0, m, cx, cy, cz, dg, wt, 1, 23, C0, None, 256)
     coefs = (cx, cy, cz, dg)
-    wait(copies[3:])
+    wait(copies[2:])
     start(1, 23, S0, (ss, cc), (us, uc), wt)
     sweep(2, 22, W0, (ss, cc), (us, uc), (vs, vc), coefs, wt)
 
@@ -525,23 +532,31 @@
 
 
 def per_device(mobility, sav_vector, cotangent):
-    own = jnp.stack([mobility, sav_vector, cotangent])
-    y_lo = shifted(own[:, :, -HALO:], "narrow", 1)
-    y_hi = shifted(own[:, :, :HALO], "narrow", -1)
-    own = jnp.concatenate([y_lo, own, y_hi], axis=2)
-    last = own.shape[1] - HALO
+    whole = jnp.stack([mobility, sav_vector, cotangent])
+    y_lo = shifted(whole[:, :, -HALO:], "narrow", 1)
+    y_hi = shifted(whole[:, :, :HALO], "narrow", -1)
+    own = jnp.concatenate([y_lo, whole, y_hi], axis=2)
     odd = lax.rem(lax.axis_index("wide"), 2)
-    x_outer = swapped(lax.dynamic_slice_in_dim(own, odd * last, HALO, axis=1), 1)
-    x_inner = swapped(lax.dynamic_slice_in_dim(own, (1 - odd) * last, HALO, axis=1), 0)
+
+    def edge(at_end):
+        return jnp.concatenate(
+            [
+                lax.dynamic_slice_in_dim(own[index], at_end * (16 - n), n, axis=0)
+                for index, n in enumerate((HALO, HALO - 1, HALO - 1))
+            ]
+        )
+
+    x_inner = swapped(edge(1 - odd), 0)
+    x_outer = swapped(edge(odd), 1)
     a0 = (24, 24, 256)
     (chunk,) = call(
         down0,
-        (own, x_inner, x_outer),
+        (own, x_outer, x_inner),
         [(4, 25, 8, 128)],
         [a0] * 13 + [(24, 24, 128)],
         "down0",
-        9,
-        [HBM] * 3,
+        6,
+        [VMEM] + [HBM] * 2,
     )
     gathered = lax.all_to_all(chunk, "narrow", 0, 0)
     outer = swapped(gathered, 1)
@@ -578,10 +593,14 @@
         [HBM, VMEM],
     )
     groups = [[i for i in range(wide) if (i // 2 + 2 * (i % 2)) % 4 == s] for s in range(4)]
+    y_lo, y_hi, mobility, sav_vector, cotangent, sums = lax.optimization_barrier(
+        (y_lo, y_hi, mobility, sav_vector, cotangent, sums)
+    )
     every = lax.all_to_all(sums, "wide", 0, 0, axis_index_groups=groups)
+    again = jnp.concatenate([y_lo, jnp.stack([mobility, sav_vector, cotangent]), y_hi], axis=2)
     out_s, out_c = call(
         up,
-        (e2, gathered, inner, outer, own, x_inner, x_outer),
+        (e2, gathered, inner, outer, again, x_inner, x_outer),
         [(16, 16, 256)] * 2,
         [a1] * 13
         + [a0] * 13

time: 103 us -> 101 us (0.981)
  waiting for transfers between devices: 18.3 us -> 14.4 us
  starting transfers between devices: 51.1 us -> 54.5 us
    ppermute x7, starting transfers between devices: 20.2 us -> 22.9 us  [swapped(): return lax.ppermute(value, 'wide', pairs + [(b, a) for a, b in pairs])]
    ppermute x2, waiting for transfers between devices: 5.1 us -> 2.56 us  [shifted(): lax.ppermute(value, axis, [(i, i + by) for i in range(size) if 0 <= i + b...]
    ppermute x7, waiting for transfers between devices: 7.42 us -> 6.07 us  [swapped(): return lax.ppermute(value, 'wide', pairs + [(b, a) for a, b in pairs])]
    slice x1 -> x0, other arithmetic: 1.34 us -> none  [per_device(): y_lo = shifted(own[:, :, -HALO:], 'narrow', 1)]
    another operation x0 -> x1, other arithmetic: none -> 1.34 us  [per_device(): whole = jnp.stack([mobility, sav_vector, cotangent])]
where the time goes in v5:
time: 101 us
  starting transfers between devices  54.5 us (54%)
  Pallas kernels  18.1 us (18%)
  waiting for transfers between devices  14.4 us (14%)
  blocking collectives  11.6 us (11%)
  other arithmetic  1.74 us (2%)
    ppermute x7, starting transfers between devices, swapped(): return lax.ppermute(value, 'wide', pairs + [(b, a) for a, b in pairs])  22.9 us
    pallas_call x5, Pallas kernels, call(): pl.pallas_call(kernel, out_shape=[jax.ShapeDtypeStruct(s, f32) for s in o...  18.1 us
    ppermute x2, starting transfers between devices, apart(): lax.ppermute(value, 'wide', [(i, (i + by * (1 - 2 * (i % 2))) % size) for...  15.4 us
    all_to_all x1, blocking collectives, per_device(): gathered = lax.all_to_all(chunk, 'narrow', 0, 0)  11.6 us
    all_to_all x1, starting transfers between devices, per_device(): every = lax.all_to_all(sums, 'wide', 0, 0, axis_index_groups=groups)  10.2 us
    ppermute x7, waiting for transfers between devices, swapped(): return lax.ppermute(value, 'wide', pairs + [(b, a) for a, b in pairs])  6.07 us
    ppermute x2, starting transfers between devices, shifted(): lax.ppermute(value, axis, [(i, i + by) for i in range(size) if 0 <= i + b...  5.88 us
    all_to_all x1, waiting for transfers between devices, per_device(): every = lax.all_to_all(sums, 'wide', 0, 0, axis_index_groups=groups)  5.73 us
  transfers between devices with their start and end apart: 12, of which 6 were waited for; matrix products, arithmetic and copies ran while one was open for 0% of the time, Pallas kernels for 7%

profile of v5, /device:TPU:1, one launch (start us, length us, event | category | flops | bytes accessed | tf_op | source)
XLA Modules:
  0.0 100.9 jit_solution(16277480558670776390)
XLA Ops:
  0.0 1.3 %pad_maximum_fusion.4 = (f32[3,16,4,256]{3,2,1,0:T(4,128)S(1)}, f32[3,16,4,256]{3,2,1,0:T(4,128)S(1)}) fusion(f32[1,16,16,256]{3,2,1,0:T(8,128)} %bitcast.18, f32[1,16,16,256]{3,2,1,0:T(8,128)} %bitcast.21, f32[1,16,16,256]{3,2,1,0:T(8,128)} %bitcast.24), kind=kLoop, calls=%fused_computation.4 | loop fusion | flops 196608 | bytes 1179648 | tf_op jit(solution)/shard_map/stack | solution.py:535
  1.4 1.3 %collective-permute-start.1 = (f32[3,16,4,256]{3,2,1,0:T(4,128)S(1)}, f32[3,16,4,256]{3,2,1,0:T(4,128)S(1)}, u32[]{:S(2)}, u32[]{:S(2)}) collective-permute-start(f32[3,16,4,256]{3,2,1,0:T(4,128)S(1)} %get-tuple-element.32), channel_id=1, source_target_pairs={{1,0},{2,1},{3,2},{5,4},{6,5},{7,6},{9,8},{10,9},{11,10},{13,12},{... | collective-permute-start | bytes 589832 | tf_op jit(solution)/shard_map/ppermute | solution.py:521
  2.7 4.6 %collective-permute-start = (f32[3,16,4,256]{3,2,1,0:T(4,128)S(1)}, f32[3,16,4,256]{3,2,1,0:T(4,128)S(1)}, u32[]{:S(2)}, u32[]{:S(2)}) collective-permute-start(f32[3,16,4,256]{3,2,1,0:T(4,128)S(1)} %get-tuple-element.33), channel_id=1, source_target_pairs={{0,1},{1,2},{2,3},{4,5},{5,6},{6,7},{8,9},{9,10},{10,11},{12,13},{... | collective-permute-start | bytes 589832 | tf_op jit(solution)/shard_map/ppermute | solution.py:521
  7.3 1.1 %collective-permute-done.1 = f32[3,16,4,256]{3,2,1,0:T(4,128)S(1)} collective-permute-done((f32[3,16,4,256]{3,2,1,0:T(4,128)S(1)}, f32[3,16,4,256]{3,2,1,0:T(4,128)S(1)}, u32[]{:S(2)}, u32[]{:S(2)}) %collective-permute-start.1) | collective-permute-done | bytes 196640 | tf_op jit(solution)/shard_map/ppermute | solution.py:521
  8.4 1.5 %collective-permute-done = f32[3,16,4,256]{3,2,1,0:T(4,128)S(1)} collective-permute-done((f32[3,16,4,256]{3,2,1,0:T(4,128)S(1)}, f32[3,16,4,256]{3,2,1,0:T(4,128)S(1)}, u32[]{:S(2)}, u32[]{:S(2)}) %collective-permute-start) | collective-permute-done | bytes 196640 | tf_op jit(solution)/shard_map/ppermute | solution.py:521
  9.8 0.2 pad_maximum_fusion.own
  10.0 0.1 fusion
  10.2 6.2 %collective-permute-start.2 = (f32[10,24,256]{2,1,0:T(8,128)S(1)}, f32[10,24,256]{2,1,0:T(8,128)S(1)}, u32[]{:S(2)}, u32[]{:S(2)}) collective-permute-start(f32[10,24,256]{2,1,0:T(8,128)S(1)} %pad_maximum_fusion.2), channel_id=1, source_target_pairs={{4,8},{12,16},{20,24},{28,32},{36,40},{44,48},{52,56},{60,64},{68,... | collective-permute-start | bytes 737288 | tf_op jit(solution)/shard_map/ppermute | solution.py:531
  16.4 3.8 %collective-permute-start.3 = (f32[10,24,256]{2,1,0:T(8,128)S(1)}, f32[10,24,256]{2,1,0:T(8,128)S(1)}, u32[]{:S(2)}, u32[]{:S(2)}) collective-permute-start(f32[10,24,256]{2,1,0:T(8,128)S(1)} %pad_maximum_fusion.3), channel_id=1, source_target_pairs={{0,4},{8,12},{16,20},{24,28},{32,36},{40,44},{48,52},{56,60},{64,6... | collective-permute-start | bytes 737288 | tf_op jit(solution)/shard_map/ppermute | solution.py:531
  20.3 0.0 collective-permute-done.2.outer.outer0
  20.3 1.1 %collective-permute-done.3.inner.inner0 = f32[10,24,256]{2,1,0:T(8,128)S(1)} collective-permute-done((f32[10,24,256]{2,1,0:T(8,128)S(1)}, f32[10,24,256]{2,1,0:T(8,128)S(1)}, u32[]{:S(2)}, u32[]{:S(2)}) %collective-permute-start.3) | collective-permute-done | bytes 245792 | tf_op jit(solution)/shard_map/ppermute | solution.py:531
  21.4 3.3 %down0.1 = f32[4,25,8,128]{3,2,1,0:T(8,128)S(1)} custom-call(f32[3,16,24,256]{3,2,1,0:T(8,128)S(1)} %pad_maximum_fusion.own, f32[10,24,256]{2,1,0:T(8,128)S(1)} %collective-permute-done.2.outer.outer0, f32[10,24,256]{2,1,0:T(8,128)S(1)} %collective-permute-done.3.inner.inner0), custom_call_target="tpu_custom_call" | custom-call | tf_op jit(solution)/shard_map/down0/pallas_call | solution.py:508
  24.7 11.6 %all_to_all.10.own.own1 = f32[4,25,8,128]{3,2,1,0:T(8,128)S(1)} all-to-all(f32[4,25,8,128]{3,2,1,0:T(8,128)S(1)} %down0.1), channel_id=1, replica_groups=mesh['wide'=128,'narrow'=4] {'narrow'}, dimensions={0} | all-to-all | bytes 819200 | tf_op jit(solution)/shard_map/all_to_all | solution.py:561
  36.4 4.7 %collective-permute-start.5 = (f32[4,25,8,128]{3,2,1,0:T(8,128)S(1)}, f32[4,25,8,128]{3,2,1,0:T(8,128)S(1)}, u32[]{:S(2)}, u32[]{:S(2)}) collective-permute-start(f32[4,25,8,128]{3,2,1,0:T(8,128)S(1)} %all_to_all.10.own.own1), channel_id=1, source_target_pairs={{4,8},{12,16},{20,24},{28,32},{36,40},{44,48},{52,56},{60,64},{68,... | collective-permute-start | bytes 1228808 | tf_op jit(solution)/shard_map/ppermute | solution.py:531
  41.1 1.9 %collective-permute-start.4 = (f32[4,25,8,128]{3,2,1,0:T(8,128)S(1)}, f32[4,25,8,128]{3,2,1,0:T(8,128)S(1)}, u32[]{:S(2)}, u32[]{:S(2)}) collective-permute-start(f32[4,25,8,128]{3,2,1,0:T(8,128)S(1)} %all_to_all.10.own.own1), channel_id=1, source_target_pairs={{0,4},{8,12},{16,20},{24,28},{32,36},{40,44},{48,52},{56,60},{64,6... | collective-permute-start | bytes 1228808 | tf_op jit(solution)/shard_map/ppermute | solution.py:531
  43.0 3.7 %collective-permute-done.5.outer.outer1 = f32[4,25,8,128]{3,2,1,0:T(8,128)S(1)} collective-permute-done((f32[4,25,8,128]{3,2,1,0:T(8,128)S(1)}, f32[4,25,8,128]{3,2,1,0:T(8,128)S(1)}, u32[]{:S(2)}, u32[]{:S(2)}) %collective-permute-start.5) | collective-permute-done | bytes 409632 | tf_op jit(solution)/shard_map/ppermute | solution.py:531
  46.7 2.3 %down1.1 = (f32[13,16,128]{2,1,0:T(8,128)S(1)}, f32[21,16,128]{2,1,0:T(8,128)S(1)}) custom-call(f32[4,25,8,128]{3,2,1,0:T(8,128)S(1)} %all_to_all.10.own.own1, f32[4,25,8,128]{3,2,1,0:T(8,128)S(1)} %collective-permute-done.4.inner.inner1, f32[4,25,8,128]{3,2,1,0:T(8,128)S(1)} %collective-permute-done.5.outer.outer1), custom_call_target="tpu_custom_call" | custom-call | tf_op jit(solution)/shard_map/down1/pallas_call | solution.py:508
  49.1 12.2 %collective-permute-start.7 = (f32[13,16,128]{2,1,0:T(8,128)S(1)}, f32[13,16,128]{2,1,0:T(8,128)S(1)}, u32[]{:S(2)}, u32[]{:S(2)}) collective-permute-start(f32[13,16,128]{2,1,0:T(8,128)S(1)} %get-tuple-element.18), channel_id=1, source_target_pairs={{0,16},{4,500},{8,24},{12,508},{16,32},{20,4},{24,40},{28,12},{32,... | collective-permute-start | bytes 319496 | tf_op jit(solution)/shard_map/ppermute | solution.py:526
  61.2 3.3 %collective-permute-start.6 = (f32[13,16,128]{2,1,0:T(8,128)S(1)}, f32[13,16,128]{2,1,0:T(8,128)S(1)}, u32[]{:S(2)}, u32[]{:S(2)}) collective-permute-start(f32[13,16,128]{2,1,0:T(8,128)S(1)} %get-tuple-element.18), channel_id=1, source_target_pairs={{0,8},{4,508},{8,16},{12,4},{16,24},{20,12},{24,32},{28,20},{32,40... | collective-permute-start | bytes 319496 | tf_op jit(solution)/shard_map/ppermute | solution.py:526
  64.5 1.9 %collective-permute-start.8 = (f32[13,16,128]{2,1,0:T(8,128)S(1)}, f32[13,16,128]{2,1,0:T(8,128)S(1)}, u32[]{:S(2)}, u32[]{:S(2)}) collective-permute-start(f32[13,16,128]{2,1,0:T(8,128)S(1)} %get-tuple-element.18), channel_id=1, source_target_pairs={{0,4},{8,12},{16,20},{24,28},{32,36},{40,44},{48,52},{56,60},{64,6... | collective-permute-start | bytes 319496 | tf_op jit(solution)/shard_map/ppermute | solution.py:531
  66.5 0.0 collective-permute-done.7.far
  66.5 2.4 %collective-permute-start.10 = (f32[13,16,128]{2,1,0:T(8,128)S(1)}, f32[13,16,128]{2,1,0:T(8,128)S(1)}, u32[]{:S(2)}, u32[]{:S(2)}) collective-permute-start(f32[13,16,128]{2,1,0:T(8,128)S(1)} %collective-permute-done.7.far), channel_id=1, source_target_pairs={{0,4},{8,12},{16,20},{24,28},{32,36},{40,44},{48,52},{56,60},{64,6... | collective-permute-start | bytes 319496 | tf_op jit(solution)/shard_map/ppermute | solution.py:531
  68.9 0.0 collective-permute-done.6.near
  68.9 1.9 %collective-permute-start.9 = (f32[13,16,128]{2,1,0:T(8,128)S(1)}, f32[13,16,128]{2,1,0:T(8,128)S(1)}, u32[]{:S(2)}, u32[]{:S(2)}) collective-permute-start(f32[13,16,128]{2,1,0:T(8,128)S(1)} %collective-permute-done.6.near), channel_id=1, source_target_pairs={{0,4},{8,12},{16,20},{24,28},{32,36},{40,44},{48,52},{56,60},{64,6... | collective-permute-start | bytes 319496 | tf_op jit(solution)/shard_map/ppermute | solution.py:531
  70.8 0.0 collective-permute-done.10.pair_far
  70.8 1.3 %collective-permute-done.9.pair_near = f32[13,16,128]{2,1,0:T(8,128)S(1)} collective-permute-done((f32[13,16,128]{2,1,0:T(8,128)S(1)}, f32[13,16,128]{2,1,0:T(8,128)S(1)}, u32[]{:S(2)}, u32[]{:S(2)}) %collective-permute-start.9) | collective-permute-done | bytes 106528 | tf_op jit(solution)/shard_map/ppermute | solution.py:531
  72.1 4.3 %bottom.1 = (f32[6144,16,128]{2,1,0:T(8,128)}, f32[32,1,128]{2,1,0:T(1,128)}) custom-call(f32[21,16,128]{2,1,0:T(8,128)S(1)} %get-tuple-element.17.mine, f32[13,16,128]{2,1,0:T(8,128)S(1)} %collective-permute-done.6.near, f32[13,16,128]{2,1,0:T(8,128)S(1)} %collective-permute-done.7.far, f32[13,16,128]{2,1,0:T(8,128)S(1)} %collective-permute-done.8.pair_own, ...), custom_call_target="tpu_custom_call" | custom-call | tf_op jit(solution)/shard_map/bottom/pallas_call | solution.py:508
  76.4 10.2 %all-to-all-start.1 = ((f32[32,1,128]{2,1,0:T(1,128)}), f32[32,1,128]{2,1,0:T(1,128)S(1)}, u32[]{:S(2)}, u32[]{:S(2)}) async-start(f32[32,1,128]{2,1,0:T(1,128)} %get-tuple-element.20), calls=%async_computation.1 | async-start | bytes 32768 | tf_op jit(solution)/shard_map/all_to_all | solution.py:599
  86.6 0.2 pad_maximum_fusion.1.own0
  86.8 7.3 %up.1 = (f32[16,16,256]{2,1,0:T(8,128)S(1)}, f32[16,16,256]{2,1,0:T(8,128)S(1)}) custom-call(f32[6144,16,128]{2,1,0:T(8,128)} %get-tuple-element.21.e2_in, f32[4,25,8,128]{3,2,1,0:T(8,128)S(1)} %all_to_all.10.own.own1, f32[4,25,8,128]{3,2,1,0:T(8,128)S(1)} %collective-permute-done.4.inner.inner1, f32[4,25,8,128]{3,2,1,0:T(8,128)S(1)} %collective-permute-done.5.outer.outer1, ...), custom_call_target="tpu_custom_call" | custom-call | tf_op jit(solution)/shard_map/up/pallas_call | solution.py:508
  94.1 5.7 %all-to-all-done.1.every = f32[32,1,128]{2,1,0:T(1,128)S(1)} async-done(((f32[32,1,128]{2,1,0:T(1,128)}), f32[32,1,128]{2,1,0:T(1,128)S(1)}, u32[]{:S(2)}, u32[]{:S(2)}) %all-to-all-start.1) | async-done | bytes 16416 | tf_op jit(solution)/shard_map/all_to_all | solution.py:599
  99.8 0.9 final.1
  (12 shorter events, 0.1 us)
Async XLA Ops:
  0.0 9.8 %copy-start = (f32[16,16,256]{2,1,0:T(8,128)S(1)}, f32[16,16,256]{2,1,0:T(8,128)}, u32[]{:S(2)}) copy-start(f32[16,16,256]{2,1,0:T(8,128)} %param.5) | copy-start | bytes 786436
  0.0 9.8 %copy-start.1 = (f32[16,16,256]{2,1,0:T(8,128)S(1)}, f32[16,16,256]{2,1,0:T(8,128)}, u32[]{:S(2)}) copy-start(f32[16,16,256]{2,1,0:T(8,128)} %param.4) | copy-start | bytes 786436
  0.0 9.8 %copy-start.2 = (f32[16,16,256]{2,1,0:T(8,128)S(1)}, f32[16,16,256]{2,1,0:T(8,128)}, u32[]{:S(2)}) copy-start(f32[16,16,256]{2,1,0:T(8,128)} %param.3) | copy-start | bytes 786436
  1.4 7.0 %collective-permute-start.1 = (f32[3,16,4,256]{3,2,1,0:T(4,128)S(1)}, f32[3,16,4,256]{3,2,1,0:T(4,128)S(1)}, u32[]{:S(2)}, u32[]{:S(2)}) collective-permute-start(f32[3,16,4,256]{3,2,1,0:T(4,128)S(1)} %get-tuple-element.32), channel_id=1, source_target_pairs={{1,0},{2,1},{3,2},{5,4},{6,5},{7,6},{9,8},{10,9},{11,10},{13,12},{... | collective-permute-start | bytes 589832 | tf_op jit(solution)/shard_map/ppermute | solution.py:521
  2.7 7.2 %collective-permute-start = (f32[3,16,4,256]{3,2,1,0:T(4,128)S(1)}, f32[3,16,4,256]{3,2,1,0:T(4,128)S(1)}, u32[]{:S(2)}, u32[]{:S(2)}) collective-permute-start(f32[3,16,4,256]{3,2,1,0:T(4,128)S(1)} %get-tuple-element.33), channel_id=1, source_target_pairs={{0,1},{1,2},{2,3},{4,5},{5,6},{6,7},{8,9},{9,10},{10,11},{12,13},{... | collective-permute-start | bytes 589832 | tf_op jit(solution)/shard_map/ppermute | solution.py:521
  10.2 10.1 %collective-permute-start.2 = (f32[10,24,256]{2,1,0:T(8,128)S(1)}, f32[10,24,256]{2,1,0:T(8,128)S(1)}, u32[]{:S(2)}, u32[]{:S(2)}) collective-permute-start(f32[10,24,256]{2,1,0:T(8,128)S(1)} %pad_maximum_fusion.2), channel_id=1, source_target_pairs={{4,8},{12,16},{20,24},{28,32},{36,40},{44,48},{52,56},{60,64},{68,... | collective-permute-start | bytes 737288 | tf_op jit(solution)/shard_map/ppermute | solution.py:531
  16.4 5.0 %collective-permute-start.3 = (f32[10,24,256]{2,1,0:T(8,128)S(1)}, f32[10,24,256]{2,1,0:T(8,128)S(1)}, u32[]{:S(2)}, u32[]{:S(2)}) collective-permute-start(f32[10,24,256]{2,1,0:T(8,128)S(1)} %pad_maximum_fusion.3), channel_id=1, source_target_pairs={{0,4},{8,12},{16,20},{24,28},{32,36},{40,44},{48,52},{56,60},{64,6... | collective-permute-start | bytes 737288 | tf_op jit(solution)/shard_map/ppermute | solution.py:531
  36.4 10.4 %collective-permute-start.5 = (f32[4,25,8,128]{3,2,1,0:T(8,128)S(1)}, f32[4,25,8,128]{3,2,1,0:T(8,128)S(1)}, u32[]{:S(2)}, u32[]{:S(2)}) collective-permute-start(f32[4,25,8,128]{3,2,1,0:T(8,128)S(1)} %all_to_all.10.own.own1), channel_id=1, source_target_pairs={{4,8},{12,16},{20,24},{28,32},{36,40},{44,48},{52,56},{60,64},{68,... | collective-permute-start | bytes 1228808 | tf_op jit(solution)/shard_map/ppermute | solution.py:531
  41.1 5.6 %collective-permute-start.4 = (f32[4,25,8,128]{3,2,1,0:T(8,128)S(1)}, f32[4,25,8,128]{3,2,1,0:T(8,128)S(1)}, u32[]{:S(2)}, u32[]{:S(2)}) collective-permute-start(f32[4,25,8,128]{3,2,1,0:T(8,128)S(1)} %all_to_all.10.own.own1), channel_id=1, source_target_pairs={{0,4},{8,12},{16,20},{24,28},{32,36},{40,44},{48,52},{56,60},{64,6... | collective-permute-start | bytes 1228808 | tf_op jit(solution)/shard_map/ppermute | solution.py:531
  49.1 17.4 %collective-permute-start.7 = (f32[13,16,128]{2,1,0:T(8,128)S(1)}, f32[13,16,128]{2,1,0:T(8,128)S(1)}, u32[]{:S(2)}, u32[]{:S(2)}) collective-permute-start(f32[13,16,128]{2,1,0:T(8,128)S(1)} %get-tuple-element.18), channel_id=1, source_target_pairs={{0,16},{4,500},{8,24},{12,508},{16,32},{20,4},{24,40},{28,12},{32,... | collective-permute-start | bytes 319496 | tf_op jit(solution)/shard_map/ppermute | solution.py:526
  61.2 7.6 %collective-permute-start.6 = (f32[13,16,128]{2,1,0:T(8,128)S(1)}, f32[13,16,128]{2,1,0:T(8,128)S(1)}, u32[]{:S(2)}, u32[]{:S(2)}) collective-permute-start(f32[13,16,128]{2,1,0:T(8,128)S(1)} %get-tuple-element.18), channel_id=1, source_target_pairs={{0,8},{4,508},{8,16},{12,4},{16,24},{20,12},{24,32},{28,20},{32,40... | collective-permute-start | bytes 319496 | tf_op jit(solution)/shard_map/ppermute | solution.py:526
  64.5 6.3 %collective-permute-start.8 = (f32[13,16,128]{2,1,0:T(8,128)S(1)}, f32[13,16,128]{2,1,0:T(8,128)S(1)}, u32[]{:S(2)}, u32[]{:S(2)}) collective-permute-start(f32[13,16,128]{2,1,0:T(8,128)S(1)} %get-tuple-element.18), channel_id=1, source_target_pairs={{0,4},{8,12},{16,20},{24,28},{32,36},{40,44},{48,52},{56,60},{64,6... | collective-permute-start | bytes 319496 | tf_op jit(solution)/shard_map/ppermute | solution.py:531
  66.5 4.4 %collective-permute-start.10 = (f32[13,16,128]{2,1,0:T(8,128)S(1)}, f32[13,16,128]{2,1,0:T(8,128)S(1)}, u32[]{:S(2)}, u32[]{:S(2)}) collective-permute-start(f32[13,16,128]{2,1,0:T(8,128)S(1)} %collective-permute-done.7.far), channel_id=1, source_target_pairs={{0,4},{8,12},{16,20},{24,28},{32,36},{40,44},{48,52},{56,60},{64,6... | collective-permute-start | bytes 319496 | tf_op jit(solution)/shard_map/ppermute | solution.py:531
  68.9 3.2 %collective-permute-start.9 = (f32[13,16,128]{2,1,0:T(8,128)S(1)}, f32[13,16,128]{2,1,0:T(8,128)S(1)}, u32[]{:S(2)}, u32[]{:S(2)}) collective-permute-start(f32[13,16,128]{2,1,0:T(8,128)S(1)} %collective-permute-done.6.near), channel_id=1, source_target_pairs={{0,4},{8,12},{16,20},{24,28},{32,36},{40,44},{48,52},{56,60},{64,6... | collective-permute-start | bytes 319496 | tf_op jit(solution)/shard_map/ppermute | solution.py:531
  76.4 23.4 %all-to-all-start.1 = ((f32[32,1,128]{2,1,0:T(1,128)}), f32[32,1,128]{2,1,0:T(1,128)S(1)}, u32[]{:S(2)}, u32[]{:S(2)}) async-start(f32[32,1,128]{2,1,0:T(1,128)} %get-tuple-element.20), calls=%async_computation.1 | async-start | bytes 32768 | tf_op jit(solution)/shard_map/all_to_all | solution.py:599

commit v6 on v5

--- a/solution.py
+++ b/solution.py
@@ -308,7 +308,7 @@
 
 
 def bottom(
-    mine, near, far, pair_own, pair_near, pair_far, e2_out, sums,
+    mine, far, near, pair_own, pair_far, pair_near, e2_out, sums,
     m2, r2, u2, v2, cx2, cy2, cz2, dg2, wt2,
     m3, r3, u3, v3, cx3, cy3, cz3, dg3, wt3,
     m4, r4, u4, v4, cx4, cy4, cz4, dg4, wt4,
@@ -579,7 +579,7 @@
     wide = lax.axis_size("wide")
     e2, sums = call(
         bottom,
-        (mine, near, far, pair_own, pair_near, pair_far),
+        (mine, far, near, pair_own, pair_far, pair_near),
         [(ROOM, 16, 128), (wide // 4, 1, 128)],
         [(44, 16, 128)] * 9
         + [(22, 8, 128)] * 9

time: 101 us -> 101 us (level)
  no operation moved by 1% of the time
where the time goes in v6:
time: 101 us
  starting transfers between devices  54.2 us (54%)
  Pallas kernels  18.1 us (18%)
  waiting for transfers between devices  14.4 us (14%)
  blocking collectives  11.6 us (11%)
  other arithmetic  1.74 us (2%)
    ppermute x7, starting transfers between devices, swapped(): return lax.ppermute(value, 'wide', pairs + [(b, a) for a, b in pairs])  22.9 us
    pallas_call x5, Pallas kernels, call(): pl.pallas_call(kernel, out_shape=[jax.ShapeDtypeStruct(s, f32) for s in o...  18.1 us
    ppermute x2, starting transfers between devices, apart(): lax.ppermute(value, 'wide', [(i, (i + by * (1 - 2 * (i % 2))) % size) for...  15.4 us
    all_to_all x1, blocking collectives, per_device(): gathered = lax.all_to_all(chunk, 'narrow', 0, 0)  11.6 us
    all_to_all x1, starting transfers between devices, per_device(): every = lax.all_to_all(sums, 'wide', 0, 0, axis_index_groups=groups)  9.96 us
    ppermute x7, waiting for transfers between devices, swapped(): return lax.ppermute(value, 'wide', pairs + [(b, a) for a, b in pairs])  6.07 us
    ppermute x2, starting transfers between devices, shifted(): lax.ppermute(value, axis, [(i, i + by) for i in range(size) if 0 <= i + b...  5.88 us
    all_to_all x1, waiting for transfers between devices, per_device(): every = lax.all_to_all(sums, 'wide', 0, 0, axis_index_groups=groups)  5.73 us
  transfers between devices with their start and end apart: 12, of which 6 were waited for; matrix products, arithmetic and copies ran while one was open for 0% of the time, Pallas kernels for 7%

profile of v6, /device:TPU:1, one launch (start us, length us, event | category | flops | bytes accessed | tf_op | source)
XLA Modules:
  0.0 100.6 jit_solution(1679458645502397864)
XLA Ops:
  0.0 1.3 %pad_maximum_fusion.4 = (f32[3,16,4,256]{3,2,1,0:T(4,128)S(1)}, f32[3,16,4,256]{3,2,1,0:T(4,128)S(1)}) fusion(f32[1,16,16,256]{3,2,1,0:T(8,128)} %bitcast.18, f32[1,16,16,256]{3,2,1,0:T(8,128)} %bitcast.21, f32[1,16,16,256]{3,2,1,0:T(8,128)} %bitcast.24), kind=kLoop, calls=%fused_computation.4 | loop fusion | flops 196608 | bytes 1179648 | tf_op jit(solution)/shard_map/stack | solution.py:535
  1.4 1.3 %collective-permute-start.1 = (f32[3,16,4,256]{3,2,1,0:T(4,128)S(1)}, f32[3,16,4,256]{3,2,1,0:T(4,128)S(1)}, u32[]{:S(2)}, u32[]{:S(2)}) collective-permute-start(f32[3,16,4,256]{3,2,1,0:T(4,128)S(1)} %get-tuple-element.32), channel_id=1, source_target_pairs={{1,0},{2,1},{3,2},{5,4},{6,5},{7,6},{9,8},{10,9},{11,10},{13,12},{... | collective-permute-start | bytes 589832 | tf_op jit(solution)/shard_map/ppermute | solution.py:521
  2.7 4.6 %collective-permute-start = (f32[3,16,4,256]{3,2,1,0:T(4,128)S(1)}, f32[3,16,4,256]{3,2,1,0:T(4,128)S(1)}, u32[]{:S(2)}, u32[]{:S(2)}) collective-permute-start(f32[3,16,4,256]{3,2,1,0:T(4,128)S(1)} %get-tuple-element.33), channel_id=1, source_target_pairs={{0,1},{1,2},{2,3},{4,5},{5,6},{6,7},{8,9},{9,10},{10,11},{12,13},{... | collective-permute-start | bytes 589832 | tf_op jit(solution)/shard_map/ppermute | solution.py:521
  7.3 1.1 %collective-permute-done.1 = f32[3,16,4,256]{3,2,1,0:T(4,128)S(1)} collective-permute-done((f32[3,16,4,256]{3,2,1,0:T(4,128)S(1)}, f32[3,16,4,256]{3,2,1,0:T(4,128)S(1)}, u32[]{:S(2)}, u32[]{:S(2)}) %collective-permute-start.1) | collective-permute-done | bytes 196640 | tf_op jit(solution)/shard_map/ppermute | solution.py:521
  8.4 1.5 %collective-permute-done = f32[3,16,4,256]{3,2,1,0:T(4,128)S(1)} collective-permute-done((f32[3,16,4,256]{3,2,1,0:T(4,128)S(1)}, f32[3,16,4,256]{3,2,1,0:T(4,128)S(1)}, u32[]{:S(2)}, u32[]{:S(2)}) %collective-permute-start) | collective-permute-done | bytes 196640 | tf_op jit(solution)/shard_map/ppermute | solution.py:521
  9.8 0.2 pad_maximum_fusion.own
  10.0 0.1 fusion
  10.2 6.2 %collective-permute-start.2 = (f32[10,24,256]{2,1,0:T(8,128)S(1)}, f32[10,24,256]{2,1,0:T(8,128)S(1)}, u32[]{:S(2)}, u32[]{:S(2)}) collective-permute-start(f32[10,24,256]{2,1,0:T(8,128)S(1)} %pad_maximum_fusion.2), channel_id=1, source_target_pairs={{4,8},{12,16},{20,24},{28,32},{36,40},{44,48},{52,56},{60,64},{68,... | collective-permute-start | bytes 737288 | tf_op jit(solution)/shard_map/ppermute | solution.py:531
  16.4 3.8 %collective-permute-start.3 = (f32[10,24,256]{2,1,0:T(8,128)S(1)}, f32[10,24,256]{2,1,0:T(8,128)S(1)}, u32[]{:S(2)}, u32[]{:S(2)}) collective-permute-start(f32[10,24,256]{2,1,0:T(8,128)S(1)} %pad_maximum_fusion.3), channel_id=1, source_target_pairs={{0,4},{8,12},{16,20},{24,28},{32,36},{40,44},{48,52},{56,60},{64,6... | collective-permute-start | bytes 737288 | tf_op jit(solution)/shard_map/ppermute | solution.py:531
  20.3 0.0 collective-permute-done.2.outer.outer0
  20.3 1.1 %collective-permute-done.3.inner.inner0 = f32[10,24,256]{2,1,0:T(8,128)S(1)} collective-permute-done((f32[10,24,256]{2,1,0:T(8,128)S(1)}, f32[10,24,256]{2,1,0:T(8,128)S(1)}, u32[]{:S(2)}, u32[]{:S(2)}) %collective-permute-start.3) | collective-permute-done | bytes 245792 | tf_op jit(solution)/shard_map/ppermute | solution.py:531
  21.4 3.3 %down0.1 = f32[4,25,8,128]{3,2,1,0:T(8,128)S(1)} custom-call(f32[3,16,24,256]{3,2,1,0:T(8,128)S(1)} %pad_maximum_fusion.own, f32[10,24,256]{2,1,0:T(8,128)S(1)} %collective-permute-done.2.outer.outer0, f32[10,24,256]{2,1,0:T(8,128)S(1)} %collective-permute-done.3.inner.inner0), custom_call_target="tpu_custom_call" | custom-call | tf_op jit(solution)/shard_map/down0/pallas_call | solution.py:508
  24.7 11.6 %all_to_all.10.own.own1 = f32[4,25,8,128]{3,2,1,0:T(8,128)S(1)} all-to-all(f32[4,25,8,128]{3,2,1,0:T(8,128)S(1)} %down0.1), channel_id=1, replica_groups=mesh['wide'=128,'narrow'=4] {'narrow'}, dimensions={0} | all-to-all | bytes 819200 | tf_op jit(solution)/shard_map/all_to_all | solution.py:561
  36.4 4.7 %collective-permute-start.5 = (f32[4,25,8,128]{3,2,1,0:T(8,128)S(1)}, f32[4,25,8,128]{3,2,1,0:T(8,128)S(1)}, u32[]{:S(2)}, u32[]{:S(2)}) collective-permute-start(f32[4,25,8,128]{3,2,1,0:T(8,128)S(1)} %all_to_all.10.own.own1), channel_id=1, source_target_pairs={{4,8},{12,16},{20,24},{28,32},{36,40},{44,48},{52,56},{60,64},{68,... | collective-permute-start | bytes 1228808 | tf_op jit(solution)/shard_map/ppermute | solution.py:531
  41.1 1.9 %collective-permute-start.4 = (f32[4,25,8,128]{3,2,1,0:T(8,128)S(1)}, f32[4,25,8,128]{3,2,1,0:T(8,128)S(1)}, u32[]{:S(2)}, u32[]{:S(2)}) collective-permute-start(f32[4,25,8,128]{3,2,1,0:T(8,128)S(1)} %all_to_all.10.own.own1), channel_id=1, source_target_pairs={{0,4},{8,12},{16,20},{24,28},{32,36},{40,44},{48,52},{56,60},{64,6... | collective-permute-start | bytes 1228808 | tf_op jit(solution)/shard_map/ppermute | solution.py:531
  43.0 3.7 %collective-permute-done.5.outer.outer1 = f32[4,25,8,128]{3,2,1,0:T(8,128)S(1)} collective-permute-done((f32[4,25,8,128]{3,2,1,0:T(8,128)S(1)}, f32[4,25,8,128]{3,2,1,0:T(8,128)S(1)}, u32[]{:S(2)}, u32[]{:S(2)}) %collective-permute-start.5) | collective-permute-done | bytes 409632 | tf_op jit(solution)/shard_map/ppermute | solution.py:531
  46.7 0.0 collective-permute-done.4.inner.inner1
  46.7 2.3 %down1.1 = (f32[13,16,128]{2,1,0:T(8,128)S(1)}, f32[21,16,128]{2,1,0:T(8,128)S(1)}) custom-call(f32[4,25,8,128]{3,2,1,0:T(8,128)S(1)} %all_to_all.10.own.own1, f32[4,25,8,128]{3,2,1,0:T(8,128)S(1)} %collective-permute-done.4.inner.inner1, f32[4,25,8,128]{3,2,1,0:T(8,128)S(1)} %collective-permute-done.5.outer.outer1), custom_call_target="tpu_custom_call" | custom-call | tf_op jit(solution)/shard_map/down1/pallas_call | solution.py:508
  49.1 8.5 %collective-permute-start.7 = (f32[13,16,128]{2,1,0:T(8,128)S(1)}, f32[13,16,128]{2,1,0:T(8,128)S(1)}, u32[]{:S(2)}, u32[]{:S(2)}) collective-permute-start(f32[13,16,128]{2,1,0:T(8,128)S(1)} %get-tuple-element.18), channel_id=1, source_target_pairs={{0,8},{4,508},{8,16},{12,4},{16,24},{20,12},{24,32},{28,20},{32,40... | collective-permute-start | bytes 319496 | tf_op jit(solution)/shard_map/ppermute | solution.py:526
  57.5 7.0 %collective-permute-start.6 = (f32[13,16,128]{2,1,0:T(8,128)S(1)}, f32[13,16,128]{2,1,0:T(8,128)S(1)}, u32[]{:S(2)}, u32[]{:S(2)}) collective-permute-start(f32[13,16,128]{2,1,0:T(8,128)S(1)} %get-tuple-element.18), channel_id=1, source_target_pairs={{0,16},{4,500},{8,24},{12,508},{16,32},{20,4},{24,40},{28,12},{32,... | collective-permute-start | bytes 319496 | tf_op jit(solution)/shard_map/ppermute | solution.py:526
  64.5 1.9 %collective-permute-start.8 = (f32[13,16,128]{2,1,0:T(8,128)S(1)}, f32[13,16,128]{2,1,0:T(8,128)S(1)}, u32[]{:S(2)}, u32[]{:S(2)}) collective-permute-start(f32[13,16,128]{2,1,0:T(8,128)S(1)} %get-tuple-element.18), channel_id=1, source_target_pairs={{0,4},{8,12},{16,20},{24,28},{32,36},{40,44},{48,52},{56,60},{64,6... | collective-permute-start | bytes 319496 | tf_op jit(solution)/shard_map/ppermute | solution.py:531
  66.5 0.0 collective-permute-done.7.near
  66.5 2.4 %collective-permute-start.10 = (f32[13,16,128]{2,1,0:T(8,128)S(1)}, f32[13,16,128]{2,1,0:T(8,128)S(1)}, u32[]{:S(2)}, u32[]{:S(2)}) collective-permute-start(f32[13,16,128]{2,1,0:T(8,128)S(1)} %collective-permute-done.7.near), channel_id=1, source_target_pairs={{0,4},{8,12},{16,20},{24,28},{32,36},{40,44},{48,52},{56,60},{64,6... | collective-permute-start | bytes 319496 | tf_op jit(solution)/shard_map/ppermute | solution.py:531
  68.9 0.0 collective-permute-done.6.far
  68.9 1.9 %collective-permute-start.9 = (f32[13,16,128]{2,1,0:T(8,128)S(1)}, f32[13,16,128]{2,1,0:T(8,128)S(1)}, u32[]{:S(2)}, u32[]{:S(2)}) collective-permute-start(f32[13,16,128]{2,1,0:T(8,128)S(1)} %collective-permute-done.6.far), channel_id=1, source_target_pairs={{0,4},{8,12},{16,20},{24,28},{32,36},{40,44},{48,52},{56,60},{64,6... | collective-permute-start | bytes 319496 | tf_op jit(solution)/shard_map/ppermute | solution.py:531
  70.8 1.3 %collective-permute-done.9.pair_far = f32[13,16,128]{2,1,0:T(8,128)S(1)} collective-permute-done((f32[13,16,128]{2,1,0:T(8,128)S(1)}, f32[13,16,128]{2,1,0:T(8,128)S(1)}, u32[]{:S(2)}, u32[]{:S(2)}) %collective-permute-start.9) | collective-permute-done | bytes 106528 | tf_op jit(solution)/shard_map/ppermute | solution.py:531
  72.1 4.3 %bottom.1 = (f32[6144,16,128]{2,1,0:T(8,128)}, f32[32,1,128]{2,1,0:T(1,128)}) custom-call(f32[21,16,128]{2,1,0:T(8,128)S(1)} %get-tuple-element.17.mine, f32[13,16,128]{2,1,0:T(8,128)S(1)} %collective-permute-done.6.far, f32[13,16,128]{2,1,0:T(8,128)S(1)} %collective-permute-done.7.near, f32[13,16,128]{2,1,0:T(8,128)S(1)} %collective-permute-done.8.pair_own, ...), custom_call_target="tpu_custom_call" | custom-call | tf_op jit(solution)/shard_map/bottom/pallas_call | solution.py:508
  76.4 10.0 %all-to-all-start.1 = ((f32[32,1,128]{2,1,0:T(1,128)}), f32[32,1,128]{2,1,0:T(1,128)S(1)}, u32[]{:S(2)}, u32[]{:S(2)}) async-start(f32[32,1,128]{2,1,0:T(1,128)} %get-tuple-element.20), calls=%async_computation.1 | async-start | bytes 32768 | tf_op jit(solution)/shard_map/all_to_all | solution.py:599
  86.4 0.2 pad_maximum_fusion.1.own0
  86.6 7.3 %up.1 = (f32[16,16,256]{2,1,0:T(8,128)S(1)}, f32[16,16,256]{2,1,0:T(8,128)S(1)}) custom-call(f32[6144,16,128]{2,1,0:T(8,128)} %get-tuple-element.21.e2_in, f32[4,25,8,128]{3,2,1,0:T(8,128)S(1)} %all_to_all.10.own.own1, f32[4,25,8,128]{3,2,1,0:T(8,128)S(1)} %collective-permute-done.4.inner.inner1, f32[4,25,8,128]{3,2,1,0:T(8,128)S(1)} %collective-permute-done.5.outer.outer1, ...), custom_call_target="tpu_custom_call" | custom-call | tf_op jit(solution)/shard_map/up/pallas_call | solution.py:508
  93.8 5.7 %all-to-all-done.1.every = f32[32,1,128]{2,1,0:T(1,128)S(1)} async-done(((f32[32,1,128]{2,1,0:T(1,128)}), f32[32,1,128]{2,1,0:T(1,128)S(1)}, u32[]{:S(2)}, u32[]{:S(2)}) %all-to-all-start.1) | async-done | bytes 16416 | tf_op jit(solution)/shard_map/all_to_all | solution.py:599
  99.5 0.9 final.1
  (12 shorter events, 0.1 us)
Async XLA Ops:
  0.0 9.8 %copy-start = (f32[16,16,256]{2,1,0:T(8,128)S(1)}, f32[16,16,256]{2,1,0:T(8,128)}, u32[]{:S(2)}) copy-start(f32[16,16,256]{2,1,0:T(8,128)} %param.5) | copy-start | bytes 786436
  0.0 9.8 %copy-start.1 = (f32[16,16,256]{2,1,0:T(8,128)S(1)}, f32[16,16,256]{2,1,0:T(8,128)}, u32[]{:S(2)}) copy-start(f32[16,16,256]{2,1,0:T(8,128)} %param.4) | copy-start | bytes 786436
  0.0 9.8 %copy-start.2 = (f32[16,16,256]{2,1,0:T(8,128)S(1)}, f32[16,16,256]{2,1,0:T(8,128)}, u32[]{:S(2)}) copy-start(f32[16,16,256]{2,1,0:T(8,128)} %param.3) | copy-start | bytes 786436
  1.4 7.0 %collective-permute-start.1 = (f32[3,16,4,256]{3,2,1,0:T(4,128)S(1)}, f32[3,16,4,256]{3,2,1,0:T(4,128)S(1)}, u32[]{:S(2)}, u32[]{:S(2)}) collective-permute-start(f32[3,16,4,256]{3,2,1,0:T(4,128)S(1)} %get-tuple-element.32), channel_id=1, source_target_pairs={{1,0},{2,1},{3,2},{5,4},{6,5},{7,6},{9,8},{10,9},{11,10},{13,12},{... | collective-permute-start | bytes 589832 | tf_op jit(solution)/shard_map/ppermute | solution.py:521
  2.7 7.2 %collective-permute-start = (f32[3,16,4,256]{3,2,1,0:T(4,128)S(1)}, f32[3,16,4,256]{3,2,1,0:T(4,128)S(1)}, u32[]{:S(2)}, u32[]{:S(2)}) collective-permute-start(f32[3,16,4,256]{3,2,1,0:T(4,128)S(1)} %get-tuple-element.33), channel_id=1, source_target_pairs={{0,1},{1,2},{2,3},{4,5},{5,6},{6,7},{8,9},{9,10},{10,11},{12,13},{... | collective-permute-start | bytes 589832 | tf_op jit(solution)/shard_map/ppermute | solution.py:521
  10.2 10.1 %collective-permute-start.2 = (f32[10,24,256]{2,1,0:T(8,128)S(1)}, f32[10,24,256]{2,1,0:T(8,128)S(1)}, u32[]{:S(2)}, u32[]{:S(2)}) collective-permute-start(f32[10,24,256]{2,1,0:T(8,128)S(1)} %pad_maximum_fusion.2), channel_id=1, source_target_pairs={{4,8},{12,16},{20,24},{28,32},{36,40},{44,48},{52,56},{60,64},{68,... | collective-permute-start | bytes 737288 | tf_op jit(solution)/shard_map/ppermute | solution.py:531
  16.4 5.0 %collective-permute-start.3 = (f32[10,24,256]{2,1,0:T(8,128)S(1)}, f32[10,24,256]{2,1,0:T(8,128)S(1)}, u32[]{:S(2)}, u32[]{:S(2)}) collective-permute-start(f32[10,24,256]{2,1,0:T(8,128)S(1)} %pad_maximum_fusion.3), channel_id=1, source_target_pairs={{0,4},{8,12},{16,20},{24,28},{32,36},{40,44},{48,52},{56,60},{64,6... | collective-permute-start | bytes 737288 | tf_op jit(solution)/shard_map/ppermute | solution.py:531
  36.4 10.4 %collective-permute-start.5 = (f32[4,25,8,128]{3,2,1,0:T(8,128)S(1)}, f32[4,25,8,128]{3,2,1,0:T(8,128)S(1)}, u32[]{:S(2)}, u32[]{:S(2)}) collective-permute-start(f32[4,25,8,128]{3,2,1,0:T(8,128)S(1)} %all_to_all.10.own.own1), channel_id=1, source_target_pairs={{4,8},{12,16},{20,24},{28,32},{36,40},{44,48},{52,56},{60,64},{68,... | collective-permute-start | bytes 1228808 | tf_op jit(solution)/shard_map/ppermute | solution.py:531
  41.1 5.6 %collective-permute-start.4 = (f32[4,25,8,128]{3,2,1,0:T(8,128)S(1)}, f32[4,25,8,128]{3,2,1,0:T(8,128)S(1)}, u32[]{:S(2)}, u32[]{:S(2)}) collective-permute-start(f32[4,25,8,128]{3,2,1,0:T(8,128)S(1)} %all_to_all.10.own.own1), channel_id=1, source_target_pairs={{0,4},{8,12},{16,20},{24,28},{32,36},{40,44},{48,52},{56,60},{64,6... | collective-permute-start | bytes 1228808 | tf_op jit(solution)/shard_map/ppermute | solution.py:531
  49.1 17.4 %collective-permute-start.7 = (f32[13,16,128]{2,1,0:T(8,128)S(1)}, f32[13,16,128]{2,1,0:T(8,128)S(1)}, u32[]{:S(2)}, u32[]{:S(2)}) collective-permute-start(f32[13,16,128]{2,1,0:T(8,128)S(1)} %get-tuple-element.18), channel_id=1, source_target_pairs={{0,8},{4,508},{8,16},{12,4},{16,24},{20,12},{24,32},{28,20},{32,40... | collective-permute-start | bytes 319496 | tf_op jit(solution)/shard_map/ppermute | solution.py:526
  57.5 11.4 %collective-permute-start.6 = (f32[13,16,128]{2,1,0:T(8,128)S(1)}, f32[13,16,128]{2,1,0:T(8,128)S(1)}, u32[]{:S(2)}, u32[]{:S(2)}) collective-permute-start(f32[13,16,128]{2,1,0:T(8,128)S(1)} %get-tuple-element.18), channel_id=1, source_target_pairs={{0,16},{4,500},{8,24},{12,508},{16,32},{20,4},{24,40},{28,12},{32,... | collective-permute-start | bytes 319496 | tf_op jit(solution)/shard_map/ppermute | solution.py:526
  64.5 6.3 %collective-permute-start.8 = (f32[13,16,128]{2,1,0:T(8,128)S(1)}, f32[13,16,128]{2,1,0:T(8,128)S(1)}, u32[]{:S(2)}, u32[]{:S(2)}) collective-permute-start(f32[13,16,128]{2,1,0:T(8,128)S(1)} %get-tuple-element.18), channel_id=1, source_target_pairs={{0,4},{8,12},{16,20},{24,28},{32,36},{40,44},{48,52},{56,60},{64,6... | collective-permute-start | bytes 319496 | tf_op jit(solution)/shard_map/ppermute | solution.py:531
  66.5 4.4 %collective-permute-start.10 = (f32[13,16,128]{2,1,0:T(8,128)S(1)}, f32[13,16,128]{2,1,0:T(8,128)S(1)}, u32[]{:S(2)}, u32[]{:S(2)}) collective-permute-start(f32[13,16,128]{2,1,0:T(8,128)S(1)} %collective-permute-done.7.near), channel_id=1, source_target_pairs={{0,4},{8,12},{16,20},{24,28},{32,36},{40,44},{48,52},{56,60},{64,6... | collective-permute-start | bytes 319496 | tf_op jit(solution)/shard_map/ppermute | solution.py:531
  68.9 3.2 %collective-permute-start.9 = (f32[13,16,128]{2,1,0:T(8,128)S(1)}, f32[13,16,128]{2,1,0:T(8,128)S(1)}, u32[]{:S(2)}, u32[]{:S(2)}) collective-permute-start(f32[13,16,128]{2,1,0:T(8,128)S(1)} %collective-permute-done.6.far), channel_id=1, source_target_pairs={{0,4},{8,12},{16,20},{24,28},{32,36},{40,44},{48,52},{56,60},{64,6... | collective-permute-start | bytes 319496 | tf_op jit(solution)/shard_map/ppermute | solution.py:531
  76.4 23.2 %all-to-all-start.1 = ((f32[32,1,128]{2,1,0:T(1,128)}), f32[32,1,128]{2,1,0:T(1,128)S(1)}, u32[]{:S(2)}, u32[]{:S(2)}) async-start(f32[32,1,128]{2,1,0:T(1,128)} %get-tuple-element.20), calls=%async_computation.1 | async-start | bytes 32768 | tf_op jit(solution)/shard_map/all_to_all | solution.py:599

commit v7 on v6

--- a/solution.py
+++ b/solution.py
@@ -215,13 +215,19 @@
 
 
 def fetch1(own, inner, outer, fields, sems):
-    inner_at, outer_at = sides(2, 18)
     sources, targets = [], []
     for index, ref in fields:
-        for source, lo in ((own, 10), (inner, inner_at), (outer, outer_at)):
+        n = 8 if index == 2 else 6
+        inner_at, _ = sides(2, 18)
+        _, outer_at = sides(10 - n, 18)
+        for source, first, lo, rows in (
+            (own, 8 * index, 10, 8),
+            (inner, 8 * index, inner_at, 8),
+            (outer, 6 * index, outer_at, n),
+        ):
             for j in range(4):
-                sources.append(source.at[j, pl.ds(index * 8, 8)])
-                targets.append(ref.at[pl.ds(lo, 8), pl.ds(8 * j, 8), :])
+                sources.append(source.at[j, pl.ds(first, rows)])
+                targets.append(ref.at[pl.ds(lo, rows), pl.ds(8 * j, 8), :])
     return fetch(sources, targets, sems)
 
 
@@ -260,18 +266,18 @@
 
 
 def down1(
-    own, inner, outer, piece, mine,
+    own, outer, inner, piece, mine,
     vs, vc, cx, cy, cz, dg, wt, ss, cc, m, us, uc, pair, thin, parts, sems,
 ):
     copies = fetch1(own, inner, outer, ((2, m), (0, ss), (1, cc)), sems)
     partial = fetch([own.at[j, 24] for j in range(4)], [parts.at[j] for j in range(4)], sems.at[pl.ds(36, 4)])
     wait(copies[:12])
-    coefficients(1, m, cx, cy, cz, dg, wt, 3, 25, C1, 32, 128)
+    coefficients(1, m, cx, cy, cz, dg, wt, 4, 24, C1, 32, 128)
     coefs = (cx, cy, cz, dg)
     wait(copies[12:])
     wait(partial)
-    start(3, 25, S1, (ss, cc), (us, uc), wt)
-    sweep(4, 24, W1, (ss, cc), (us, uc), (vs, vc), coefs, wt)
+    start(4, 24, S1, (ss, cc), (us, uc), wt)
+    sweep(5, 23, W1, (ss, cc), (us, uc), (vs, vc), coefs, wt)
 
     def rest(i, n, sums):
         res_s, res_c, sums = products(i, n, ss, cc, vs, vc, coefs, sums)
@@ -559,12 +565,13 @@
         [VMEM] + [HBM] * 2,
     )
     gathered = lax.all_to_all(chunk, "narrow", 0, 0)
-    outer = swapped(gathered, 1)
+    edges = [lax.dynamic_slice_in_dim(gathered, 8 * index + 2 * odd, 6, axis=1) for index in range(2)]
+    outer = swapped(jnp.concatenate([*edges, gathered[:, 16:24]], axis=1), 1)
     inner = swapped(gathered, 0)
     a1 = (28, 32, 128)
     piece, mine = call(
         down1,
-        (gathered, inner, outer),
+        (gathered, outer, inner),
         [(13, 16, 128), (21, 16, 128)],
         [a1] * 12 + [(20, 32, 256), (20, 32, 128), (4, 8, 128)],
         "down1",

time: 101 us -> 103 us (1.020)
  blocking collectives: 11.6 us -> 0 us
  waiting for transfers between devices: 14.4 us -> 23.8 us
  starting transfers between devices: 54.2 us -> 57.7 us
    all_to_all x1 -> x0, blocking collectives: 11.6 us -> none  [per_device(): gathered = lax.all_to_all(chunk, 'narrow', 0, 0)]
    all_to_all x0 -> x1, waiting for transfers between devices: none -> 8.15 us  [per_device(): gathered = lax.all_to_all(chunk, 'narrow', 0, 0)]
    all_to_all x0 -> x1, starting transfers between devices: none -> 3.96 us  [per_device(): gathered = lax.all_to_all(chunk, 'narrow', 0, 0)]
    ppermute x7, waiting for transfers between devices: 6.07 us -> 7.31 us  [swapped(): return lax.ppermute(value, 'wide', pairs + [(b, a) for a, b in pairs])]
  transfers between devices with their start and end apart: 12 -> 13, of which waited for: 6 -> 7; matrix products, arithmetic and copies ran while one was open for 0% -> 0% of each run, Pallas kernels for 7% -> 7%
where the time goes in v7:
time: 103 us
  starting transfers between devices  57.7 us (56%)
  waiting for transfers between devices  23.8 us (23%)
  Pallas kernels  18.9 us (18%)
  other arithmetic  1.76 us (2%)
    ppermute x7, starting transfers between devices, swapped(): return lax.ppermute(value, 'wide', pairs + [(b, a) for a, b in pairs])  22.7 us
    pallas_call x5, Pallas kernels, call(): pl.pallas_call(kernel, out_shape=[jax.ShapeDtypeStruct(s, f32) for s in o...  18.9 us
    ppermute x2, starting transfers between devices, apart(): lax.ppermute(value, 'wide', [(i, (i + by * (1 - 2 * (i % 2))) % size) for...  16 us
    all_to_all x1, starting transfers between devices, per_device(): every = lax.all_to_all(sums, 'wide', 0, 0, axis_index_groups=groups)  9.16 us
    all_to_all x1, waiting for transfers between devices, per_device(): gathered = lax.all_to_all(chunk, 'narrow', 0, 0)  8.15 us
    ppermute x7, waiting for transfers between devices, swapped(): return lax.ppermute(value, 'wide', pairs + [(b, a) for a, b in pairs])  7.31 us
    ppermute x2, starting transfers between devices, shifted(): lax.ppermute(value, axis, [(i, i + by) for i in range(size) if 0 <= i + b...  5.88 us
    all_to_all x1, waiting for transfers between devices, per_device(): every = lax.all_to_all(sums, 'wide', 0, 0, axis_index_groups=groups)  5.73 us
  transfers between devices with their start and end apart: 13, of which 7 were waited for; matrix products, arithmetic and copies ran while one was open for 0% of the time, Pallas kernels for 7%

profile of v7, /device:TPU:1, one launch (start us, length us, event | category | flops | bytes accessed | tf_op | source)
XLA Modules:
  0.0 102.7 jit_solution(10621301160344891461)
XLA Ops:
  0.0 1.3 %pad_maximum_fusion.5 = (f32[3,16,4,256]{3,2,1,0:T(4,128)S(1)}, f32[3,16,4,256]{3,2,1,0:T(4,128)S(1)}) fusion(f32[1,16,16,256]{3,2,1,0:T(8,128)} %bitcast.18, f32[1,16,16,256]{3,2,1,0:T(8,128)} %bitcast.21, f32[1,16,16,256]{3,2,1,0:T(8,128)} %bitcast.24), kind=kLoop, calls=%fused_computation.5 | loop fusion | flops 196608 | bytes 1179648 | tf_op jit(solution)/shard_map/stack | solution.py:541
  1.4 1.3 %collective-permute-start.1 = (f32[3,16,4,256]{3,2,1,0:T(4,128)S(1)}, f32[3,16,4,256]{3,2,1,0:T(4,128)S(1)}, u32[]{:S(2)}, u32[]{:S(2)}) collective-permute-start(f32[3,16,4,256]{3,2,1,0:T(4,128)S(1)} %get-tuple-element.32), channel_id=1, source_target_pairs={{1,0},{2,1},{3,2},{5,4},{6,5},{7,6},{9,8},{10,9},{11,10},{13,12},{... | collective-permute-start | bytes 589832 | tf_op jit(solution)/shard_map/ppermute | solution.py:527
  2.7 4.6 %collective-permute-start = (f32[3,16,4,256]{3,2,1,0:T(4,128)S(1)}, f32[3,16,4,256]{3,2,1,0:T(4,128)S(1)}, u32[]{:S(2)}, u32[]{:S(2)}) collective-permute-start(f32[3,16,4,256]{3,2,1,0:T(4,128)S(1)} %get-tuple-element.33), channel_id=1, source_target_pairs={{0,1},{1,2},{2,3},{4,5},{5,6},{6,7},{8,9},{9,10},{10,11},{12,13},{... | collective-permute-start | bytes 589832 | tf_op jit(solution)/shard_map/ppermute | solution.py:527
  7.3 1.1 %collective-permute-done.1 = f32[3,16,4,256]{3,2,1,0:T(4,128)S(1)} collective-permute-done((f32[3,16,4,256]{3,2,1,0:T(4,128)S(1)}, f32[3,16,4,256]{3,2,1,0:T(4,128)S(1)}, u32[]{:S(2)}, u32[]{:S(2)}) %collective-permute-start.1) | collective-permute-done | bytes 196640 | tf_op jit(solution)/shard_map/ppermute | solution.py:527
  8.4 1.5 %collective-permute-done = f32[3,16,4,256]{3,2,1,0:T(4,128)S(1)} collective-permute-done((f32[3,16,4,256]{3,2,1,0:T(4,128)S(1)}, f32[3,16,4,256]{3,2,1,0:T(4,128)S(1)}, u32[]{:S(2)}, u32[]{:S(2)}) %collective-permute-start) | collective-permute-done | bytes 196640 | tf_op jit(solution)/shard_map/ppermute | solution.py:527
  9.8 0.2 pad_maximum_fusion.own
  10.0 0.1 fusion
  10.2 6.2 %collective-permute-start.2 = (f32[10,24,256]{2,1,0:T(8,128)S(1)}, f32[10,24,256]{2,1,0:T(8,128)S(1)}, u32[]{:S(2)}, u32[]{:S(2)}) collective-permute-start(f32[10,24,256]{2,1,0:T(8,128)S(1)} %pad_maximum_fusion.3), channel_id=1, source_target_pairs={{4,8},{12,16},{20,24},{28,32},{36,40},{44,48},{52,56},{60,64},{68,... | collective-permute-start | bytes 737288 | tf_op jit(solution)/shard_map/ppermute | solution.py:537
  16.4 3.8 %collective-permute-start.3 = (f32[10,24,256]{2,1,0:T(8,128)S(1)}, f32[10,24,256]{2,1,0:T(8,128)S(1)}, u32[]{:S(2)}, u32[]{:S(2)}) collective-permute-start(f32[10,24,256]{2,1,0:T(8,128)S(1)} %pad_maximum_fusion.4), channel_id=1, source_target_pairs={{0,4},{8,12},{16,20},{24,28},{32,36},{40,44},{48,52},{56,60},{64,6... | collective-permute-start | bytes 737288 | tf_op jit(solution)/shard_map/ppermute | solution.py:537
  20.3 0.0 collective-permute-done.2.outer.outer0
  20.3 1.1 %collective-permute-done.3.inner.inner0 = f32[10,24,256]{2,1,0:T(8,128)S(1)} collective-permute-done((f32[10,24,256]{2,1,0:T(8,128)S(1)}, f32[10,24,256]{2,1,0:T(8,128)S(1)}, u32[]{:S(2)}, u32[]{:S(2)}) %collective-permute-start.3) | collective-permute-done | bytes 245792 | tf_op jit(solution)/shard_map/ppermute | solution.py:537
  21.4 4.1 %down0.1 = f32[4,25,8,128]{3,2,1,0:T(8,128)} custom-call(f32[3,16,24,256]{3,2,1,0:T(8,128)S(1)} %pad_maximum_fusion.own, f32[10,24,256]{2,1,0:T(8,128)S(1)} %collective-permute-done.2.outer.outer0, f32[10,24,256]{2,1,0:T(8,128)S(1)} %collective-permute-done.3.inner.inner0), custom_call_target="tpu_custom_call" | custom-call | tf_op jit(solution)/shard_map/down0/pallas_call | solution.py:514
  25.5 4.0 %all-to-all-start = ((f32[4,25,8,128]{3,2,1,0:T(8,128)}), f32[4,25,8,128]{3,2,1,0:T(8,128)S(1)}, u32[]{:S(2)}, u32[]{:S(2)}) async-start(f32[4,25,8,128]{3,2,1,0:T(8,128)} %down0.1), calls=%async_computation | async-start | bytes 819200 | tf_op jit(solution)/shard_map/all_to_all | solution.py:567
  29.4 8.2 %all-to-all-done.own.own1 = f32[4,25,8,128]{3,2,1,0:T(8,128)S(1)} async-done(((f32[4,25,8,128]{3,2,1,0:T(8,128)}), f32[4,25,8,128]{3,2,1,0:T(8,128)S(1)}, u32[]{:S(2)}, u32[]{:S(2)}) %all-to-all-start) | async-done | bytes 409632 | tf_op jit(solution)/shard_map/all_to_all | solution.py:567
  37.6 3.0 %collective-permute-start.5 = (f32[4,25,8,128]{3,2,1,0:T(8,128)S(1)}, f32[4,25,8,128]{3,2,1,0:T(8,128)S(1)}, u32[]{:S(2)}, u32[]{:S(2)}) collective-permute-start(f32[4,25,8,128]{3,2,1,0:T(8,128)S(1)} %all-to-all-done.own.own1), channel_id=1, source_target_pairs={{0,4},{8,12},{16,20},{24,28},{32,36},{40,44},{48,52},{56,60},{64,6... | collective-permute-start | bytes 1228808 | tf_op jit(solution)/shard_map/ppermute | solution.py:537
  40.6 3.4 %collective-permute-start.4 = (f32[4,20,8,128]{3,2,1,0:T(8,128)S(1)}, f32[4,20,8,128]{3,2,1,0:T(8,128)S(1)}, u32[]{:S(2)}, u32[]{:S(2)}) collective-permute-start(f32[4,20,8,128]{3,2,1,0:T(8,128)S(1)} %pad_maximum_fusion.2), channel_id=1, source_target_pairs={{4,8},{12,16},{20,24},{28,32},{36,40},{44,48},{52,56},{60,64},{68,... | collective-permute-start | bytes 983048 | tf_op jit(solution)/shard_map/ppermute | solution.py:537
  44.1 4.9 %collective-permute-done.4.outer.outer1 = f32[4,20,8,128]{3,2,1,0:T(8,128)S(1)} collective-permute-done((f32[4,20,8,128]{3,2,1,0:T(8,128)S(1)}, f32[4,20,8,128]{3,2,1,0:T(8,128)S(1)}, u32[]{:S(2)}, u32[]{:S(2)}) %collective-permute-start.4) | collective-permute-done | bytes 327712 | tf_op jit(solution)/shard_map/ppermute | solution.py:537
  49.0 0.0 collective-permute-done.5.inner.inner1
  49.0 2.3 %down1.1 = (f32[13,16,128]{2,1,0:T(8,128)S(1)}, f32[21,16,128]{2,1,0:T(8,128)S(1)}) custom-call(f32[4,25,8,128]{3,2,1,0:T(8,128)S(1)} %all-to-all-done.own.own1, f32[4,20,8,128]{3,2,1,0:T(8,128)S(1)} %collective-permute-done.4.outer.outer1, f32[4,25,8,128]{3,2,1,0:T(8,128)S(1)} %collective-permute-done.5.inner.inner1), custom_call_target="tpu_custom_call" | custom-call | tf_op jit(solution)/shard_map/down1/pallas_call | solution.py:514
  51.4 5.2 %collective-permute-start.7 = (f32[13,16,128]{2,1,0:T(8,128)S(1)}, f32[13,16,128]{2,1,0:T(8,128)S(1)}, u32[]{:S(2)}, u32[]{:S(2)}) collective-permute-start(f32[13,16,128]{2,1,0:T(8,128)S(1)} %get-tuple-element.18), channel_id=1, source_target_pairs={{0,8},{4,508},{8,16},{12,4},{16,24},{20,12},{24,32},{28,20},{32,40... | collective-permute-start | bytes 319496 | tf_op jit(solution)/shard_map/ppermute | solution.py:532
  56.6 10.8 %collective-permute-start.6 = (f32[13,16,128]{2,1,0:T(8,128)S(1)}, f32[13,16,128]{2,1,0:T(8,128)S(1)}, u32[]{:S(2)}, u32[]{:S(2)}) collective-permute-start(f32[13,16,128]{2,1,0:T(8,128)S(1)} %get-tuple-element.18), channel_id=1, source_target_pairs={{0,16},{4,500},{8,24},{12,508},{16,32},{20,4},{24,40},{28,12},{32,... | collective-permute-start | bytes 319496 | tf_op jit(solution)/shard_map/ppermute | solution.py:532
  67.4 1.9 %collective-permute-start.8 = (f32[13,16,128]{2,1,0:T(8,128)S(1)}, f32[13,16,128]{2,1,0:T(8,128)S(1)}, u32[]{:S(2)}, u32[]{:S(2)}) collective-permute-start(f32[13,16,128]{2,1,0:T(8,128)S(1)} %get-tuple-element.18), channel_id=1, source_target_pairs={{0,4},{8,12},{16,20},{24,28},{32,36},{40,44},{48,52},{56,60},{64,6... | collective-permute-start | bytes 319496 | tf_op jit(solution)/shard_map/ppermute | solution.py:537
  69.4 0.0 collective-permute-done.7.near
  69.4 2.4 %collective-permute-start.10 = (f32[13,16,128]{2,1,0:T(8,128)S(1)}, f32[13,16,128]{2,1,0:T(8,128)S(1)}, u32[]{:S(2)}, u32[]{:S(2)}) collective-permute-start(f32[13,16,128]{2,1,0:T(8,128)S(1)} %collective-permute-done.7.near), channel_id=1, source_target_pairs={{0,4},{8,12},{16,20},{24,28},{32,36},{40,44},{48,52},{56,60},{64,6... | collective-permute-start | bytes 319496 | tf_op jit(solution)/shard_map/ppermute | solution.py:537
  71.8 1.9 %collective-permute-start.9 = (f32[13,16,128]{2,1,0:T(8,128)S(1)}, f32[13,16,128]{2,1,0:T(8,128)S(1)}, u32[]{:S(2)}, u32[]{:S(2)}) collective-permute-start(f32[13,16,128]{2,1,0:T(8,128)S(1)} %collective-permute-done.6.far), channel_id=1, source_target_pairs={{0,4},{8,12},{16,20},{24,28},{32,36},{40,44},{48,52},{56,60},{64,6... | collective-permute-start | bytes 319496 | tf_op jit(solution)/shard_map/ppermute | solution.py:537
  73.7 1.3 %collective-permute-done.9.pair_far = f32[13,16,128]{2,1,0:T(8,128)S(1)} collective-permute-done((f32[13,16,128]{2,1,0:T(8,128)S(1)}, f32[13,16,128]{2,1,0:T(8,128)S(1)}, u32[]{:S(2)}, u32[]{:S(2)}) %collective-permute-start.9) | collective-permute-done | bytes 106528 | tf_op jit(solution)/shard_map/ppermute | solution.py:537
  75.0 4.3 %bottom.1 = (f32[6144,16,128]{2,1,0:T(8,128)}, f32[32,1,128]{2,1,0:T(1,128)}) custom-call(f32[21,16,128]{2,1,0:T(8,128)S(1)} %get-tuple-element.17.mine, f32[13,16,128]{2,1,0:T(8,128)S(1)} %collective-permute-done.6.far, f32[13,16,128]{2,1,0:T(8,128)S(1)} %collective-permute-done.7.near, f32[13,16,128]{2,1,0:T(8,128)S(1)} %collective-permute-done.8.pair_own, ...), custom_call_target="tpu_custom_call" | custom-call | tf_op jit(solution)/shard_map/bottom/pallas_call | solution.py:514
  79.3 9.2 %all-to-all-start.1 = ((f32[32,1,128]{2,1,0:T(1,128)}), f32[32,1,128]{2,1,0:T(1,128)S(1)}, u32[]{:S(2)}, u32[]{:S(2)}) async-start(f32[32,1,128]{2,1,0:T(1,128)} %get-tuple-element.20), calls=%async_computation.1 | async-start | bytes 32768 | tf_op jit(solution)/shard_map/all_to_all | solution.py:606
  88.5 0.2 pad_maximum_fusion.1.own0
  88.6 7.3 %up.1 = (f32[16,16,256]{2,1,0:T(8,128)S(1)}, f32[16,16,256]{2,1,0:T(8,128)S(1)}) custom-call(f32[6144,16,128]{2,1,0:T(8,128)} %get-tuple-element.21.e2_in, f32[4,25,8,128]{3,2,1,0:T(8,128)S(1)} %all-to-all-done.own.own1, f32[4,25,8,128]{3,2,1,0:T(8,128)S(1)} %collective-permute-done.5.inner.inner1, ...), custom_call_target="tpu_custom_call" | custom-call | tf_op jit(solution)/shard_map/up/pallas_call | solution.py:514
  95.9 5.7 %all-to-all-done.1.every = f32[32,1,128]{2,1,0:T(1,128)S(1)} async-done(((f32[32,1,128]{2,1,0:T(1,128)}), f32[32,1,128]{2,1,0:T(1,128)S(1)}, u32[]{:S(2)}, u32[]{:S(2)}) %all-to-all-start.1) | async-done | bytes 16416 | tf_op jit(solution)/shard_map/all_to_all | solution.py:606
  101.6 0.9 final.1
  (16 shorter events, 0.2 us)
Async XLA Ops:
  0.0 9.8 %copy-start = (f32[16,16,256]{2,1,0:T(8,128)S(1)}, f32[16,16,256]{2,1,0:T(8,128)}, u32[]{:S(2)}) copy-start(f32[16,16,256]{2,1,0:T(8,128)} %param.5) | copy-start | bytes 786436
  0.0 9.8 %copy-start.1 = (f32[16,16,256]{2,1,0:T(8,128)S(1)}, f32[16,16,256]{2,1,0:T(8,128)}, u32[]{:S(2)}) copy-start(f32[16,16,256]{2,1,0:T(8,128)} %param.4) | copy-start | bytes 786436
  0.0 9.8 %copy-start.2 = (f32[16,16,256]{2,1,0:T(8,128)S(1)}, f32[16,16,256]{2,1,0:T(8,128)}, u32[]{:S(2)}) copy-start(f32[16,16,256]{2,1,0:T(8,128)} %param.3) | copy-start | bytes 786436
  1.4 7.0 %collective-permute-start.1 = (f32[3,16,4,256]{3,2,1,0:T(4,128)S(1)}, f32[3,16,4,256]{3,2,1,0:T(4,128)S(1)}, u32[]{:S(2)}, u32[]{:S(2)}) collective-permute-start(f32[3,16,4,256]{3,2,1,0:T(4,128)S(1)} %get-tuple-element.32), channel_id=1, source_target_pairs={{1,0},{2,1},{3,2},{5,4},{6,5},{7,6},{9,8},{10,9},{11,10},{13,12},{... | collective-permute-start | bytes 589832 | tf_op jit(solution)/shard_map/ppermute | solution.py:527
  2.7 7.2 %collective-permute-start = (f32[3,16,4,256]{3,2,1,0:T(4,128)S(1)}, f32[3,16,4,256]{3,2,1,0:T(4,128)S(1)}, u32[]{:S(2)}, u32[]{:S(2)}) collective-permute-start(f32[3,16,4,256]{3,2,1,0:T(4,128)S(1)} %get-tuple-element.33), channel_id=1, source_target_pairs={{0,1},{1,2},{2,3},{4,5},{5,6},{6,7},{8,9},{9,10},{10,11},{12,13},{... | collective-permute-start | bytes 589832 | tf_op jit(solution)/shard_map/ppermute | solution.py:527
  10.2 10.1 %collective-permute-start.2 = (f32[10,24,256]{2,1,0:T(8,128)S(1)}, f32[10,24,256]{2,1,0:T(8,128)S(1)}, u32[]{:S(2)}, u32[]{:S(2)}) collective-permute-start(f32[10,24,256]{2,1,0:T(8,128)S(1)} %pad_maximum_fusion.3), channel_id=1, source_target_pairs={{4,8},{12,16},{20,24},{28,32},{36,40},{44,48},{52,56},{60,64},{68,... | collective-permute-start | bytes 737288 | tf_op jit(solution)/shard_map/ppermute | solution.py:537
  16.4 5.0 %collective-permute-start.3 = (f32[10,24,256]{2,1,0:T(8,128)S(1)}, f32[10,24,256]{2,1,0:T(8,128)S(1)}, u32[]{:S(2)}, u32[]{:S(2)}) collective-permute-start(f32[10,24,256]{2,1,0:T(8,128)S(1)} %pad_maximum_fusion.4), channel_id=1, source_target_pairs={{0,4},{8,12},{16,20},{24,28},{32,36},{40,44},{48,52},{56,60},{64,6... | collective-permute-start | bytes 737288 | tf_op jit(solution)/shard_map/ppermute | solution.py:537
  25.5 12.1 %all-to-all-start = ((f32[4,25,8,128]{3,2,1,0:T(8,128)}), f32[4,25,8,128]{3,2,1,0:T(8,128)S(1)}, u32[]{:S(2)}, u32[]{:S(2)}) async-start(f32[4,25,8,128]{3,2,1,0:T(8,128)} %down0.1), calls=%async_computation | async-start | bytes 819200 | tf_op jit(solution)/shard_map/all_to_all | solution.py:567
  37.6 11.4 %collective-permute-start.5 = (f32[4,25,8,128]{3,2,1,0:T(8,128)S(1)}, f32[4,25,8,128]{3,2,1,0:T(8,128)S(1)}, u32[]{:S(2)}, u32[]{:S(2)}) collective-permute-start(f32[4,25,8,128]{3,2,1,0:T(8,128)S(1)} %all-to-all-done.own.own1), channel_id=1, source_target_pairs={{0,4},{8,12},{16,20},{24,28},{32,36},{40,44},{48,52},{56,60},{64,6... | collective-permute-start | bytes 1228808 | tf_op jit(solution)/shard_map/ppermute | solution.py:537
  40.6 8.4 %collective-permute-start.4 = (f32[4,20,8,128]{3,2,1,0:T(8,128)S(1)}, f32[4,20,8,128]{3,2,1,0:T(8,128)S(1)}, u32[]{:S(2)}, u32[]{:S(2)}) collective-permute-start(f32[4,20,8,128]{3,2,1,0:T(8,128)S(1)} %pad_maximum_fusion.2), channel_id=1, source_target_pairs={{4,8},{12,16},{20,24},{28,32},{36,40},{44,48},{52,56},{60,64},{68,... | collective-permute-start | bytes 983048 | tf_op jit(solution)/shard_map/ppermute | solution.py:537
  51.4 18.0 %collective-permute-start.7 = (f32[13,16,128]{2,1,0:T(8,128)S(1)}, f32[13,16,128]{2,1,0:T(8,128)S(1)}, u32[]{:S(2)}, u32[]{:S(2)}) collective-permute-start(f32[13,16,128]{2,1,0:T(8,128)S(1)} %get-tuple-element.18), channel_id=1, source_target_pairs={{0,8},{4,508},{8,16},{12,4},{16,24},{20,12},{24,32},{28,20},{32,40... | collective-permute-start | bytes 319496 | tf_op jit(solution)/shard_map/ppermute | solution.py:532
  56.6 15.2 %collective-permute-start.6 = (f32[13,16,128]{2,1,0:T(8,128)S(1)}, f32[13,16,128]{2,1,0:T(8,128)S(1)}, u32[]{:S(2)}, u32[]{:S(2)}) collective-permute-start(f32[13,16,128]{2,1,0:T(8,128)S(1)} %get-tuple-element.18), channel_id=1, source_target_pairs={{0,16},{4,500},{8,24},{12,508},{16,32},{20,4},{24,40},{28,12},{32,... | collective-permute-start | bytes 319496 | tf_op jit(solution)/shard_map/ppermute | solution.py:532
  67.4 6.3 %collective-permute-start.8 = (f32[13,16,128]{2,1,0:T(8,128)S(1)}, f32[13,16,128]{2,1,0:T(8,128)S(1)}, u32[]{:S(2)}, u32[]{:S(2)}) collective-permute-start(f32[13,16,128]{2,1,0:T(8,128)S(1)} %get-tuple-element.18), channel_id=1, source_target_pairs={{0,4},{8,12},{16,20},{24,28},{32,36},{40,44},{48,52},{56,60},{64,6... | collective-permute-start | bytes 319496 | tf_op jit(solution)/shard_map/ppermute | solution.py:537
  69.4 4.4 %collective-permute-start.10 = (f32[13,16,128]{2,1,0:T(8,128)S(1)}, f32[13,16,128]{2,1,0:T(8,128)S(1)}, u32[]{:S(2)}, u32[]{:S(2)}) collective-permute-start(f32[13,16,128]{2,1,0:T(8,128)S(1)} %collective-permute-done.7.near), channel_id=1, source_target_pairs={{0,4},{8,12},{16,20},{24,28},{32,36},{40,44},{48,52},{56,60},{64,6... | collective-permute-start | bytes 319496 | tf_op jit(solution)/shard_map/ppermute | solution.py:537
  71.8 3.2 %collective-permute-start.9 = (f32[13,16,128]{2,1,0:T(8,128)S(1)}, f32[13,16,128]{2,1,0:T(8,128)S(1)}, u32[]{:S(2)}, u32[]{:S(2)}) collective-permute-start(f32[13,16,128]{2,1,0:T(8,128)S(1)} %collective-permute-done.6.far), channel_id=1, source_target_pairs={{0,4},{8,12},{16,20},{24,28},{32,36},{40,44},{48,52},{56,60},{64,6... | collective-permute-start | bytes 319496 | tf_op jit(solution)/shard_map/ppermute | solution.py:537
  79.3 22.4 %all-to-all-start.1 = ((f32[32,1,128]{2,1,0:T(1,128)}), f32[32,1,128]{2,1,0:T(1,128)S(1)}, u32[]{:S(2)}, u32[]{:S(2)}) async-start(f32[32,1,128]{2,1,0:T(1,128)} %get-tuple-element.20), calls=%async_computation.1 | async-start | bytes 32768 | tf_op jit(solution)/shard_map/all_to_all | solution.py:606
